TPU v7x, 32 devices: a whole 2x2x4 slice. The times are simulated.
32 devices in a mesh: ctx: 16 (over z, y, x), fsdp: 2 (over core).
Axes of the slice: x: 2, y: 2, z: 4, core: 2. Of those that a mesh axis runs over, the one named last changes fastest.
Arguments:
- tokens: bfloat16 [2, 2048, 1600], P('fsdp', 'ctx'), may hold values from -6 to 6
- qkv_weight: bfloat16 [1600, 4800], P('ctx', 'fsdp'), may hold values from -0.15625 to 0.15625
- proj_weight: bfloat16 [1600, 1600], P('ctx', 'fsdp'), may hold values from -3 to 3
- fc_weight: bfloat16 [1600, 6400], P('ctx', 'fsdp'), may hold values from -0.15625 to 0.15625
- out_weight: bfloat16 [6400, 1600], P('ctx', 'fsdp'), may hold values from -0.078125 to 0.078125
- gains: bfloat16 [2, 1600], P('fsdp', 'ctx'), may hold values from 0.5 to 1.5
- biases: bfloat16 [6, 1600], P('fsdp', 'ctx'), may hold values from -0.119628906 to 0.119628906
- fc_bias: bfloat16 [6400], P(('ctx', 'fsdp')), may hold values from -3 to 3
- cotangent: bfloat16 [2, 2048, 1600], P('fsdp', 'ctx'), may hold values from -6 to 6
Outputs:
- mixed: bfloat16 [2, 2048, 1600], P('fsdp', 'ctx')
- input_grad: float32 [2, 2048, 1600], P('fsdp', 'ctx')
- qkv_weight_grad: float32 [1600, 4800], P('ctx', 'fsdp')
- proj_weight_grad: float32 [1600, 1600], P('ctx', 'fsdp')
- fc_weight_grad: float32 [1600, 6400], P('ctx', 'fsdp')
- out_weight_grad: float32 [6400, 1600], P('ctx', 'fsdp')
- gains_grad: float32 [2, 1600], P('fsdp', 'ctx')
- biases_grad: float32 [6, 1600], P('fsdp', 'ctx')
- fc_bias_grad: float32 [6400], P(('ctx', 'fsdp'))
All inputs are finite; a program needn't handle non-finite values.
Results may differ from a plain program's by a relative error of at most 0.019.
Values may be sent and summed in bfloat16 or wider, within the bound.
A program may use at most 576 MiB of HBM per device.

v0:
```python
import math

import jax
import jax.numpy as jnp
from jax import lax
from jax.sharding import PartitionSpec as P

D = 1600
HEADS = 25
HEAD_DIM = 64
FF = 6400


EPS = 1e-05


def shifted(block, axis, distance):
    devices = range(lax.axis_size(axis))
    route = [(i - distance, i) for i in devices if i - distance in devices]
    return lax.ppermute(block, axis, route)


def passed_along(block, axis, distance):
    devices = range(lax.axis_size(axis))
    route = [((i - distance) % len(devices), i) for i in devices]
    return lax.ppermute(block, axis, route)


def gelu_tanh(values):
    return jax.nn.gelu(values, approximate=True)


def norm_forward(values, gain, bias):
    centre = values - jnp.mean(values, axis=-1, keepdims=True)
    spread = lax.rsqrt(jnp.mean(centre * centre, axis=-1, keepdims=True) + EPS)
    normed = centre * spread
    return (normed * gain + bias, normed, spread)


def norm_back(grad_out, normed, spread, gain):
    scaled = grad_out * gain
    grad_in = spread * (
        scaled
        - jnp.mean(scaled, axis=-1, keepdims=True)
        - normed * jnp.mean(scaled * normed, axis=-1, keepdims=True)
    )
    return (grad_in, jnp.sum(grad_out * normed, axis=0), jnp.sum(grad_out, axis=0))


def contract_rows(left, right):
    return lax.dot_general(
        left, right, (((0,), (0,)), ((), ())), preferred_element_type=jnp.float32
    )


def times_transpose(left, right):
    return lax.dot_general(
        left, right, (((1,), (1,)), ((), ())), preferred_element_type=jnp.float32
    )


def tile_blocks(matrix, row_parts, col_parts):
    rows, cols = matrix.shape
    split = matrix.reshape(row_parts, rows // row_parts, col_parts, cols // col_parts)
    return jnp.transpose(split, (0, 2, 1, 3)).reshape(row_parts * col_parts, -1)


def pair_grads(
    query_heads, dout_heads, log_total, delta_rows, key_heads, value_heads, query_pos, key_pos
):
    scale = 1.0 / math.sqrt(HEAD_DIM)
    scores = (
        jnp.einsum("qhd,khd->hqk", query_heads, key_heads, preferred_element_type=jnp.float32)
        * scale
    )
    visible = key_pos[None, :] <= query_pos[:, None]
    probs = jnp.where(visible[None], jnp.exp(scores - log_total[:, :, None]), 0.0)
    dprobs = jnp.einsum("qhd,khd->hqk", dout_heads, value_heads, preferred_element_type=jnp.float32)
    dscores = (probs * (dprobs - delta_rows[:, :, None])).astype(jnp.bfloat16)
    query_part = (
        jnp.einsum("hqk,khd->qhd", dscores, key_heads, preferred_element_type=jnp.float32) * scale
    )
    key_part = (
        jnp.einsum("hqk,qhd->khd", dscores, query_heads, preferred_element_type=jnp.float32) * scale
    )
    value_part = jnp.einsum(
        "hqk,qhd->khd", probs.astype(jnp.bfloat16), dout_heads, preferred_element_type=jnp.float32
    )
    return (query_part, key_part, value_part)


def shards(
    tokens, qkv_weight, proj_weight, fc_weight, out_weight, gains, biases, fc_bias, cotangent
):
    columns = (
        lax.all_gather(qkv_weight, "fsdp", axis=1, tiled=True),
        lax.all_gather(proj_weight, "fsdp", axis=1, tiled=True),
        lax.all_gather(fc_weight, "fsdp", axis=1, tiled=True),
        lax.all_gather(out_weight, "fsdp", axis=1, tiled=True),
        lax.all_gather(gains, "fsdp", axis=0, tiled=True),
        lax.all_gather(biases, "fsdp", axis=0, tiled=True),
        lax.all_gather(fc_bias, "fsdp", axis=0, tiled=True),
    )
    gathered = (
        lax.all_gather(columns[0], "ctx", axis=0, tiled=True),
        lax.all_gather(columns[1], "ctx", axis=0, tiled=True),
        lax.all_gather(columns[2], "ctx", axis=0, tiled=True),
        lax.all_gather(columns[3], "ctx", axis=0, tiled=True),
        lax.all_gather(columns[4], "ctx", axis=1, tiled=True),
        lax.all_gather(columns[5], "ctx", axis=1, tiled=True),
        lax.all_gather(columns[6], "ctx", axis=0, tiled=True),
    )
    w_qkv = gathered[0]
    w_proj = gathered[1]
    w_fc = gathered[2]
    w_out = gathered[3]
    gain_rows = gathered[4].astype(jnp.float32)
    bias_rows = gathered[5].astype(jnp.float32)
    fc_shift = gathered[6].astype(jnp.float32)
    tok_rows = tokens.shape[1]
    flat_rows = tokens.reshape(tok_rows, D).astype(jnp.float32)
    grad_out = cotangent.reshape(tok_rows, D)
    n_ctx = lax.axis_size("ctx")
    n_fsdp = lax.axis_size("fsdp")
    my_block = lax.axis_index("ctx")
    my_first = my_block * tok_rows
    offsets = jnp.arange(tok_rows, dtype=jnp.int32)
    own_pos = my_first + offsets
    scale = 1.0 / math.sqrt(HEAD_DIM)
    normed_one, hat_one, spread_one = norm_forward(flat_rows, gain_rows[0], bias_rows[0])
    normed_low = normed_one.astype(jnp.bfloat16)
    projected = jnp.dot(normed_low, w_qkv, preferred_element_type=jnp.float32)
    queries = (
        (projected[:, :D] + bias_rows[1]).astype(jnp.bfloat16).reshape(tok_rows, HEADS, HEAD_DIM)
    )
    keys_own = projected[:, D : 2 * D].astype(jnp.bfloat16).reshape(tok_rows, HEADS, HEAD_DIM)
    values_own = (
        (projected[:, 2 * D :] + bias_rows[2])
        .astype(jnp.bfloat16)
        .reshape(tok_rows, HEADS, HEAD_DIM)
    )
    start_state = (
        jnp.full((HEADS, tok_rows), -1e30, jnp.float32),
        jnp.zeros((HEADS, tok_rows), jnp.float32),
        jnp.zeros((HEADS, tok_rows, HEAD_DIM), jnp.float32),
    )
    key_piece = lax.all_gather(keys_own, "ctx", axis=0, tiled=True)
    value_piece = lax.all_gather(values_own, "ctx", axis=0, tiled=True)
    key_pos = jnp.arange(key_piece.shape[0], dtype=jnp.int32)

    def fold_active(state):
        peak, total, accum = state
        scores = (
            jnp.einsum("qhd,khd->hqk", queries, key_piece, preferred_element_type=jnp.float32)
            * scale
        )
        visible = (key_pos[None, :] <= own_pos[:, None])[None]
        new_peak = jnp.maximum(peak, jnp.max(jnp.where(visible, scores, -1e30), axis=-1))
        expd = jnp.where(visible, jnp.exp(scores - new_peak[:, :, None]), 0.0)
        total = jnp.sum(expd, axis=-1)
        accum = jnp.einsum(
            "hqk,khd->hqd",
            expd.astype(jnp.bfloat16),
            value_piece,
            preferred_element_type=jnp.float32,
        )
        return (new_peak, total, accum)

    peak, total, accum = lax.cond(
        jnp.int32(0) <= my_first + tok_rows - 1, fold_active, lambda state: state, start_state
    )
    attended_f = jnp.transpose(accum / total[:, :, None], (1, 0, 2)).reshape(tok_rows, D)
    log_total = peak + jnp.log(total)
    attended_low = attended_f.astype(jnp.bfloat16)
    middle = (
        flat_rows + jnp.dot(attended_low, w_proj, preferred_element_type=jnp.float32) + bias_rows[3]
    )
    normed_two, hat_two, spread_two = norm_forward(middle, gain_rows[1], bias_rows[4])
    normed_two_low = normed_two.astype(jnp.bfloat16)
    hidden_pre = jnp.dot(normed_two_low, w_fc, preferred_element_type=jnp.float32) + fc_shift
    hidden_act, gelu_back = jax.vjp(gelu_tanh, hidden_pre)
    hidden_low = hidden_act.astype(jnp.bfloat16)
    mixed = (
        middle + jnp.dot(hidden_low, w_out, preferred_element_type=jnp.float32) + bias_rows[5]
    ).astype(jnp.bfloat16)
    out_grad_w = contract_rows(hidden_low, grad_out)
    out_bias_g = jnp.sum(grad_out.astype(jnp.float32), axis=0)
    hidden_grad = gelu_back(times_transpose(grad_out, w_out))[0]
    pre_low = hidden_grad.astype(jnp.bfloat16)
    fc_grad_w = contract_rows(normed_two_low, pre_low)
    fc_bias_g = jnp.sum(pre_low.astype(jnp.float32), axis=0)
    back_two, gain_two_g, bias_two_g = norm_back(
        times_transpose(pre_low, w_fc), hat_two, spread_two, gain_rows[1]
    )
    middle_grad = grad_out.astype(jnp.float32) + back_two
    branch_low = middle_grad.astype(jnp.bfloat16)
    proj_grad_w = contract_rows(attended_low, branch_low)
    proj_bias_g = jnp.sum(branch_low.astype(jnp.float32), axis=0)
    grad_heads = (
        times_transpose(branch_low, w_proj).astype(jnp.bfloat16).reshape(tok_rows, HEADS, HEAD_DIM)
    )
    delta_rows = jnp.sum(
        grad_heads.astype(jnp.float32) * attended_f.reshape(tok_rows, HEADS, HEAD_DIM), axis=-1
    ).T
    zero_heads = jnp.zeros((tok_rows, HEADS, HEAD_DIM), jnp.float32)

    def key_step(step, carry):
        key_blk, value_blk, key_acc, value_acc, query_acc = carry
        owner = jnp.remainder(my_block - step, n_ctx)
        key_pos = owner * tok_rows + offsets

        def key_active(sums):
            parts = pair_grads(
                queries, grad_heads, log_total, delta_rows, key_blk, value_blk, own_pos, key_pos
            )
            return (sums[0] + parts[0], sums[1] + parts[1], sums[2] + parts[2])

        query_acc, key_acc, value_acc = lax.cond(
            owner <= my_block, key_active, lambda sums: sums, (query_acc, key_acc, value_acc)
        )
        key_blk, value_blk = shifted((key_blk, value_blk), "ctx", 1)
        key_acc, value_acc = (
            passed_along(key_acc.astype(jnp.bfloat16), "ctx", 1).astype(key_acc.dtype),
            passed_along(value_acc.astype(jnp.bfloat16), "ctx", 1).astype(value_acc.dtype),
        )
        return (key_blk, value_blk, key_acc, value_acc, query_acc)

    finished = lax.fori_loop(
        0, n_ctx, key_step, (keys_own, values_own, zero_heads, zero_heads, zero_heads)
    )
    key_grad = finished[2]
    value_grad = finished[3]
    query_grad = finished[4]
    query_low = query_grad.reshape(tok_rows, D).astype(jnp.bfloat16)
    key_low = key_grad.reshape(tok_rows, D).astype(jnp.bfloat16)
    value_low = value_grad.reshape(tok_rows, D).astype(jnp.bfloat16)
    qkv_rows = jnp.concatenate([query_low, key_low, value_low], axis=1)
    qkv_grad_w = contract_rows(normed_low, qkv_rows)
    back_one, gain_one_g, bias_one_g = norm_back(
        times_transpose(qkv_rows, w_qkv), hat_one, spread_one, gain_rows[0]
    )
    input_grad = (middle_grad + back_one).reshape(tokens.shape)
    gains_g = jnp.stack([gain_one_g, gain_two_g])
    biases_g = jnp.stack(
        [
            bias_one_g,
            jnp.sum(query_low.astype(jnp.float32), axis=0),
            jnp.sum(value_low.astype(jnp.float32), axis=0),
            proj_bias_g,
            bias_two_g,
            out_bias_g,
        ]
    )
    owners = n_ctx * n_fsdp
    packed = jnp.concatenate(
        [
            tile_blocks(qkv_grad_w, n_ctx, n_fsdp),
            tile_blocks(proj_grad_w, n_ctx, n_fsdp),
            tile_blocks(fc_grad_w, n_ctx, n_fsdp),
            tile_blocks(out_grad_w, n_ctx, n_fsdp),
            tile_blocks(gains_g.T, n_ctx, n_fsdp),
            tile_blocks(biases_g.T, n_ctx, n_fsdp),
            fc_bias_g.reshape(owners, -1),
        ],
        axis=1,
    )
    summed = lax.psum_scatter(packed, ("ctx", "fsdp"), scatter_dimension=0, tiled=True)
    flat_sum = summed.reshape(-1)
    row_d = D // n_ctx
    row_ff = FF // n_ctx
    shapes = [
        (row_d, 3 * D // n_fsdp),
        (row_d, D // n_fsdp),
        (row_d, FF // n_fsdp),
        (row_ff, D // n_fsdp),
        (row_d, 2 // n_fsdp),
        (row_d, 6 // n_fsdp),
        (FF // owners, 1),
    ]
    pieces = []
    first = 0
    for shape in shapes:
        count = shape[0] * shape[1]
        pieces.append(flat_sum[first : first + count].reshape(shape))
        first = first + count
    gains_out = pieces[4].T
    biases_out = pieces[5].T
    fc_bias_out = pieces[6].reshape(-1)
    return (
        mixed.reshape(tokens.shape),
        input_grad,
        pieces[0],
        pieces[1],
        pieces[2],
        pieces[3],
        gains_out,
        biases_out,
        fc_bias_out,
    )


def solution(mesh):
    in_specs = (
        P("fsdp", "ctx", None),
        P("ctx", "fsdp"),
        P("ctx", "fsdp"),
        P("ctx", "fsdp"),
        P("ctx", "fsdp"),
        P("fsdp", "ctx"),
        P("fsdp", "ctx"),
        P(("ctx", "fsdp")),
        P("fsdp", "ctx", None),
    )
    out_specs = (
        P("fsdp", "ctx", None),
        P("fsdp", "ctx", None),
        P("ctx", "fsdp"),
        P("ctx", "fsdp"),
        P("ctx", "fsdp"),
        P("ctx", "fsdp"),
        P("fsdp", "ctx"),
        P("fsdp", "ctx"),
        P(("ctx", "fsdp")),
    )
    return jax.shard_map(shards, mesh=mesh, in_specs=in_specs, out_specs=out_specs, check_vma=False)
```

profile of v0, /device:TPU:0, one launch (start us, length us, event | category | flops | bytes accessed | tf_op | source)
XLA Modules:
  0.0 3865.7 jit_solution(15117004033829695681)
XLA Ops:
  23.6 42.0 %all-gather.3 = bf16[16,100,6]{1,2,0:T(8,128)(2,1)S(1)} all-gather(bf16[1,100,6]{1,2,0:T(8,128)(2,1)S(1)} %bitcast.246), channel_id=1, replica_groups=mesh['ctx'=16,'fsdp'=2] {'ctx'}, dimensions={0}, use_global_device_ids=true | all-gather | bytes 20400 | tf_op jit(solution)/shard_map/all_gather | solution.py:110
  67.5 35.9 all-gather.1
  104.6 108.0 %all-gather.27.cloned.1.call-done = bf16[16,100,4800]{2,1,0:T(8,128)(2,1)} async-done(((bf16[1,100,4800]{2,1,0:T(8,128)(2,1)}), bf16[16,100,4800]{2,1,0:T(8,128)(2,1)}) %all-gather.27.cloned.1.call-update) | async-done | bytes 15360016 | tf_op jit(solution)/shard_map/all_gather | solution.py:105
  212.6 16.0 reshape.261
  228.6 10.5 fusion.70
  251.3 75.5 %all-reduce.1 = bf16[6400]{0:T(1024)(128)(2,1)S(1)} all-reduce(bf16[6400]{0:T(1024)(128)(2,1)S(1)} %dynamic-update-slice.1), channel_id=1, replica_groups=mesh['ctx'=16,'fsdp'=2] {'ctx'}, use_global_device_ids=true, to_apply=%add.1 | all-reduce | flops 6400 | bytes 25600
  334.9 216.3 %all-gather.31.cloned.1.call-done = bf16[16,100,6400]{2,1,0:T(8,128)(2,1)} async-done(((bf16[1,100,6400]{2,1,0:T(8,128)(2,1)}), bf16[16,100,6400]{2,1,0:T(8,128)(2,1)}) %all-gather.31.cloned.1.call-update) | async-done | bytes 20480016 | tf_op jit(solution)/shard_map/all_gather | solution.py:107
  551.2 17.3 reshape.267
  568.4 102.4 %all-gather.19.cloned.1.call-done = bf16[2048,25,64]{0,2,1:T(8,128)(2,1)} async-done(((bf16[128,25,64]{0,2,1:T(8,128)(2,1)}), bf16[2048,25,64]{0,2,1:T(8,128)(2,1)}) %all-gather.19.cloned.1.call-update) | async-done | bytes 6553616 | tf_op jit(solution)/shard_map/all_gather | solution.py:147
  670.9 120.4 %all-gather.21.cloned.1.call-done = bf16[2048,25,64]{0,2,1:T(8,128)(2,1)} async-done(((bf16[128,25,64]{0,2,1:T(8,128)(2,1)}), bf16[2048,25,64]{0,2,1:T(8,128)(2,1)}) %all-gather.21.cloned.1.call-update) | async-done | bytes 6553616 | tf_op jit(solution)/shard_map/all_gather | solution.py:148
  791.3 41.7 %conditional.2 = (f32[25,128]{1,0:T(8,128)}, f32[25,128]{1,0:T(8,128)}, f32[25,128,64]{1,2,0:T(8,128)S(1)}, f32[25,128]{1,0:T(8,128)S(1)}) conditional(s32[]{:T(128)} %convert_element_type.159, () %tuple.52, (s32[2048]{0:T(1024)S(1)}, s32[]{:T(128)}, bf16[128,25,64]{0,2,1:T(8,128)(2,1)}, bf16[2048,25,64]{0,2,1:T(8,128)(2,1)}, ...), branch_computations={%region_2.0_spmd, %region_3.6_spmd} | conditional | flops 1750070272 | bytes 94139936 | solution.py:169
  791.5 14.0 select_reduce_fusion
  806.1 12.4 fusion.5
  818.5 13.7 fusion.6
  839.0 14.5 fusion.31
  853.5 173.8 %all-gather.25.cloned.1.call-done = bf16[6400,1600]{1,0:T(8,128)(2,1)} async-done(((bf16[400,1600]{1,0:T(8,128)(2,1)}), bf16[6400,1600]{1,0:T(8,128)(2,1)}) %all-gather.25.cloned.1.call-update) | async-done | bytes 20480016 | tf_op jit(solution)/shard_map/all_gather | solution.py:108
  1027.3 12.0 convert_reduce_fusion
  1039.3 12.7 multiply_reduce_fusion
  1060.0 651.1 %while.24 = (s32[]{:T(128)}, bf16[128,25,64]{0,2,1:T(8,128)(2,1)S(1)}, bf16[128,25,64]{0,2,1:T(8,128)(2,1)S(1)}, f32[128,25,64]{0,2,1:T(8,128)}, f32[128,25,64]{...) while((s32[]{:T(128)}, ...), condition=%wide.region_14.15_spmd.clone, body=%wide.region_11.14_spmd.clone.sunk | while | flops 267280656 | bytes 39793868 | solution.py:228
  1154.7 9.0 collective-permute-start.3
  1249.9 11.8 collective-permute-start.1
  1283.2 11.0 collective-permute-start
  1338.2 12.2 collective-permute-done.2
  1375.8 17.6 collective-permute-done.2
  1414.3 20.3 collective-permute-done.2
  1452.8 22.2 collective-permute-done.2
  1492.0 22.6 collective-permute-done.2
  1532.0 22.0 collective-permute-done.2
  1568.8 24.0 collective-permute-done.2
  1606.0 24.8 collective-permute-done.2
  1646.0 21.9 collective-permute-done.2
  1685.0 19.7 collective-permute-done.2
  1725.8 16.4 fusion.73
  1744.9 15.1 convolution_bitcast_fusion.1
  1760.0 36.4 reshape.229
  1796.4 20.7 constant_dynamic-update-slice_fusion.3
  1823.2 9.7 reshape.230
  1832.9 44.6 %reshape.231 = f32[16,100,2,3200]{3,2,1,0:T(2,128)} reshape(f32[1600,6400]{1,0:T(8,128)} %fusion.73) | data formatting | bytes 81920000 | tf_op jit(solution)/shard_map/reshape | solution.py:64
  1877.4 31.5 copy.45
  1908.9 34.5 copy.54
  1944.9 18.6 convolution_bitcast_fusion.2
  1963.7 55.3 %reshape.233 = f32[32,320000]{1,0:T(8,128)} reshape(f32[16,2,400,800]{3,2,1,0:T(8,128)} %convolution_bitcast_fusion.2) | data formatting | bytes 81920000 | tf_op jit(solution)/shard_map/reshape | solution.py:65
  2031.1 27.9 constant_dynamic-update-slice_fusion.1
  2059.0 27.7 constant_dynamic-update-slice_fusion
  2091.8 14.9 fusion.35
  2106.7 1710.3 %all-reduce.5.cloned.1.call-done = f32[32,960600]{1,0:T(8,128)} async-done(((f32[32,960600]{1,0:T(8,128)}), f32[32,960600]{1,0:T(8,128)}) %all-reduce.5.cloned.1.call-update) | async-done | bytes 122956816
  3817.1 12.0 dynamic-slice_reduce_fusion.2
  3834.3 16.9 dynamic-slice_reduce_fusion
  (494 shorter events, 524.8 us)
Async XLA Ops:
  7.9 204.7 %all-gather.27.cloned.1.call-start = ((), (), s32[]{:S(2)}) async-start(), calls=%async_computation.4 | async-start | bytes 17199104 | tf_op jit(solution)/shard_map/all_gather | solution.py:105
  13.5 228.0 %all-gather.33.cloned.1.call-start = ((), (), s32[]{:S(2)}) async-start(), calls=%async_computation.7 | async-start | bytes 2150400 | tf_op jit(solution)/shard_map/all_gather | solution.py:99
  14.2 312.5 %all-gather.29.cloned.1.call-start = ((), (), s32[]{:S(2)}) async-start(), calls=%async_computation.5 | async-start | bytes 5883904 | tf_op jit(solution)/shard_map/all_gather | solution.py:106
  17.7 533.5 %all-gather.31.cloned.1.call-start = ((), (), s32[]{:S(2)}) async-start(), calls=%async_computation.6 | async-start | bytes 22630400 | tf_op jit(solution)/shard_map/all_gather | solution.py:107
  21.8 649.1 %all-gather.19.cloned.1.call-start = ((), (), s32[]{:S(2)}) async-start(), calls=%async_computation | async-start | bytes 6963200 | tf_op jit(solution)/shard_map/all_gather | solution.py:147
  239.9 551.3 %all-gather.21.cloned.1.call-start = ((), (), s32[]{:S(2)}) async-start(), calls=%async_computation.1 | async-start | bytes 6963200 | tf_op jit(solution)/shard_map/all_gather | solution.py:148
  241.5 785.8 %all-gather.25.cloned.1.call-start = ((), (), s32[]{:S(2)}) async-start(), calls=%async_computation.3 | async-start | bytes 22630400 | tf_op jit(solution)/shard_map/all_gather | solution.py:108
  245.8 3571.2 %all-reduce.5.cloned.1.call-start = ((), (), s32[]{:S(2)}) async-start(), calls=%async_computation.8 | async-start | bytes 245923840
  1073.0 30.8 collective-permute-start.1
  1238.5 31.0 collective-permute-start.3
  1274.7 33.5 collective-permute-start.2
  1278.4 34.3 collective-permute-start.3
  1283.2 31.5 collective-permute-start
  1317.8 32.6 collective-permute-start.2
  1318.3 36.6 collective-permute-start.3
  1325.7 31.2 collective-permute-start
  1360.1 33.3 collective-permute-start.2
  1360.2 37.7 collective-permute-start.3
  1362.4 37.4 collective-permute-start
  1369.1 30.8 collective-permute-start.1
  1403.0 31.6 collective-permute-start.2
  1403.1 36.0 collective-permute-start.3
  1403.2 37.9 collective-permute-start
  1408.1 33.0 collective-permute-start.1
  1444.3 30.7 collective-permute-start.2
  1444.4 35.1 collective-permute-start.3
  1444.5 37.1 collective-permute-start
  1446.1 35.4 collective-permute-start.1
  1484.7 29.9 collective-permute-start.2
  1484.8 34.4 collective-permute-start.3
  1484.8 36.3 collective-permute-start
  1486.2 35.0 collective-permute-start.1
  1524.3 29.7 collective-permute-start.2
  1524.4 34.2 collective-permute-start.3
  1524.4 36.1 collective-permute-start
  1525.8 34.8 collective-permute-start.1
  1563.8 33.6 collective-permute-start.3
  1563.8 35.5 collective-permute-start
  1565.2 34.2 collective-permute-start.1
  1602.6 32.7 collective-permute-start.3
  1602.7 34.6 collective-permute-start
  1604.0 33.3 collective-permute-start.1
  1640.5 31.8 collective-permute-start.3
  1640.6 33.8 collective-permute-start
  1641.9 32.4 collective-permute-start.1
  1677.6 31.6 collective-permute-start.3
  1677.7 33.5 collective-permute-start
  1679.0 32.2 collective-permute-start.1
  (81 other events, 11557.1 us)
Sparse Core Ops, SparseCore 0:
  9.6 12.1 all-gather.22
  25.0 187.5 all-gather.26
  214.2 7.7 all-gather.32
  225.1 90.4 all-gather.28
  318.2 232.9 all-gather.30
  553.7 117.0 all-gather.18
  674.1 117.0 all-gather.20
  794.5 232.7 all-gather.24
  2091.2 1725.7 all-reduce.4
where the time goes:
time: 3880 us; the launch traced here: 3870 us
  waiting for transfers between devices  2770 us (71%)
  local copies, waits for them, and re-layouts  416 us (11%)
  starting transfers between devices  212 us (5%)
  matrix products  171 us (4%)
  blocking collectives  164 us (4%)
  other arithmetic  113 us (3%)
    unnamed x10, waiting for transfers between devices  1710 us
    ppermute x32, waiting for transfers between devices, passed_along(): return lax.ppermute(block, axis, route)  302 us
    all_gather x1, waiting for transfers between devices, shards(): lax.all_gather(columns[2], 'ctx', axis=0, tiled=True)  216 us
    all_gather x1, waiting for transfers between devices, shards(): lax.all_gather(columns[3], 'ctx', axis=0, tiled=True)  174 us
    unnamed x128, local copies, waits for them, and re-layouts  173 us
    ppermute x32, starting transfers between devices, shifted(): return lax.ppermute(block, axis, route)  147 us
    all_gather x1, waiting for transfers between devices, shards(): value_piece = lax.all_gather(values_own, 'ctx', axis=0, tiled=True)  120 us
    all_gather x1, waiting for transfers between devices, shards(): lax.all_gather(columns[0], 'ctx', axis=0, tiled=True)  108 us
  transfers between devices with their start and end apart: 73, of which 47 were waited for; matrix products, arithmetic and copies ran while one was open for 5% of the time, Pallas kernels for 0%

commit v1 on v0

v1 whole, which is shorter than its diff:
```python
import functools
import math

import jax
import jax.numpy as jnp
from jax import lax
from jax.experimental import pallas as pl
from jax.experimental.pallas import tpu as pltpu
from jax.sharding import PartitionSpec as P

D = 1600
HEADS = 25
HEAD_DIM = 64
FF = 6400
EPS = 1e-05
UNITS = 8
HU = -(-HEADS // UNITS)
QKV = 3 * HEAD_DIM
TP_BITS = (1, 4)
MESH = pl.DeviceIdType.MESH
BF = jnp.bfloat16
F32 = jnp.float32
VMEM_LIMIT = 56 * 1024 * 1024
LOG2E = 1.0 / math.log(2.0)


class Layout:
    def __init__(self, n_ctx):
        self.n_ctx = n_ctx
        self.tp_bits = TP_BITS
        bits = [1 << i for i in range(n_ctx.bit_length() - 1)]
        self.dp_bits = tuple(b for b in bits if b not in TP_BITS)[::-1]
        self.n_dp = n_ctx // 4
        self.dp_order = [(b, b) for b in self.dp_bits]
        a, b = TP_BITS
        self.tp_order = [(a, b), (b, a)]
        self.tp_masks = [[], [(a, a)], [(b, b)], [(a, a), (b, b)]]

    def tp_index(self, c):
        return sum(((c // b) % 2) * (1 << i) for i, b in enumerate(self.tp_bits))

    def dp_index(self, c):
        return sum(((c // b) % 2) * (1 << i) for i, b in enumerate(self.dp_bits))

    def compose(self, t, d):
        return sum(((t // (1 << i)) % 2) * b for i, b in enumerate(self.tp_bits)) + sum(
            ((d // (1 << i)) % 2) * b for i, b in enumerate(self.dp_bits)
        )

    def head_rank(self, h):
        u, j = h // HU, h % HU
        return self.compose(u // 2, j) * 2 + u % 2

    def to_natural(self, x):
        labels = list(self.dp_bits[::-1]) + list(self.tp_bits[::-1])
        k = len(labels)
        rest = x.shape[2:]
        x = x.reshape((2,) * k + rest)
        order = sorted(range(k), key=lambda i: -labels[i])
        x = jnp.transpose(x, order + list(range(k, k + len(rest))))
        return x.reshape((self.n_ctx,) + rest)

    def from_natural(self, x):
        labels = list(self.dp_bits[::-1]) + list(self.tp_bits[::-1])
        k = len(labels)
        rest = x.shape[1:]
        x = x.reshape((2,) * k + rest)
        natural = sorted(labels, reverse=True)
        order = [natural.index(b) for b in labels]
        x = jnp.transpose(x, order + list(range(k, k + len(rest))))
        return x.reshape((self.n_dp, 4) + rest)


def flip(c, sym, s):
    def one(b):
        return c + b * (1 - 2 * ((c // b) % 2))

    if sym[0] == sym[1]:
        return one(sym[0])
    return one(sym[0]) * (1 - s) + one(sym[1]) * s


def flips(c, masks, s):
    for sym in masks:
        c = flip(c, sym, s)
    return c


class Env:
    def __init__(self, layout):
        self.lay = layout
        self.c = lax.axis_index("ctx")
        self.s = lax.axis_index("fsdp")
        self.t = layout.tp_index(self.c)
        self.d = layout.dp_index(self.c)
        self.rank = self.c * 2 + self.s
        self.n_dev = layout.n_ctx * 2

    def other(self):
        return (self.c, 1 - self.s)


class Links:
    def __init__(self, sems):
        self.send_sems, self.recv_sems, self.local_sems = sems
        self.count = 0
        self.local_count = 0
        self.sent = []
        self.locals = []

    def send(self, src, dst, device):
        copy = pltpu.make_async_remote_copy(
            src_ref=src,
            dst_ref=dst,
            send_sem=self.send_sems.at[self.count],
            recv_sem=self.recv_sems.at[self.count],
            device_id=device,
            device_id_type=MESH,
        )
        copy.start()
        self.count += 1
        self.sent.append(copy)
        return copy

    def local(self, src, dst):
        copy = pltpu.make_async_copy(src, dst, self.local_sems.at[self.local_count])
        copy.start()
        self.local_count += 1
        self.locals.append(copy)
        return copy

    def finish(self):
        for copy in self.locals:
            copy.wait()
        for copy in self.sent:
            copy.wait_send()


def sem_shapes(sends, local=1):
    sends = max(sends, 1)
    return [
        pltpu.SemaphoreType.DMA((sends,)),
        pltpu.SemaphoreType.DMA((sends,)),
        pltpu.SemaphoreType.DMA((local,)),
    ]


def meet(env, devices):
    barrier = pltpu.get_barrier_semaphore()
    for device in devices:
        pl.semaphore_signal(barrier, inc=1, device_id=device, device_id_type=MESH)
    pl.semaphore_wait(barrier, len(devices))


def meet_all(env):
    barrier = pltpu.get_barrier_semaphore()

    def hail(i, carry):
        rank = (env.rank + i) % env.n_dev
        pl.semaphore_signal(barrier, inc=1, device_id=(rank // 2, rank % 2), device_id_type=MESH)
        return carry

    lax.fori_loop(1, env.n_dev, hail, 0)
    pl.semaphore_wait(barrier, env.n_dev - 1)


def tp_partners(env):
    return [(flips(env.c, m, env.s), env.s) for m in env.lay.tp_masks[1:]]


def dp_partners(env):
    return [(flip(env.c, sym, env.s), env.s) for sym in env.lay.dp_order]


def run(generators):
    active = list(generators)
    while active:
        left = []
        for g in active:
            try:
                next(g)
                left.append(g)
            except StopIteration:
                pass
        active = left


def gather_sends(have, bits, core, rows):
    return (3 if rows else 0) + have * ((1 << bits) - 1) + (have << bits if core else 0)


def gather(env, src, buf, sems, bits, slot, core=False, rows=False):
    c, s = env.c, env.s
    links = Links(sems)

    def place(masks):
        index = slot(flips(c, masks, s))
        return buf.at[s, index] if core else buf.at[index]

    own = src.at[env.t] if rows else src
    links.local(own, place([]))
    levels = [[([], None)]] + [[] for _ in bits]
    if rows:
        for m in env.lay.tp_masks[1:]:
            there = flips(c, m, s)
            copy = links.send(src.at[env.lay.tp_index(there)], place([]), (there, s))
            levels[0].append((m, copy))
    crossing = []
    for k in range(len(bits) + 1):
        for masks, copy in levels[k]:
            if copy is None:
                ref = own
            else:
                copy.wait_recv()
                ref = place(masks)
            for j in range(k, len(bits)):
                forward = links.send(ref, place(masks), (flip(c, bits[j], s), s))
                levels[j + 1].append((masks + [bits[j]], forward))
            if core:
                crossing.append(links.send(ref, place(masks), env.other()))
            yield
    for copy in crossing:
        copy.wait_recv()
    links.finish()
    yield


def reduce_sends(have, bits, core, rows, halves):
    return (have << bits if core else 0) + have * ((1 << bits) - 1) + (3 + 4 if rows else 0) + (1 if halves else 0)


def reduce_scratch(have, bits, core, block):
    counts = [have << j for j in range(bits + (1 if core else 0))]
    return [pltpu.VMEM((n,) + block, BF) for n in counts]


def reduce(env, inp, out, parts, sems, bits, slot, core=False, rows=False, halves=False):
    c, s = env.c, env.s
    links = Links(sems)
    levels = [list(env.lay.tp_masks) if rows else [[]]]
    for sym in bits:
        levels.append(levels[-1] + [m + [sym] for m in levels[-1]])

    def at(side, masks):
        index = slot(flips(c, masks, side))
        return inp.at[side, index] if core else inp.at[index]

    last = levels[-1]
    now = [at(s, m) for m in last]
    copies = {}
    if core:
        stage = len(bits)
        for i in reversed(range(len(last))):
            copies[i] = links.send(at(1 - s, last[i]), parts[stage].at[i], env.other())
    else:
        stage = len(bits) - 1
        n = len(levels[stage])
        for i in reversed(range(n)):
            copies[i] = links.send(now[n + i], parts[stage].at[i], (flip(c, bits[stage], s), s))
    yield
    while stage >= 0:
        n = len(levels[stage])
        got = parts[stage]
        after = {}
        for i in reversed(range(n)):
            copies[i].wait_recv()
            got[i] = got[i] + now[i][...]
            if stage > 0 and i >= n // 2:
                after[i - n // 2] = links.send(
                    got.at[i], parts[stage - 1].at[i - n // 2], (flip(c, bits[stage - 1], s), s)
                )
            yield
        now = [got.at[i] for i in range(n)]
        copies = after
        stage -= 1
    if rows:
        arrivals = []
        links.local(now[0], out.at[s, env.t])
        arrivals.append((env.t, None, now[0]))
        for i, m in enumerate(env.lay.tp_masks):
            if i > 0:
                there = flips(c, m, s)
                copy = links.send(now[i], out.at[s, env.t], (there, s))
                index = env.lay.tp_index(there)
                arrivals.append((index, copy, out.at[s, index]))
        yield
        crossing = []
        for index, copy, ref in arrivals:
            if copy is not None:
                copy.wait_recv()
            crossing.append(links.send(ref, out.at[s, index], env.other()))
            yield
        for copy in crossing:
            copy.wait_recv()
    elif halves:
        links.local(now[0], out.at[s])
        copy = links.send(now[0], out.at[s], env.other())
        yield
        copy.wait_recv()
    else:
        out[...] = now[0][...]
    links.finish()
    yield


def to_everyone(env, src, out, sems, same):
    send_sems, recv_sems, local_sems = sems

    def own(ref):
        return ref if same else ref.at[env.rank]

    def copy(i):
        rank = (env.rank + i) % env.n_dev
        return pltpu.make_async_remote_copy(
            src_ref=src if same else src.at[rank],
            dst_ref=out.at[env.rank],
            send_sem=send_sems.at[i],
            recv_sem=recv_sems.at[i],
            device_id=(rank // 2, rank % 2),
            device_id_type=MESH,
        )

    def begin(i, carry):
        copy(i).start()
        return carry

    def end(i, carry):
        copy(i).wait()
        return carry

    lax.fori_loop(1, env.n_dev, begin, 0)
    local = pltpu.make_async_copy(own(src), out.at[env.rank], local_sems.at[0])
    local.start()
    yield
    lax.fori_loop(1, env.n_dev, end, 0)
    local.wait()
    yield


def own_head(env):
    h = (env.t * 2 + env.s) * HU + env.d
    return h, jnp.logical_and(env.d < HU, h < HEADS)


def heads_to_tokens(env, src, out, sems):
    send_sems, recv_sems, local_sems = sems
    h, active = own_head(env)
    lay = env.lay

    def copy(i):
        rank = (env.rank + i) % env.n_dev
        return pltpu.make_async_remote_copy(
            src_ref=src.at[rank % 2, rank // 2],
            dst_ref=out.at[h],
            send_sem=send_sems.at[i],
            recv_sem=recv_sems.at[h],
            device_id=(rank // 2, rank % 2),
            device_id_type=MESH,
        )

    @pl.when(active)
    def _():
        def begin(i, carry):
            copy(i).start()
            return carry

        lax.fori_loop(1, env.n_dev, begin, 0)
        local = pltpu.make_async_copy(src.at[env.s, env.c], out.at[h], local_sems.at[0])
        local.start()
        local.wait()

    def receive(j, carry):
        @pl.when(lay.head_rank(j) != env.rank)
        def _():
            pltpu.make_async_remote_copy(
                src_ref=src.at[0, 0],
                dst_ref=out.at[j],
                send_sem=send_sems.at[0],
                recv_sem=recv_sems.at[j],
                device_id=env.other(),
                device_id_type=MESH,
            ).wait_recv()

        return carry

    lax.fori_loop(0, HEADS, receive, 0)

    @pl.when(active)
    def _():
        def end(i, carry):
            copy(i).wait_send()
            return carry

        lax.fori_loop(1, env.n_dev, end, 0)


def tokens_to_heads(env, src, out, sems):
    send_sems, recv_sems, local_sems = sems
    h, active = own_head(env)
    lay = env.lay

    def copy(j):
        rank = lay.head_rank(j)
        return rank, pltpu.make_async_remote_copy(
            src_ref=src.at[j],
            dst_ref=out.at[env.s, env.c],
            send_sem=send_sems.at[j],
            recv_sem=recv_sems.at[(rank - env.rank + env.n_dev) % env.n_dev],
            device_id=(rank // 2, rank % 2),
            device_id_type=MESH,
        )

    def begin(i, carry):
        rank, cp = copy((env.rank + i) % HEADS)

        @pl.when(rank != env.rank)
        def _():
            cp.start()

        return carry

    lax.fori_loop(0, HEADS, begin, 0)

    @pl.when(active)
    def _():
        local = pltpu.make_async_copy(src.at[h], out.at[env.s, env.c], local_sems.at[0])
        local.start()
        local.wait()

        def receive(i, carry):
            rank = (env.rank - i + env.n_dev) % env.n_dev
            pltpu.make_async_remote_copy(
                src_ref=src.at[0],
                dst_ref=out.at[rank % 2, rank // 2],
                send_sem=send_sems.at[0],
                recv_sem=recv_sems.at[i],
                device_id=env.other(),
                device_id_type=MESH,
            ).wait_recv()
            return carry

        lax.fori_loop(1, env.n_dev, receive, 0)

    def end(j, carry):
        rank, cp = copy(j)

        @pl.when(rank != env.rank)
        def _():
            cp.wait_send()

        return carry

    lax.fori_loop(0, HEADS, end, 0)


def data_partners(env):
    lay = env.lay
    return [(lay.compose(env.t, (env.d + i) % lay.n_dp), env.s) for i in range(1, lay.n_dp)]


def group_to_heads(env, src, out, sems):
    send_sems, recv_sems, local_sems = sems
    lay = env.lay

    def copy(j, source, target):
        return pltpu.make_async_remote_copy(
            src_ref=src.at[j],
            dst_ref=out.at[source],
            send_sem=send_sems.at[j],
            recv_sem=recv_sems.at[source],
            device_id=(lay.compose(env.t, target), env.s),
            device_id_type=MESH,
        )

    for i in range(1, HU + 1):
        j = (env.d + i) % HU

        @pl.when(j != env.d)
        def _():
            copy(j, env.d, j).start()

    @pl.when(env.d < HU)
    def _():
        local = pltpu.make_async_copy(src.at[env.d], out.at[env.d], local_sems.at[0])
        local.start()
        local.wait()
        for i in range(1, lay.n_dp):
            source = (env.d + i) % lay.n_dp
            copy(0, source, source).wait_recv()

    for j in range(HU):

        @pl.when(j != env.d)
        def _():
            copy(j, env.d, j).wait_send()


def heads_to_group(env, src, out, sems):
    send_sems, recv_sems, local_sems = sems
    lay = env.lay

    def copy(there, j, target):
        return pltpu.make_async_remote_copy(
            src_ref=src.at[there],
            dst_ref=out.at[j],
            send_sem=send_sems.at[there],
            recv_sem=recv_sems.at[j],
            device_id=(lay.compose(env.t, target), env.s),
            device_id_type=MESH,
        )

    @pl.when(env.d < HU)
    def _():
        for i in range(1, lay.n_dp):
            there = (env.d + i) % lay.n_dp
            copy(there, env.d, there).start()
        local = pltpu.make_async_copy(src.at[env.d], out.at[env.d], local_sems.at[0])
        local.start()
        local.wait()

    for j in range(HU):

        @pl.when(j != env.d)
        def _():
            copy(0, j, j).wait_recv()

    @pl.when(env.d < HU)
    def _():
        for i in range(1, lay.n_dp):
            there = (env.d + i) % lay.n_dp
            copy(there, env.d, there).wait_send()


ANY = pl.BlockSpec(memory_space=pl.ANY)
VM = pl.BlockSpec(memory_space=pltpu.VMEM)


def struct(*shape, dtype=BF):
    return jax.ShapeDtypeStruct(shape, dtype)


def call(name, cid, body, args, in_specs, outs, out_specs, scratch):
    return pl.pallas_call(
        body,
        out_shape=outs,
        in_specs=in_specs,
        out_specs=out_specs,
        scratch_shapes=scratch,
        compiler_params=pltpu.CompilerParams(
            collective_id=cid, has_side_effects=True, vmem_limit_bytes=VMEM_LIMIT
        ),
        name=name,
    )(*args)


def exchange_start(lay, small, qkv, fc, out):
    def body(small_r, qkv_r, fc_r, out_r, small_o, qkv_o, fc_o, out_o, *sems):
        env = Env(lay)
        meet_all(env)
        links = Links((sems[0], sems[1], sems[2]))
        copies = [
            links.send(a, b, env.other()) for a, b in ((qkv_r, qkv_o), (fc_r, fc_o), (out_r, out_o))
        ]
        run([to_everyone(env, small_r, small_o, sems[3:6], True)])
        for copy in copies:
            copy.wait_recv()
        links.finish()

    n_dev = lay.n_ctx * 2
    return call(
        "exchange_start",
        0,
        body,
        (small, qkv, fc, out),
        [ANY] * 4,
        [struct(n_dev, *small.shape), struct(*qkv.shape), struct(*fc.shape), struct(*out.shape)],
        [ANY] * 4,
        sem_shapes(3) + sem_shapes(n_dev),
    )


def gather_weights(lay, qkv, fc, out, proj, h1, dy):
    n_ctx, n_dp = lay.n_ctx, lay.n_dp
    k = len(lay.dp_bits)

    def natural(c):
        return c

    def body(qkv_r, fc_r, out_r, proj_r, h1_r, dy_r, qkv_o, fc_o, out_o, proj_o, h1_o, dy_o, *sems):
        env = Env(lay)
        meet(env, tp_partners(env) + dp_partners(env) + [env.other()])
        groups = [sems[3 * i : 3 * i + 3] for i in range(6)]
        run(
            [
                gather(env, qkv_r, qkv_o, groups[0], lay.dp_order, natural, rows=True),
                gather(env, h1_r, h1_o, groups[4], lay.tp_order, lay.tp_index, core=True),
                gather(env, proj_r, proj_o, groups[3], lay.dp_order + lay.tp_order, natural, core=True),
                gather(env, fc_r, fc_o, groups[1], lay.dp_order, natural, rows=True),
                gather(env, out_r, out_o, groups[2], lay.dp_order, lay.dp_index),
                gather(env, dy_r, dy_o, groups[5], lay.tp_order, lay.tp_index, core=True),
            ]
        )

    outs = [
        struct(n_ctx, *qkv.shape[1:]),
        struct(n_ctx, *fc.shape[1:]),
        struct(n_dp, *out.shape),
        struct(2, n_ctx, *proj.shape),
        struct(2, 4, *h1.shape),
        struct(2, 4, *dy.shape),
    ]
    scratch = (
        sem_shapes(gather_sends(4, k, False, True)) * 2
        + sem_shapes(gather_sends(1, k, False, False))
        + sem_shapes(gather_sends(1, k + 2, True, False))
        + sem_shapes(gather_sends(1, 2, True, False)) * 2
    )
    return call(
        "gather_weights", 1, body, (qkv, fc, out, proj, h1, dy), [ANY] * 6, outs, [ANY] * 6, scratch
    )


def gather_rows(lay, h2):
    def body(h2_r, h2_o, *sems):
        env = Env(lay)
        meet(env, tp_partners(env) + [env.other()])
        run([gather(env, h2_r, h2_o, sems, lay.tp_order, lay.tp_index, core=True)])

    return call(
        "gather_rows",
        2,
        body,
        (h2,),
        [ANY],
        struct(2, 4, *h2.shape),
        ANY,
        sem_shapes(gather_sends(1, 2, True, False)),
    )


def reduce_rows(lay, first, second):
    block = first.shape[2:]

    def body(a_r, b_r, a_o, b_o, *rest):
        env = Env(lay)
        meet(env, tp_partners(env) + [env.other()])
        run(
            [
                reduce(env, a_r, a_o, rest[0:3], rest[6:9], lay.tp_order, lay.tp_index, core=True),
                reduce(env, b_r, b_o, rest[3:6], rest[9:12], lay.tp_order, lay.tp_index, core=True),
            ]
        )

    return call(
        "reduce_rows",
        3,
        body,
        (first, second),
        [VM] * 2,
        [struct(*block)] * 2,
        [VM] * 2,
        reduce_scratch(1, 2, True, block) * 2 + sem_shapes(reduce_sends(1, 2, True, False, False)) * 2,
    )


def exchange(lay, name, cid, op, partners, src, out, counts):
    def body(src_r, out_r, *sems):
        env = Env(lay)
        if partners is None:
            meet_all(env)
        else:
            meet(env, partners(env))
        op(env, src_r, out_r, sems)

    scratch = [
        pltpu.SemaphoreType.DMA((counts[0],)),
        pltpu.SemaphoreType.DMA((counts[1],)),
        pltpu.SemaphoreType.DMA((1,)),
    ]
    return call(name, cid, body, (src,), [ANY], out, ANY, scratch)


def reduce_grads(lay, rows, qkv, fc, out, proj, small):
    n_ctx = lay.n_ctx
    k = len(lay.dp_bits)
    n_dev = 2 * n_ctx

    def natural(c):
        return c

    plan = [
        (rows.shape[2:], 1, 2, True, False, False),
        (qkv.shape[1:], 4, k, False, True, False),
        (fc.shape[1:], 4, k, False, True, False),
        (out.shape[1:], 1, k, False, False, True),
        (proj.shape[2:], 1, k + 2, True, False, False),
    ]
    scratch, spans = [], []
    for block, have, bits, core, is_rows, halves in plan:
        part = reduce_scratch(have, bits, core, block)
        sems = sem_shapes(reduce_sends(have, bits, core, is_rows, halves))
        spans.append((len(scratch), len(part)))
        scratch = scratch + part + sems
    scratch = scratch + sem_shapes(n_dev)

    def body(rows_r, qkv_r, fc_r, out_r, proj_r, small_r, rows_o, qkv_o, fc_o, out_o, proj_o, small_o, *rest):
        env = Env(lay)
        meet_all(env)

        def space(i):
            first, n = spans[i]
            return rest[first : first + n], rest[first + n : first + n + 3]

        run(
            [
                to_everyone(env, small_r, small_o, rest[-3:], False),
                reduce(env, qkv_r, qkv_o, *space(1), lay.dp_order, natural, rows=True),
                reduce(env, rows_r, rows_o, *space(0), lay.tp_order, lay.tp_index, core=True),
                reduce(env, proj_r, proj_o, *space(4), lay.dp_order + lay.tp_order, natural, core=True),
                reduce(env, fc_r, fc_o, *space(2), lay.dp_order, natural, rows=True),
                reduce(env, out_r, out_o, *space(3), lay.dp_order, lay.dp_index, halves=True),
            ]
        )

    outs = [
        struct(*rows.shape[2:]),
        struct(2, 4, *qkv.shape[1:]),
        struct(2, 4, *fc.shape[1:]),
        struct(2, *out.shape[1:]),
        struct(*proj.shape[2:]),
        struct(*small.shape, dtype=F32),
    ]
    return call(
        "reduce_grads",
        8,
        body,
        (rows, qkv, fc, out, proj, small),
        [VM] * 5 + [ANY],
        outs,
        [VM, ANY, ANY, ANY, VM, ANY],
        scratch,
    )


def dot(left, right, dims):
    return lax.dot_general(left, right, (dims, ((), ())), preferred_element_type=F32)


NN = ((1,), (0,))
NT = ((1,), (1,))
TN = ((0,), (0,))
SCALE = 1.0 / math.sqrt(HEAD_DIM)
TILE = 512


def attend(lay, q, k, v, rows):
    length = q.shape[2]
    tile = min(TILE, length)
    n = length // tile
    per = tile // rows

    def body(q_ref, k_ref, v_ref, o_ref, low_ref, lse_ref, keys):
        i = pl.program_id(1)

        @pl.when(i == 0)
        def _():
            keys[...] = k_ref[0].T

        qt = q_ref[0]

        def step(j, carry, masked):
            peak, total, acc = carry
            first = pl.multiple_of(j * tile, tile)
            st = dot(keys[pl.ds(first, tile), :], qt, NN) * (SCALE * LOG2E)
            if masked:
                row = lax.broadcasted_iota(jnp.int32, (tile, tile), 0)
                col = lax.broadcasted_iota(jnp.int32, (tile, tile), 1)
                st = jnp.where(row <= col, st, -1e30)
            new = jnp.maximum(peak, jnp.max(st, axis=0, keepdims=True))
            p = jnp.exp2(st - new)
            shrink = jnp.exp2(peak - new)
            total = total * shrink + jnp.sum(p, axis=0, keepdims=True)
            acc = acc * shrink + dot(v_ref[0, :, pl.ds(first, tile)], p.astype(BF), NN)
            return new, total, acc

        start = (
            jnp.full((1, tile), -1e30, F32),
            jnp.zeros((1, tile), F32),
            jnp.zeros((HEAD_DIM, tile), F32),
        )
        carry = lax.fori_loop(0, i, functools.partial(step, masked=False), start)
        peak, total, acc = step(i, carry, True)
        o = acc / total
        o_ref[0] = o
        low = o.astype(BF)
        for b in range(per):
            low_ref[0, b] = low[:, b * rows : (b + 1) * rows]
        lse_ref[0] = peak + jnp.log2(total)

    whole = pl.BlockSpec((1, HEAD_DIM, length), lambda b, i: (b, 0, 0))
    tiled = pl.BlockSpec((1, HEAD_DIM, tile), lambda b, i: (b, 0, i))
    return pl.pallas_call(
        body,
        grid=(2, n),
        in_specs=[tiled, whole, whole],
        out_specs=[
            tiled,
            pl.BlockSpec((1, per, HEAD_DIM, rows), lambda b, i: (b, i, 0, 0)),
            pl.BlockSpec((1, 1, tile), lambda b, i: (b, 0, i)),
        ],
        out_shape=[
            struct(2, HEAD_DIM, length, dtype=F32),
            struct(2, length // rows, HEAD_DIM, rows),
            struct(2, 1, length, dtype=F32),
        ],
        scratch_shapes=[pltpu.VMEM((length, HEAD_DIM), BF)],
        compiler_params=pltpu.CompilerParams(vmem_limit_bytes=VMEM_LIMIT),
        name="attend",
    )(q, k, v)


def attend_back(lay, q, k, v, o, lse, dob):
    length = q.shape[2]
    tile = min(TILE, length)
    n = length // tile

    def body(q_ref, k_ref, v_ref, o_ref, lse_ref, dob_ref, dq_ref, dk_ref, dv_ref, qs, dobs, delta, dq_acc):
        j = pl.program_id(1)

        @pl.when(j == 0)
        def _():
            qs[...] = q_ref[0].T
            dobs[...] = dob_ref[0].T
            delta[...] = jnp.sum(dob_ref[0].astype(F32) * o_ref[0], axis=0, keepdims=True)
            dq_acc[...] = jnp.zeros_like(dq_acc)

        kt = k_ref[0]
        keys = kt.T
        values = v_ref[0].T

        def step(i, carry, masked):
            dk, dv = carry
            at = pl.ds(pl.multiple_of(i * tile, tile), tile)
            st = dot(keys, q_ref[0, :, at], NN) * (SCALE * LOG2E)
            p = jnp.exp2(st - lse_ref[0, :, at])
            if masked:
                row = lax.broadcasted_iota(jnp.int32, (tile, tile), 0)
                col = lax.broadcasted_iota(jnp.int32, (tile, tile), 1)
                p = jnp.where(row <= col, p, 0.0)
            dp = dot(values, dob_ref[0, :, at], NN)
            ds = (p * (dp - delta[:, at])).astype(BF)
            dv = dv + dot(p.astype(BF), dobs[at, :], NN)
            dk = dk + dot(ds, qs[at, :], NN)
            dq_acc[:, at] += dot(kt, ds, NN)
            return dk, dv

        zero = jnp.zeros((tile, HEAD_DIM), F32)
        carry = step(j, (zero, zero), True)
        dk, dv = lax.fori_loop(j + 1, n, functools.partial(step, masked=False), carry)
        dk_ref[0] = (dk * SCALE).T.astype(BF)
        dv_ref[0] = dv.T.astype(BF)

        @pl.when(j == n - 1)
        def _():
            dq_ref[0] = (dq_acc[...] * SCALE).astype(BF)

    whole = pl.BlockSpec((1, HEAD_DIM, length), lambda b, i: (b, 0, 0))
    tiled = pl.BlockSpec((1, HEAD_DIM, tile), lambda b, i: (b, 0, i))
    line = pl.BlockSpec((1, 1, length), lambda b, i: (b, 0, 0))
    return pl.pallas_call(
        body,
        grid=(2, n),
        in_specs=[whole, tiled, tiled, whole, line, whole],
        out_specs=[whole, tiled, tiled],
        out_shape=[struct(2, HEAD_DIM, length)] * 3,
        scratch_shapes=[
            pltpu.VMEM((length, HEAD_DIM), BF),
            pltpu.VMEM((length, HEAD_DIM), BF),
            pltpu.VMEM((1, length), F32),
            pltpu.VMEM((HEAD_DIM, length), F32),
        ],
        compiler_params=pltpu.CompilerParams(vmem_limit_bytes=VMEM_LIMIT),
        name="attend_back",
    )(q, k, v, o, lse, dob)


def norm_forward(values, gain, bias):
    centre = values - jnp.mean(values, axis=-1, keepdims=True)
    spread = lax.rsqrt(jnp.mean(centre * centre, axis=-1, keepdims=True) + EPS)
    normed = centre * spread
    return (normed * gain + bias, normed, spread)


def norm_back(grad_out, normed, spread, gain):
    scaled = grad_out * gain
    grad_in = spread * (
        scaled
        - jnp.mean(scaled, axis=-1, keepdims=True)
        - normed * jnp.mean(scaled * normed, axis=-1, keepdims=True)
    )
    return (grad_in, jnp.sum(grad_out * normed, axis=0), jnp.sum(grad_out, axis=0))


def gelu_tanh(values):
    return jax.nn.gelu(values, approximate=True)


def pad_to(x, axis, size):
    if x.shape[axis] == size:
        return x
    widths = [(0, 0)] * x.ndim
    widths[axis] = (0, size - x.shape[axis])
    return jnp.pad(x, widths)


def shards(lay, tokens, qkv_weight, proj_weight, fc_weight, out_weight, gains, biases, fc_bias, cotangent):
    n_ctx, n_dp = lay.n_ctx, lay.n_dp
    c = lax.axis_index("ctx")
    s = lax.axis_index("fsdp")
    t = lay.tp_index(c)
    unit = 2 * t + s
    T = tokens.shape[1]
    M = 8 * T
    R = D // n_ctx
    FB = FF // n_ctx
    FH = FB // 2
    W = HU * HEAD_DIM
    length = n_ctx * T

    def both(own, other, axis):
        return jnp.where(
            s == 0, jnp.concatenate([own, other], axis), jnp.concatenate([other, own], axis)
        )

    def side(x, axis):
        return lax.dynamic_index_in_dim(x, s, axis, keepdims=False)

    x = tokens.reshape(T, D).astype(F32)
    dy = cotangent.reshape(T, D)

    small = jnp.concatenate([gains.reshape(-1), biases.reshape(-1), fc_bias])
    small = pad_to(small, 0, 2048).reshape(16, 128)
    small_all, qkv_other, fc_other, out_other = exchange_start(
        lay, small, qkv_weight, fc_weight, out_weight
    )
    small_all = small_all.reshape(n_ctx, 2, 2048)
    gain_rows = jnp.transpose(small_all[:, :, :R], (1, 0, 2)).reshape(2, D).astype(F32)
    bias_rows = (
        jnp.transpose(small_all[:, :, R : 4 * R].reshape(n_ctx, 2, 3, R), (1, 2, 0, 3))
        .reshape(6, D)
        .astype(F32)
    )
    fcb = side(small_all[:, :, 4 * R : 4 * R + FH], 1)
    fc_shift = lax.dynamic_index_in_dim(
        lay.from_natural(fcb), t, 1, keepdims=False
    ).reshape(n_dp * FH).astype(F32)

    normed_one, hat_one, spread_one = norm_forward(x, gain_rows[0], bias_rows[0])
    h1 = normed_one.astype(BF)

    qkv_full = both(qkv_weight, qkv_other, 1).reshape(R, 3, D)
    qkv_full = pad_to(qkv_full, 2, UNITS * W).reshape(R, 3, 4, 2, W)
    qkv_src = jnp.transpose(side(qkv_full, 3), (2, 0, 1, 3)).reshape(4, R, 3 * W)
    fc_full = side(both(fc_weight, fc_other, 1).reshape(R, n_ctx, 2, FH), 2)
    fc_src = jnp.stack(
        [
            jnp.concatenate([fc_full[:, lay.compose(u, d)] for d in range(n_dp)], axis=1)
            for u in range(4)
        ]
    )
    out_src = side(both(out_weight, out_other, 1).reshape(2, FH, D), 0)

    qkv_buf, fc_buf, out_buf, proj_buf, h1_all, dy_all = gather_weights(
        lay, qkv_src, fc_src, out_src, proj_weight, h1, dy
    )
    w_qkv = qkv_buf.reshape(D, 3 * W)
    w_fc = fc_buf.reshape(D, n_dp * FH)
    w_out = out_buf.reshape(n_dp * FH, D)
    w_proj = jnp.transpose(proj_buf, (1, 2, 0, 3)).reshape(D, D)
    h1_rows = h1_all.reshape(M, D)
    dy_rows = dy_all.reshape(M, D)

    def unit_bias(row):
        return lax.dynamic_slice_in_dim(pad_to(row, 0, UNITS * W), unit * W, W)

    shift = jnp.concatenate([unit_bias(bias_rows[1]), jnp.zeros((W,), F32), unit_bias(bias_rows[2])])
    qkv = (dot(w_qkv, h1_rows, ((0,), (1,))) + shift[:, None]).astype(BF)
    qkv = jnp.transpose(qkv.reshape(3, HU, HEAD_DIM, M), (1, 0, 2, 3)).reshape(HU, QKV, M)
    mine = exchange(
        lay, "group_to_heads", 4, group_to_heads, data_partners, qkv, struct(n_dp, QKV, M), (HU, n_dp)
    )
    mine = jnp.transpose(mine.reshape(n_dp, 3, HEAD_DIM, 2, 4, T), (0, 4, 1, 3, 2, 5))
    mine = jnp.transpose(lay.to_natural(mine), (1, 2, 3, 0, 4)).reshape(3, 2, HEAD_DIM, length)
    q, k, v = mine[0], mine[1], mine[2]
    o, o_low, lse = attend(lay, q, k, v, T)
    n_dev = 2 * n_ctx
    ob = exchange(
        lay,
        "heads_to_tokens",
        5,
        heads_to_tokens,
        None,
        o_low,
        struct(HEADS, HEAD_DIM, T),
        (n_dev, HEADS),
    ).reshape(D, T)
    x1 = x + dot(ob, w_proj, TN) + bias_rows[3]
    normed_two, hat_two, spread_two = norm_forward(x1, gain_rows[1], bias_rows[4])
    h2_rows = gather_rows(lay, normed_two.astype(BF)).reshape(M, D)
    hidden_pre = dot(h2_rows, w_fc, NN) + fc_shift
    hidden, gelu_back = jax.vjp(gelu_tanh, hidden_pre)
    gb = hidden.astype(BF)
    mixed_part = dot(gb, w_out, NN).astype(BF).reshape(2, 4, T, D)
    du = gelu_back(dot(dy_rows, w_out, NT))[0].astype(BF)
    dh2_part = dot(du, w_fc, NT).astype(BF).reshape(2, 4, T, D)
    mixed_sum, dh2 = reduce_rows(lay, mixed_part, dh2_part)
    fc_grad = dot(h2_rows, du, TN).astype(BF).reshape(n_ctx, R, n_dp * FH)
    out_grad = dot(gb, dy_rows, TN).astype(BF).reshape(n_dp, FH, D)
    fc_bias_part = jnp.sum(du.astype(F32), axis=0)
    mixed = (x1 + mixed_sum.astype(F32) + bias_rows[5]).astype(BF)
    back_two, gain_two_g, bias_two_g = norm_back(dh2.astype(F32), hat_two, spread_two, gain_rows[1])
    dx1 = dy.astype(F32) + back_two
    da = dx1.astype(BF)
    proj_grad = jnp.transpose(dot(ob, da, NN).astype(BF).reshape(n_ctx, R, 2, D // 2), (2, 0, 1, 3))
    proj_bias_g = jnp.sum(da.astype(F32), axis=0)
    dob = dot(w_proj, da, NT).astype(BF).reshape(HEADS, HEAD_DIM, T)
    dob = exchange(
        lay,
        "tokens_to_heads",
        6,
        tokens_to_heads,
        None,
        dob,
        struct(2, n_ctx, HEAD_DIM, T),
        (HEADS, n_dev),
    )
    dob = jnp.transpose(dob, (0, 2, 1, 3)).reshape(2, HEAD_DIM, length)
    dq, dk, dv = attend_back(lay, q, k, v, o, lse, dob)
    grads = jnp.stack([dq, dk, dv]).reshape(3, 2, HEAD_DIM, n_ctx, T)
    grads = lay.from_natural(jnp.transpose(grads, (3, 0, 2, 1, 4)))
    grads = jnp.transpose(grads, (0, 2, 3, 4, 1, 5)).reshape(n_dp, QKV, M)
    dqkv = exchange(
        lay, "heads_to_group", 7, heads_to_group, data_partners, grads, struct(HU, QKV, M), (n_dp, HU)
    )
    dqkv = jnp.transpose(dqkv.reshape(HU, 3, HEAD_DIM, M), (1, 0, 2, 3)).reshape(3 * W, M)
    dh1_part = dot(dqkv, w_qkv, ((0,), (1,))).astype(BF).reshape(2, 4, T, D)
    qkv_grad = dot(h1_rows, dqkv, ((0,), (1,))).astype(BF).reshape(n_ctx, R, 3 * W)
    qkv_bias_part = jnp.sum(dqkv.astype(F32), axis=1)

    def unit_row(part):
        row = lax.dynamic_update_slice_in_dim(jnp.zeros((UNITS * W,), F32), part, unit * W, 0)
        return row[:D]

    dy_sum = jnp.sum(dy.astype(F32), axis=0)
    gains_part = jnp.stack([jnp.zeros((D,), F32), gain_two_g])
    biases_part = jnp.stack(
        [
            jnp.zeros((D,), F32),
            unit_row(qkv_bias_part[:W]),
            unit_row(qkv_bias_part[2 * W :]),
            proj_bias_g,
            bias_two_g,
            dy_sum,
        ]
    )
    parts = lay.from_natural(jnp.zeros((n_ctx, 2, FH), F32))
    mask = (jnp.arange(4)[None, :, None, None] == t) & (jnp.arange(2)[None, None, :, None] == s)
    parts = jnp.where(mask, fc_bias_part.reshape(n_dp, 1, 1, FH), parts)
    fc_bias_full = lay.to_natural(parts)
    small_parts = jnp.concatenate(
        [
            jnp.transpose(gains_part.reshape(2, n_ctx, R), (1, 0, 2)),
            jnp.transpose(biases_part.reshape(2, 3, n_ctx, R), (2, 0, 1, 3)).reshape(n_ctx, 2, 3 * R),
            fc_bias_full,
        ],
        axis=2,
    )
    small_parts = pad_to(small_parts, 2, 1024).reshape(n_dev, 8, 128)
    dh1, qkv_sum, fc_sum, out_sum, proj_sum, small_sum = reduce_grads(
        lay, dh1_part, qkv_grad, fc_grad, out_grad, proj_grad, small_parts
    )
    back_one, gain_one_g, bias_one_g = norm_back(dh1.astype(F32), hat_one, spread_one, gain_rows[0])
    input_grad = (dx1 + back_one).reshape(tokens.shape)
    first_rows = jnp.stack([gain_one_g, bias_one_g])
    first_rows = lax.psum(first_rows, ("ctx", "fsdp"))
    small_sum = jnp.sum(small_sum.reshape(n_dev, 1024), axis=0)
    own_cols = lax.dynamic_slice_in_dim(first_rows, c * R, R, 1)
    first_side = (s == 0).astype(F32)
    gains_out = (small_sum[:R] + own_cols[0] * first_side).reshape(1, R)
    biases_out = small_sum[R : 4 * R].reshape(3, R)
    biases_out = biases_out.at[0].add(own_cols[1] * first_side)
    fc_bias_out = small_sum[4 * R : 4 * R + FH]

    qkv_out = jnp.transpose(qkv_sum.reshape(2, 4, R, 3, W), (2, 3, 1, 0, 4))
    qkv_out = qkv_out.reshape(R, 3, UNITS * W)[:, :, :D].reshape(R, 2, 3 * D // 2)
    qkv_out = side(qkv_out, 1).astype(F32)
    fc_out = fc_sum.reshape(2, 4, R, n_dp, FH)
    fc_cols = []
    for b in range(n_ctx):
        for half in range(2):
            fc_cols.append(fc_sum[half, lay.tp_index(b), :, lay.dp_index(b) * FH : (lay.dp_index(b) + 1) * FH])
    half = n_ctx
    fc_out = jnp.where(
        s == 0, jnp.concatenate(fc_cols[:half], axis=1), jnp.concatenate(fc_cols[half:], axis=1)
    ).astype(F32)
    out_out = side(out_sum.reshape(FB, 2, D // 2), 1).astype(F32)
    proj_out = proj_sum.astype(F32)
    return (
        mixed.reshape(tokens.shape),
        input_grad,
        qkv_out,
        proj_out,
        fc_out,
        out_out,
        gains_out,
        biases_out,
        fc_bias_out,
    )


def solution(mesh):
    lay = Layout(mesh.shape["ctx"])
    in_specs = (
        P("fsdp", "ctx", None),
        P("ctx", "fsdp"),
        P("ctx", "fsdp"),
        P("ctx", "fsdp"),
        P("ctx", "fsdp"),
        P("fsdp", "ctx"),
        P("fsdp", "ctx"),
        P(("ctx", "fsdp")),
        P("fsdp", "ctx", None),
    )
    out_specs = (
        P("fsdp", "ctx", None),
        P("fsdp", "ctx", None),
        P("ctx", "fsdp"),
        P("ctx", "fsdp"),
        P("ctx", "fsdp"),
        P("ctx", "fsdp"),
        P("fsdp", "ctx"),
        P("fsdp", "ctx"),
        P(("ctx", "fsdp")),
    )
    return jax.shard_map(
        functools.partial(shards, lay), mesh=mesh, in_specs=in_specs, out_specs=out_specs, check_vma=False
    )
```

time: 3880 us -> 852 us (0.22)
  waiting for transfers between devices: 2770 us -> 0 us
  Pallas kernels: 0 us -> 554 us
  local copies, waits for them, and re-layouts: 416 us -> 164 us
  starting transfers between devices: 212 us -> 0 us
  blocking collectives: 164 us -> 37.2 us
  matrix products: 171 us -> 59.1 us
  other arithmetic: 113 us -> 25.1 us
    unnamed x10 -> x0, waiting for transfers between devices: 1710 us -> none
    all_gather x8 -> x0, waiting for transfers between devices: 725 us -> none  [the longest x1 216 us: shards(): lax.all_gather(columns[2], 'ctx', axis=0, tiled=True)]
    pallas_call x0 -> x11, Pallas kernels: none -> 554 us  [the longest x9 519 us: call(): pl.pallas_call(body, out_shape=outs, in_specs=in_specs, out_specs=out_spe...]
    ppermute x64 -> x0, waiting for transfers between devices: 335 us -> none  [the longest x32 302 us: passed_along(): return lax.ppermute(block, axis, route)]
    ppermute x64 -> x0, starting transfers between devices: 212 us -> none  [the longest x32 147 us: shifted(): return lax.ppermute(block, axis, route)]
    unnamed x128 -> x57, local copies, waits for them, and re-layouts: 173 us -> 10.3 us
    dot_general x19 -> x12, matrix products: 171 us -> 59.1 us  [dot(): lax.dot_general(left, right, (dims, ((), ())), preferred_element_type=F32)]
    reshape x14 -> x28, local copies, waits for them, and re-layouts: 184 us -> 84.9 us  [the longest x2 19 us: shards(): dot(ob, da, NN).astype(BF).reshape(n_ctx, R, 2, D // 2)]
  transfers between devices with their start and end apart: 73 -> 0, of which waited for: 47 -> 0; matrix products, arithmetic and copies ran while one was open for 5% -> 0% of each run, Pallas kernels for 0% -> 0%
where the time goes in v1:
time: 852 us; the launch traced here: 841 us
  Pallas kernels  554 us (65%)
  local copies, waits for them, and re-layouts  164 us (19%)
  matrix products  59.1 us (7%)
  blocking collectives  37.2 us (4%)
  other arithmetic  25.1 us (3%)
    pallas_call x9, Pallas kernels, call(): pl.pallas_call(body, out_shape=outs, in_specs=in_specs, out_specs=out_spe...  519 us
    dot_general x12, matrix products, dot(): lax.dot_general(left, right, (dims, ((), ())), preferred_element_type=F32)  59.1 us
    psum x1, blocking collectives, shards(): first_rows = lax.psum(first_rows, ('ctx', 'fsdp'))  37.2 us
    transpose x1, local copies, waits for them, and re-layouts, shards(): w_proj = jnp.transpose(proj_buf, (1, 2, 0, 3)).reshape(D, D)  23 us
    pallas_call x1, Pallas kernels, attend_back(): pl.pallas_call(body, grid=(2, n), in_specs=[whole, tiled, tiled, whole, l...  20.9 us
    reshape x2, local copies, waits for them, and re-layouts, shards(): dot(ob, da, NN).astype(BF).reshape(n_ctx, R, 2, D // 2)  19 us

profile of v1, /device:TPU:0, one launch (start us, length us, event | category | flops | bytes accessed | tf_op | source)
XLA Modules:
  0.0 841.2 jit_solution(16826196554611740136)
XLA Ops:
  4.7 2.0 copy.82
  6.7 4.1 concatenate.63
  12.0 11.6 %exchange_start.1 = (bf16[32,16,128]{2,1,0:T(8,128)(2,1)}, bf16[100,2400]{1,0:T(8,128)(2,1)}, bf16[100,3200]{1,0:T(8,128)(2,1)}, bf16[400,800]{1,0:T(8,128)(2,1)}) custom-call(bf16[16,128]{1,0:T(8,128)(2,1)} %fusion.47.small_r, bf16[100,2400]{1,0:T(8,128)(2,1)} %qkv_r.1, bf16[100,3200]{1,0:T(8,128)(2,1)} %fc_r.1, bf16[400,800]{1,0:T(8,128)(2,1)} %out_r.1), custom_call_target="tpu_custom_call" | custom-call | tf_op jit(solution)/shard_map/exchange_start/pallas_call | solution.py:543
  27.3 1.7 maximum_select_fusion
  32.9 2.3 fusion.39.out_r
  35.2 4.0 concatenate.64
  41.4 137.9 %gather_weights.1 = (bf16[16,100,768]{2,1,0:T(8,128)(2,1)}, bf16[16,100,800]{2,1,0:T(8,128)(2,1)}, bf16[4,200,1600]{2,1,0:T(8,128)(2,1)}, bf16[2,16,100,800]{3,2...) custom-call(bf16[4,100,768]{2,1,0:T(8,128)(2,1)} %reshape.359.qkv_r, ...), custom_call_target="tpu_custom_call" | custom-call | tf_op jit(solution)/shard_map/gather_weights/pallas_call | solution.py:543
  179.3 4.6 reshape.362
  183.9 5.8 add_convert_fusion
  191.0 37.1 %group_to_heads.1 = bf16[4,192,1024]{2,1,0:T(8,128)(2,1)} custom-call(bf16[4,192,1024]{2,1,0:T(8,128)(2,1)} %bitcast.298), custom_call_target="tpu_custom_call" | custom-call | tf_op jit(solution)/shard_map/group_to_heads/pallas_call | solution.py:543
  228.2 2.8 reshape.366
  235.4 14.5 %attend.1 = (f32[2,64,2048]{2,1,0:T(8,128)}, bf16[2,16,64,128]{3,2,1,0:T(8,128)(2,1)}, f32[2,1,2048]{2,1,0:T(1,128)}) custom-call(bf16[2,64,2048]{2,1,0:T(8,128)(2,1)} %squeeze.202.q_ref, bf16[2,64,2048]{2,1,0:T(8,128)(2,1)} %squeeze.203.k_ref, bf16[2,64,2048]{2,1,0:T(8,128)(2,1)} %squeeze.204.v_ref), custom_call_target="tpu_custom_call" | custom-call | tf_op jit(solution)/shard_map/attend/pallas_call | solution.py:802
  249.9 13.7 %heads_to_tokens.1 = bf16[25,64,128]{2,1,0:T(8,128)(2,1)} custom-call(bf16[2,16,64,128]{3,2,1,0:T(8,128)(2,1)} %get-tuple-element.51.src_r), custom_call_target="tpu_custom_call" | custom-call | tf_op jit(solution)/shard_map/heads_to_tokens/pallas_call | solution.py:543
  263.6 4.8 reshape.372
  268.4 23.0 %copy.85 = bf16[16,100,2,800]{3,2,1,0:T(2,128)(2,1)} copy(bf16[16,100,2,800]{3,1,0,2:T(8,128)(2,1)} %bitcast.301) | data formatting | bytes 10240000 | tf_op jit(solution)/shard_map/transpose | solution.py:979
  291.4 12.4 %reshape.370 = bf16[1600,1600]{1,0:T(8,128)(2,1)} reshape(bf16[16,100,2,800]{3,2,1,0:T(2,128)(2,1)} %copy.85) | data formatting | bytes 10240000 | tf_op jit(solution)/shard_map/reshape | solution.py:979
  303.8 3.6 fusion.54
  308.7 24.8 %gather_rows.1 = bf16[2,4,128,1600]{3,2,1,0:T(8,128)(2,1)} custom-call(bf16[128,1600]{1,0:T(8,128)(2,1)} %add_convert_fusion.2.h2_r), custom_call_target="tpu_custom_call" | custom-call | tf_op jit(solution)/shard_map/gather_rows/pallas_call | solution.py:543
  333.5 5.3 fusion.55
  338.8 4.5 convert_reduce_fusion
  343.3 5.6 convolution_convert_fusion.5
  348.9 5.7 convolution_convert_fusion.3
  354.6 4.4 convolution_convert_fusion.4
  359.8 5.4 copy.89
  365.2 7.5 convolution_convert_fusion.2
  372.8 5.4 copy.90
  378.2 37.6 %reduce_rows.1 = (bf16[128,1600]{1,0:T(8,128)(2,1)}, bf16[128,1600]{1,0:T(8,128)(2,1)}) custom-call(bf16[2,4,128,1600]{3,2,1,0:T(8,128)(2,1)} %bitcast.293, bf16[2,4,128,1600]{3,2,1,0:T(8,128)(2,1)} %bitcast.294), custom_call_target="tpu_custom_call" | custom-call | tf_op jit(solution)/shard_map/reduce_rows/pallas_call | solution.py:543
  417.4 2.5 convert_reduce_fusion.6
  419.9 2.3 convolution_convert_fusion.7
  422.4 17.4 %tokens_to_heads.1 = bf16[2,16,64,128]{3,2,1,0:T(8,128)(2,1)} custom-call(bf16[25,64,128]{2,1,0:T(8,128)(2,1)} %bitcast.309), custom_call_target="tpu_custom_call" | custom-call | tf_op jit(solution)/shard_map/tokens_to_heads/pallas_call | solution.py:543
  439.7 2.0 copy_bitcast_fusion.2.dob_ref
  441.7 20.9 %attend_back.1 = (bf16[2,64,2048]{2,1,0:T(8,128)(2,1)}, bf16[2,64,2048]{2,1,0:T(8,128)(2,1)}, bf16[2,64,2048]{2,1,0:T(8,128)(2,1)}) custom-call(bf16[2,64,2048]{2,1,0:T(8,128)(2,1)} %squeeze.202.q_ref, bf16[2,64,2048]{2,1,0:T(8,128)(2,1)} %squeeze.203.k_ref, bf16[2,64,2048]{2,1,0:T(8,128)(2,1)} %squeeze.204.v_ref, f32[2,64,2048]{2,1,0:T(8,128)} %get-tuple-element.58.o_ref, ...), custom_call_target="tpu_custom_call" | custom-call | tf_op jit(solution)/shard_map/attend_back/pallas_call | solution.py:870
  467.2 2.6 copy.92
  469.8 3.8 reshape.384.src_r
  473.6 37.5 %heads_to_group.1 = bf16[4,192,1024]{2,1,0:T(8,128)(2,1)} custom-call(bf16[4,192,1024]{2,1,0:T(8,128)(2,1)} %reshape.384.src_r), custom_call_target="tpu_custom_call" | custom-call | tf_op jit(solution)/shard_map/heads_to_group/pallas_call | solution.py:543
  514.8 6.5 convolution_convert_fusion.6
  521.2 4.1 convolution_convert_fusion.1
  526.9 4.1 reshape.388.qkv_r
  531.0 5.4 copy.94
  536.4 9.0 %reshape.410 = bf16[16,100,800]{1,0,2:T(8,128)(2,1)} reshape(bf16[1600,800]{0,1:T(8,128)(2,1)} %convolution_convert_fusion.4) | data formatting | bytes 5120000 | tf_op jit(solution)/shard_map/reshape | solution.py:1017
  545.4 6.7 copy.108.fc_r
  552.2 3.9 convolution_convert_fusion
  556.0 13.1 %reshape.391 = bf16[16,100,2,800]{3,2,1,0:T(2,128)(2,1)} reshape(bf16[1600,1600]{1,0:T(8,128)(2,1)} %convolution_convert_fusion) | data formatting | bytes 10240000 | tf_op jit(solution)/shard_map/reshape | solution.py:1024
  569.2 5.9 copy.129
  575.1 201.4 %reduce_grads.1 = (bf16[128,1600]{1,0:T(8,128)(2,1)}, bf16[2,4,100,768]{3,2,1,0:T(8,128)(2,1)}, bf16[2,4,100,800]{3,2,1,0:T(8,128)(2,1)}, bf16[2,200,1600]{2,1,0...) custom-call(bf16[2,4,128,1600]{3,2,1,0:T(8,128)(2,1)} %bitcast.292, ...), custom_call_target="tpu_custom_call" | custom-call | tf_op jit(solution)/shard_map/reduce_grads/pallas_call | solution.py:543
  782.3 37.2 %psum.7 = f32[2,1600]{1,0:T(2,128)S(1)} all-reduce(f32[2,1600]{1,0:T(2,128)S(1)} %pad_maximum_fusion.3), channel_id=1, replica_groups=mesh['ctx'=16,'fsdp'=2] {'ctx','fsdp'}, use_global_device_ids=true, to_apply=%region_17.18 | all-reduce | flops 3200 | bytes 25600 | tf_op jit(solution)/shard_map/psum | solution.py:1085
  820.1 2.6 reshape.398
  833.6 2.2 concatenate.77
  (174 shorter events, 56.1 us)
Async XLA Ops:
  4.4 21.8 %copy-start.13 = (f32[128]{0:T(128)}, f32[128]{0:T(128)S(1)}, u32[]{:S(2)}) copy-start(f32[128]{0:T(128)S(1)} %broadcast_multiply_fusion.5) | copy-start | bytes 1540
  4.7 21.5 %copy-start.16 = (f32[128]{0:T(128)}, f32[128]{0:T(128)S(1)}, u32[]{:S(2)}) copy-start(f32[128]{0:T(128)S(1)} %add_rsqrt_fusion.1) | copy-start | bytes 1540
  6.7 20.6 %copy-start.7 = (bf16[100,2400]{1,0:T(8,128)(2,1)S(1)}, bf16[100,2400]{1,0:T(8,128)(2,1)}, u32[]{:S(2)}) copy-start(bf16[100,2400]{1,0:T(8,128)(2,1)} %qkv_r.1) | copy-start | bytes 1440004
  30.4 2.5 copy-start.5
  31.4 8.1 copy-start.2
  291.4 12.4 %copy-start = (bf16[25,64,128]{2,1,0:T(8,128)(2,1)S(1)}, bf16[25,64,128]{2,1,0:T(8,128)(2,1)}, u32[]{:S(2)}) copy-start(bf16[25,64,128]{2,1,0:T(8,128)(2,1)} %heads_to_tokens.1) | copy-start | bytes 1228804
  307.4 26.1 %copy-start.4 = (bf16[1600,800]{1,0:T(8,128)(2,1)S(1)}, bf16[1600,800]{1,0:T(8,128)(2,1)}, u32[]{:S(2)}) copy-start(bf16[1600,800]{1,0:T(8,128)(2,1)} %reshape.372) | copy-start | bytes 7680004
  307.4 108.5 %copy-start.12 = (f32[128]{0:T(128)}, f32[128]{0:T(128)S(1)}, u32[]{:S(2)}) copy-start(f32[128]{0:T(128)S(1)} %broadcast_multiply_fusion.4) | copy-start | bytes 1540
  307.7 108.2 %copy-start.15 = (f32[128]{0:T(128)}, f32[128]{0:T(128)S(1)}, u32[]{:S(2)}) copy-start(f32[128]{0:T(128)S(1)} %add_rsqrt_fusion) | copy-start | bytes 1540
  333.5 5.3 copy-start.19
  333.5 5.3 copy-start.20
  343.3 11.3 %copy-start.21 = (bf16[1024,800]{0,1:T(8,128)(2,1)}, bf16[1024,800]{0,1:T(8,128)(2,1)S(1)}, u32[]{:S(2)}) copy-start(bf16[1024,800]{0,1:T(8,128)(2,1)S(1)} %get-tuple-element.115) | copy-start | bytes 4915204
  348.9 5.7 copy-start.3
  378.2 41.7 %slice-start = ((s8[5324800]{0:T(1024)(128)(4,1)}), s8[4194304]{0:T(1024)(128)(4,1)S(1)}, s32[]{:S(2)}) async-start(s8[5324800]{0:T(1024)(128)(4,1)} %bitcast.287), calls=%async_computation | async-start | bytes 8388608
  378.2 39.1 %copy-start.1 = (bf16[1,128,1600]{2,1,0:T(8,128)(2,1)S(1)}, bf16[1,128,1600]{2,1,0:T(8,128)(2,1)}, u32[]{:S(2)}) copy-start(bf16[1,128,1600]{2,1,0:T(8,128)(2,1)} %copy.82) | copy-start | bytes 1228804
  378.2 41.7 %slice-start.1 = ((s8[5324800]{0:T(1024)(128)(4,1)}), s8[1130496]{0:T(1024)(128)(4,1)S(1)}, s32[]{:S(2)}) async-start(s8[5324800]{0:T(1024)(128)(4,1)} %bitcast.287), calls=%async_computation.1 | async-start | bytes 2260992
  439.7 25.2 %copy-start.9 = (bf16[1,128,1600]{2,1,0:T(8,128)(2,1)S(1)}, bf16[1,128,1600]{2,1,0:T(8,128)(2,1)}, u32[]{:S(2)}) copy-start(bf16[1,128,1600]{2,1,0:T(8,128)(2,1)} %get-tuple-element.151) | copy-start | bytes 1228804
  514.8 6.5 copy-start.6
  521.2 4.7 copy-start.11
  575.1 203.1 %copy-start.14 = (f32[128]{0:T(128)S(1)}, f32[128]{0:T(128)}, u32[]{:S(2)}) copy-start(f32[128]{0:T(128)} %copy-done.13) | copy-start | bytes 1540
  575.1 203.1 %copy-start.17 = (f32[128]{0:T(128)S(1)}, f32[128]{0:T(128)}, u32[]{:S(2)}) copy-start(f32[128]{0:T(128)} %copy-done.16) | copy-start | bytes 1540
  820.1 4.9 copy-start.18
  826.3 4.4 copy-start.8
  831.9 5.0 copy-start.10

commit v2 on v1

--- a/solution.py
+++ b/solution.py
@@ -16,7 +16,6 @@
 UNITS = 8
 HU = -(-HEADS // UNITS)
 QKV = 3 * HEAD_DIM
-TP_BITS = (1, 4)
 MESH = pl.DeviceIdType.MESH
 BF = jnp.bfloat16
 F32 = jnp.float32
@@ -27,13 +26,12 @@
 class Layout:
     def __init__(self, n_ctx):
         self.n_ctx = n_ctx
-        self.tp_bits = TP_BITS
-        bits = [1 << i for i in range(n_ctx.bit_length() - 1)]
-        self.dp_bits = tuple(b for b in bits if b not in TP_BITS)[::-1]
+        a, b = n_ctx // 4, n_ctx // 2
+        self.tp_bits = (a, b)
+        self.dp_bits = tuple(1 << i for i in range(n_ctx.bit_length() - 3))
         self.n_dp = n_ctx // 4
-        self.dp_order = [(b, b) for b in self.dp_bits]
-        a, b = TP_BITS
-        self.tp_order = [(a, b), (b, a)]
+        self.dp_order = list(zip(self.dp_bits, self.dp_bits[::-1]))
+        self.tp_order = [(b, b), (a, a)]
         self.tp_masks = [[], [(a, a)], [(b, b)], [(a, a), (b, b)]]
 
     def tp_index(self, c):
@@ -342,58 +340,6 @@
     return h, jnp.logical_and(env.d < HU, h < HEADS)
 
 
-def heads_to_tokens(env, src, out, sems):
-    send_sems, recv_sems, local_sems = sems
-    h, active = own_head(env)
-    lay = env.lay
-
-    def copy(i):
-        rank = (env.rank + i) % env.n_dev
-        return pltpu.make_async_remote_copy(
-            src_ref=src.at[rank % 2, rank // 2],
-            dst_ref=out.at[h],
-            send_sem=send_sems.at[i],
-            recv_sem=recv_sems.at[h],
-            device_id=(rank // 2, rank % 2),
-            device_id_type=MESH,
-        )
-
-    @pl.when(active)
-    def _():
-        def begin(i, carry):
-            copy(i).start()
-            return carry
-
-        lax.fori_loop(1, env.n_dev, begin, 0)
-        local = pltpu.make_async_copy(src.at[env.s, env.c], out.at[h], local_sems.at[0])
-        local.start()
-        local.wait()
-
-    def receive(j, carry):
-        @pl.when(lay.head_rank(j) != env.rank)
-        def _():
-            pltpu.make_async_remote_copy(
-                src_ref=src.at[0, 0],
-                dst_ref=out.at[j],
-                send_sem=send_sems.at[0],
-                recv_sem=recv_sems.at[j],
-                device_id=env.other(),
-                device_id_type=MESH,
-            ).wait_recv()
-
-        return carry
-
-    lax.fori_loop(0, HEADS, receive, 0)
-
-    @pl.when(active)
-    def _():
-        def end(i, carry):
-            copy(i).wait_send()
-            return carry
-
-        lax.fori_loop(1, env.n_dev, end, 0)
-
-
 def tokens_to_heads(env, src, out, sems):
     send_sems, recv_sems, local_sems = sems
     h, active = own_head(env)
@@ -456,43 +402,6 @@
 def data_partners(env):
     lay = env.lay
     return [(lay.compose(env.t, (env.d + i) % lay.n_dp), env.s) for i in range(1, lay.n_dp)]
-
-
-def group_to_heads(env, src, out, sems):
-    send_sems, recv_sems, local_sems = sems
-    lay = env.lay
-
-    def copy(j, source, target):
-        return pltpu.make_async_remote_copy(
-            src_ref=src.at[j],
-            dst_ref=out.at[source],
-            send_sem=send_sems.at[j],
-            recv_sem=recv_sems.at[source],
-            device_id=(lay.compose(env.t, target), env.s),
-            device_id_type=MESH,
-        )
-
-    for i in range(1, HU + 1):
-        j = (env.d + i) % HU
-
-        @pl.when(j != env.d)
-        def _():
-            copy(j, env.d, j).start()
-
-    @pl.when(env.d < HU)
-    def _():
-        local = pltpu.make_async_copy(src.at[env.d], out.at[env.d], local_sems.at[0])
-        local.start()
-        local.wait()
-        for i in range(1, lay.n_dp):
-            source = (env.d + i) % lay.n_dp
-            copy(0, source, source).wait_recv()
-
-    for j in range(HU):
-
-        @pl.when(j != env.d)
-        def _():
-            copy(j, env.d, j).wait_send()
 
 
 def heads_to_group(env, src, out, sems):
@@ -551,91 +460,6 @@
         ),
         name=name,
     )(*args)
-
-
-def exchange_start(lay, small, qkv, fc, out):
-    def body(small_r, qkv_r, fc_r, out_r, small_o, qkv_o, fc_o, out_o, *sems):
-        env = Env(lay)
-        meet_all(env)
-        links = Links((sems[0], sems[1], sems[2]))
-        copies = [
-            links.send(a, b, env.other()) for a, b in ((qkv_r, qkv_o), (fc_r, fc_o), (out_r, out_o))
-        ]
-        run([to_everyone(env, small_r, small_o, sems[3:6], True)])
-        for copy in copies:
-            copy.wait_recv()
-        links.finish()
-
-    n_dev = lay.n_ctx * 2
-    return call(
-        "exchange_start",
-        0,
-        body,
-        (small, qkv, fc, out),
-        [ANY] * 4,
-        [struct(n_dev, *small.shape), struct(*qkv.shape), struct(*fc.shape), struct(*out.shape)],
-        [ANY] * 4,
-        sem_shapes(3) + sem_shapes(n_dev),
-    )
-
-
-def gather_weights(lay, qkv, fc, out, proj, h1, dy):
-    n_ctx, n_dp = lay.n_ctx, lay.n_dp
-    k = len(lay.dp_bits)
-
-    def natural(c):
-        return c
-
-    def body(qkv_r, fc_r, out_r, proj_r, h1_r, dy_r, qkv_o, fc_o, out_o, proj_o, h1_o, dy_o, *sems):
-        env = Env(lay)
-        meet(env, tp_partners(env) + dp_partners(env) + [env.other()])
-        groups = [sems[3 * i : 3 * i + 3] for i in range(6)]
-        run(
-            [
-                gather(env, qkv_r, qkv_o, groups[0], lay.dp_order, natural, rows=True),
-                gather(env, h1_r, h1_o, groups[4], lay.tp_order, lay.tp_index, core=True),
-                gather(env, proj_r, proj_o, groups[3], lay.dp_order + lay.tp_order, natural, core=True),
-                gather(env, fc_r, fc_o, groups[1], lay.dp_order, natural, rows=True),
-                gather(env, out_r, out_o, groups[2], lay.dp_order, lay.dp_index),
-                gather(env, dy_r, dy_o, groups[5], lay.tp_order, lay.tp_index, core=True),
-            ]
-        )
-
-    outs = [
-        struct(n_ctx, *qkv.shape[1:]),
-        struct(n_ctx, *fc.shape[1:]),
-        struct(n_dp, *out.shape),
-        struct(2, n_ctx, *proj.shape),
-        struct(2, 4, *h1.shape),
-        struct(2, 4, *dy.shape),
-    ]
-    scratch = (
-        sem_shapes(gather_sends(4, k, False, True)) * 2
-        + sem_shapes(gather_sends(1, k, False, False))
-        + sem_shapes(gather_sends(1, k + 2, True, False))
-        + sem_shapes(gather_sends(1, 2, True, False)) * 2
-    )
-    return call(
-        "gather_weights", 1, body, (qkv, fc, out, proj, h1, dy), [ANY] * 6, outs, [ANY] * 6, scratch
-    )
-
-
-def gather_rows(lay, h2):
-    def body(h2_r, h2_o, *sems):
-        env = Env(lay)
-        meet(env, tp_partners(env) + [env.other()])
-        run([gather(env, h2_r, h2_o, sems, lay.tp_order, lay.tp_index, core=True)])
-
-    return call(
-        "gather_rows",
-        2,
-        body,
-        (h2,),
-        [ANY],
-        struct(2, 4, *h2.shape),
-        ANY,
-        sem_shapes(gather_sends(1, 2, True, False)),
-    )
 
 
 def reduce_rows(lay, first, second):
@@ -716,7 +540,7 @@
                 to_everyone(env, small_r, small_o, rest[-3:], False),
                 reduce(env, qkv_r, qkv_o, *space(1), lay.dp_order, natural, rows=True),
                 reduce(env, rows_r, rows_o, *space(0), lay.tp_order, lay.tp_index, core=True),
-                reduce(env, proj_r, proj_o, *space(4), lay.dp_order + lay.tp_order, natural, core=True),
+                reduce(env, proj_r, proj_o, *space(4), lay.tp_order + lay.dp_order, natural, core=True),
                 reduce(env, fc_r, fc_o, *space(2), lay.dp_order, natural, rows=True),
                 reduce(env, out_r, out_o, *space(3), lay.dp_order, lay.dp_index, halves=True),
             ]
@@ -751,72 +575,6 @@
 TN = ((0,), (0,))
 SCALE = 1.0 / math.sqrt(HEAD_DIM)
 TILE = 512
-
-
-def attend(lay, q, k, v, rows):
-    length = q.shape[2]
-    tile = min(TILE, length)
-    n = length // tile
-    per = tile // rows
-
-    def body(q_ref, k_ref, v_ref, o_ref, low_ref, lse_ref, keys):
-        i = pl.program_id(1)
-
-        @pl.when(i == 0)
-        def _():
-            keys[...] = k_ref[0].T
-
-        qt = q_ref[0]
-
-        def step(j, carry, masked):
-            peak, total, acc = carry
-            first = pl.multiple_of(j * tile, tile)
-            st = dot(keys[pl.ds(first, tile), :], qt, NN) * (SCALE * LOG2E)
-            if masked:
-                row = lax.broadcasted_iota(jnp.int32, (tile, tile), 0)
-                col = lax.broadcasted_iota(jnp.int32, (tile, tile), 1)
-                st = jnp.where(row <= col, st, -1e30)
-            new = jnp.maximum(peak, jnp.max(st, axis=0, keepdims=True))
-            p = jnp.exp2(st - new)
-            shrink = jnp.exp2(peak - new)
-            total = total * shrink + jnp.sum(p, axis=0, keepdims=True)
-            acc = acc * shrink + dot(v_ref[0, :, pl.ds(first, tile)], p.astype(BF), NN)
-            return new, total, acc
-
-        start = (
-            jnp.full((1, tile), -1e30, F32),
-            jnp.zeros((1, tile), F32),
-            jnp.zeros((HEAD_DIM, tile), F32),
-        )
-        carry = lax.fori_loop(0, i, functools.partial(step, masked=False), start)
-        peak, total, acc = step(i, carry, True)
-        o = acc / total
-        o_ref[0] = o
-        low = o.astype(BF)
-        for b in range(per):
-            low_ref[0, b] = low[:, b * rows : (b + 1) * rows]
-        lse_ref[0] = peak + jnp.log2(total)
-
-    whole = pl.BlockSpec((1, HEAD_DIM, length), lambda b, i: (b, 0, 0))
-    tiled = pl.BlockSpec((1, HEAD_DIM, tile), lambda b, i: (b, 0, i))
-    return pl.pallas_call(
-        body,
-        grid=(2, n),
-        in_specs=[tiled, whole, whole],
-        out_specs=[
-            tiled,
-            pl.BlockSpec((1, per, HEAD_DIM, rows), lambda b, i: (b, i, 0, 0)),
-            pl.BlockSpec((1, 1, tile), lambda b, i: (b, 0, i)),
-        ],
-        out_shape=[
-            struct(2, HEAD_DIM, length, dtype=F32),
-            struct(2, length // rows, HEAD_DIM, rows),
-            struct(2, 1, length, dtype=F32),
-        ],
-        scratch_shapes=[pltpu.VMEM((length, HEAD_DIM), BF)],
-        compiler_params=pltpu.CompilerParams(vmem_limit_bytes=VMEM_LIMIT),
-        name="attend",
-    )(q, k, v)
 
 
 def attend_back(lay, q, k, v, o, lse, dob):
@@ -884,6 +642,399 @@
     )(q, k, v, o, lse, dob)
 
 
+class Background:
+    def __init__(self):
+        self.active = []
+
+    def add(self, generator):
+        self.active.append(generator)
+
+    def step(self, count=1):
+        for _ in range(count):
+            if not self.active:
+                return
+            g = self.active.pop(0)
+            try:
+                next(g)
+                self.active.append(g)
+            except StopIteration:
+                pass
+
+    def finish(self):
+        while self.active:
+            self.step()
+
+
+def finish(generator):
+    for _ in generator:
+        pass
+
+
+def group_to_heads(env, src, out, sems, q):
+    send_sems, recv_sems, local_sems = sems
+    lay = env.lay
+
+    def copy(j, source, target):
+        return pltpu.make_async_remote_copy(
+            src_ref=src.at[q, j],
+            dst_ref=out.at[q, source],
+            send_sem=send_sems.at[q, j],
+            recv_sem=recv_sems.at[q, source],
+            device_id=(lay.compose(env.t, target), env.s),
+            device_id_type=MESH,
+        )
+
+    for i in range(1, HU + 1):
+        j = (env.d + i) % HU
+
+        @pl.when(j != env.d)
+        def _():
+            copy(j, env.d, j).start()
+
+    local = pltpu.make_async_copy(src.at[q, env.d % HU], out.at[q, env.d], local_sems.at[q])
+
+    @pl.when(env.d < HU)
+    def _():
+        local.start()
+
+    yield
+
+    @pl.when(env.d < HU)
+    def _():
+        local.wait()
+        for i in range(1, lay.n_dp):
+            source = (env.d + i) % lay.n_dp
+            copy(0, source, source).wait_recv()
+
+    yield
+    for j in range(HU):
+
+        @pl.when(j != env.d)
+        def _():
+            copy(j, env.d, j).wait_send()
+
+
+def heads_out(env, src, out, sems, q):
+    send_sems, recv_sems, local_sems = sems
+    h, active = own_head(env)
+    n_ctx = env.lay.n_ctx
+
+    def copy(i):
+        there = (env.c + i) % n_ctx
+        return pltpu.make_async_remote_copy(
+            src_ref=src.at[q, there],
+            dst_ref=out.at[h],
+            send_sem=send_sems.at[q, i],
+            recv_sem=recv_sems.at[h],
+            device_id=(there, q),
+            device_id_type=MESH,
+        )
+
+    local = pltpu.make_async_copy(src.at[q, env.c], out.at[h], local_sems.at[q])
+    mine = jnp.logical_and(active, env.s == q)
+    theirs = jnp.logical_and(active, env.s != q)
+
+    def begin(i, carry):
+        copy(i).start()
+        return carry
+
+    def end(i, carry):
+        copy(i).wait_send()
+        return carry
+
+    @pl.when(mine)
+    def _():
+        local.start()
+
+    @pl.when(theirs)
+    def _():
+        copy(0).start()
+
+    @pl.when(active)
+    def _():
+        lax.fori_loop(1, n_ctx, begin, 0)
+
+    yield
+
+    @pl.when(mine)
+    def _():
+        local.wait()
+
+    @pl.when(theirs)
+    def _():
+        copy(0).wait_send()
+
+    @pl.when(active)
+    def _():
+        lax.fori_loop(1, n_ctx, end, 0)
+
+
+def heads_in(env, src, out, sems):
+    def receive(j, carry):
+        @pl.when(env.lay.head_rank(j) != env.rank)
+        def _():
+            pltpu.make_async_remote_copy(
+                src_ref=src.at[0, 0],
+                dst_ref=out.at[j],
+                send_sem=sems[0].at[0, 0],
+                recv_sem=sems[1].at[j],
+                device_id=env.other(),
+                device_id_type=MESH,
+            ).wait_recv()
+
+        return carry
+
+    lax.fori_loop(0, HEADS, receive, 0)
+
+
+def norm_stats(values):
+    centre = values - jnp.mean(values, axis=-1, keepdims=True)
+    spread = lax.rsqrt(jnp.mean(centre * centre, axis=-1, keepdims=True) + EPS)
+    return centre * spread, spread
+
+
+def attend_tile(i, tile, qt, keys, v_ref):
+    def step(j, carry, masked):
+        peak, total, acc = carry
+        at = pl.ds(pl.multiple_of(j * tile, tile), tile)
+        st = dot(keys[at, :], qt, NN) * (SCALE * LOG2E)
+        if masked:
+            row = lax.broadcasted_iota(jnp.int32, (tile, tile), 0)
+            col = lax.broadcasted_iota(jnp.int32, (tile, tile), 1)
+            st = jnp.where(row <= col, st, -1e30)
+        new = jnp.maximum(peak, jnp.max(st, axis=0, keepdims=True))
+        p = jnp.exp2(st - new)
+        shrink = jnp.exp2(peak - new)
+        total = total * shrink + jnp.sum(p, axis=0, keepdims=True)
+        acc = acc * shrink + dot(v_ref[:, at], p.astype(BF), NN)
+        return new, total, acc
+
+    start = (
+        jnp.full((1, tile), -1e30, F32),
+        jnp.zeros((1, tile), F32),
+        jnp.zeros((HEAD_DIM, tile), F32),
+    )
+    carry = start
+    if i > 0:
+        carry = lax.fori_loop(0, i, functools.partial(step, masked=False), carry)
+    peak, total, acc = step(i, carry, True)
+    return acc / total, peak + jnp.log2(total)
+
+
+def forward(lay, x, gains, biases, fc_bias, qkv, fc, out, proj, dy):
+    n_ctx, n_dp = lay.n_ctx, lay.n_dp
+    n_dev = 2 * n_ctx
+    k = len(lay.dp_bits)
+    T = x.shape[0]
+    R, FB = D // n_ctx, FF // n_ctx
+    FH = FB // 2
+    W = HU * HEAD_DIM
+    G = 4 * T
+    length = n_ctx * T
+    tile = min(TILE, length)
+    n_tiles = length // tile
+    half = D // 2
+    wide = UNITS * W
+
+    def natural(c):
+        return c
+
+    def body(*refs):
+        (x_r, gains_r, biases_r, fcb_r, qkv_r, fc_r, out_r, proj_r, dy_r) = refs[:9]
+        (h1_o, wq_o, heads_o, o_o, lse_o, ob_o, pj_o, x1_o, h2_o, fc_o, out_o, dy_o, shift_o, par_o) = refs[9:23]
+        (
+            pack, small, qkv_x, fc_x, out_x, qkv_s, fc_s, out_s, wq_b, h1_s, par_w,
+            parts, mine, keys, o_low, ob_b, proj_b, h2_s,
+        ) = refs[23:41]
+        sems = refs[41:]
+        groups = [sems[3 * i : 3 * i + 3] for i in range(len(sems) // 3)]
+        env = Env(lay)
+        s = env.s
+
+        pack[...] = jnp.zeros_like(pack)
+        pack[0:1, :R] = gains_r[...].astype(F32)
+        pack[1:4, :R] = biases_r[...].astype(F32)
+        pack[4:6, : FH // 2] = fcb_r[...].astype(F32)
+        meet_all(env)
+        links = Links(groups[0])
+        crossing = [
+            links.send(a, b, env.other()) for a, b in ((qkv_r, qkv_x), (fc_r, fc_x), (out_r, out_x))
+        ]
+        everyone = to_everyone(env, pack, small, groups[1], True)
+        next(everyone)
+        hat, _ = norm_stats(x_r[...].astype(F32))
+
+        def fill_qkv(a, b, side):
+            q = a[:, :D]
+            keys_all = jnp.concatenate([a[:, D:], b[:, : D // 2]], axis=1)
+            v = b[:, D // 2 :]
+            for u in range(4):
+                first = (2 * u + side) * W
+                width = max(0, min(W, D - first))
+                for n, part in enumerate((q, keys_all, v)):
+                    if width < W:
+                        qkv_s[u, :, n * W : (n + 1) * W] = jnp.zeros((R, W), BF)
+                    if width > 0:
+                        qkv_s[u, :, n * W : n * W + width] = part[:, first : first + width]
+
+        def fill_rest(a, b, oa, ob, side):
+            for u in range(4):
+                for d in range(n_dp):
+                    first = lay.compose(u, d) * FB + side * FH
+                    source, first = (a, first) if first < FF // 2 else (b, first - FF // 2)
+                    fc_s[u, :, d * FH : (d + 1) * FH] = source[:, first : first + FH]
+            out_s[:, :half] = oa[side * FH : (side + 1) * FH, :]
+            out_s[:, half:] = ob[side * FH : (side + 1) * FH, :]
+
+        def by_side(f, own, other):
+            @pl.when(s == 0)
+            def _():
+                f(*own_other(own, other), 0)
+
+            @pl.when(s == 1)
+            def _():
+                f(*own_other(other, own), 1)
+
+        def own_other(first, second):
+            return [r for pair in zip(first, second) for r in pair]
+
+        crossing[0].wait_recv()
+        by_side(fill_qkv, (qkv_r,), (qkv_x,))
+        weights = gather(env, qkv_s, wq_b, groups[2], lay.dp_order, natural, rows=True)
+        next(weights)
+        finish(everyone)
+        for f in range(2):
+            rows = jnp.concatenate([small[2 * c + f][:, :R] for c in range(n_ctx)], axis=1)
+            par_o[f] = rows
+        par_w[...] = jnp.zeros_like(par_w)
+        par_w[:, :D] = par_o[0]
+        h1_s[...] = (hat * par_o[0, 0:1, :] + par_o[0, 1:2, :]).astype(BF)
+        rows_h1 = gather(env, h1_s, h1_o, groups[3], lay.tp_order, lay.tp_index, core=True)
+        next(rows_h1)
+        shift_parts = []
+        for d in range(n_dp):
+            block = small[lay.compose(env.t, d) * 2 + s]
+            shift_parts += [block[4:5, : FH // 2], block[5:6, : FH // 2]]
+        shift_o[...] = jnp.concatenate(shift_parts, axis=1)
+        run([weights, rows_h1])
+        crossing[1].wait_recv()
+        crossing[2].wait_recv()
+        by_side(fill_rest, (fc_r, out_r), (fc_x, out_x))
+        bg = Background()
+        bg.add(gather(env, dy_r, dy_o, groups[4], lay.tp_order, lay.tp_index, core=True))
+        bg.add(gather(env, fc_s, fc_o, groups[5], lay.dp_order, natural, rows=True))
+        bg.step(2)
+        for c in range(n_ctx):
+            wq_o[c * R : (c + 1) * R, :] = wq_b[c]
+        unit = 2 * env.t + s
+        cols = pl.ds(pl.multiple_of(unit * W, W), W)
+        shift = jnp.concatenate(
+            [par_w[2:3, cols], jnp.zeros((1, W), F32), par_w[3:4, cols]], axis=1
+        )
+        moving = []
+        for q in range(2):
+            rows = h1_o[q].reshape(G, D)
+            made = (dot(rows, wq_o[...], NN) + shift).astype(BF).T
+            for n in range(3):
+                for j in range(HU):
+                    first = n * W + j * HEAD_DIM
+                    parts[q, j, n * HEAD_DIM : (n + 1) * HEAD_DIM, :] = made[first : first + HEAD_DIM]
+            g = group_to_heads(env, parts, mine, groups[6], q)
+            next(g)
+            moving.append(g)
+        bg.add(gather(env, proj_r, proj_b, groups[7], lay.tp_order + lay.dp_order, natural, core=True))
+        bg.add(gather(env, out_s, out_o, groups[8], lay.dp_order, lay.dp_index))
+        bg.step(4)
+        leaving = []
+        for q in range(2):
+            next(moving[q])
+            for c in range(n_ctx):
+                tc, dc = lay.tp_index(c), lay.dp_index(c)
+                for n in range(3):
+                    heads_o[n, q, :, c * T : (c + 1) * T] = mine[
+                        q, dc, n * HEAD_DIM : (n + 1) * HEAD_DIM, tc * T : (tc + 1) * T
+                    ]
+            keys[...] = heads_o[1, q].T
+            for i in range(n_tiles):
+                at = slice(i * tile, (i + 1) * tile)
+                o, lse = attend_tile(i, tile, heads_o[0, q, :, at], keys, heads_o.at[2, q])
+                o_o[q, :, at] = o
+                lse_o[q, :, at] = lse
+                low = o.astype(BF)
+                for b in range(tile // T):
+                    o_low[q, i * (tile // T) + b] = low[:, b * T : (b + 1) * T]
+                bg.step(3)
+            g = heads_out(env, o_low, ob_b, groups[9], q)
+            next(g)
+            leaving.append(g)
+        bg.finish()
+        for g in moving + leaving:
+            finish(g)
+        for n in range(2):
+            for c in range(n_ctx):
+                pj_o[n, c * R : (c + 1) * R, :] = proj_b[n, c]
+        heads_in(env, o_low, ob_b, groups[9])
+        ob_o[...] = ob_b[...].reshape(D, T).T
+        branch = jnp.concatenate([dot(ob_o[...], pj_o[n], NN) for n in range(2)], axis=1)
+        x1 = x_r[...].astype(F32) + branch + par_o[1, 1:2, :]
+        x1_o[...] = x1
+        hat, _ = norm_stats(x1)
+        h2_s[...] = (hat * par_o[1, 0:1, :] + par_o[1, 2:3, :]).astype(BF)
+        finish(gather(env, h2_s, h2_o, groups[10], lay.tp_order, lay.tp_index, core=True))
+        links.finish()
+
+    outs = [
+        struct(2, 4, T, D),
+        struct(D, 3 * W),
+        struct(3, 2, HEAD_DIM, length),
+        struct(2, HEAD_DIM, length, dtype=F32),
+        struct(2, 1, length, dtype=F32),
+        struct(T, D),
+        struct(2, D, half),
+        struct(T, D, dtype=F32),
+        struct(2, 4, T, D),
+        struct(n_ctx, R, n_dp * FH),
+        struct(n_dp, FH, D),
+        struct(2, 4, T, D),
+        struct(1, n_dp * FH, dtype=F32),
+        struct(2, 8, D, dtype=F32),
+    ]
+    out_specs = [VM] * 8 + [ANY] * 4 + [VM] * 2
+    scratch = [
+        pltpu.VMEM((8, 128), F32),
+        pltpu.VMEM((n_dev, 8, 128), F32),
+        pltpu.VMEM(qkv.shape, BF),
+        pltpu.VMEM(fc.shape, BF),
+        pltpu.VMEM(out.shape, BF),
+        pltpu.VMEM((4, R, 3 * W), BF),
+        pltpu.VMEM((4, R, n_dp * FH), BF),
+        pltpu.VMEM((FH, D), BF),
+        pltpu.VMEM((n_ctx, R, 3 * W), BF),
+        pltpu.VMEM((T, D), BF),
+        pltpu.VMEM((8, wide), F32),
+        pltpu.VMEM((2, HU, QKV, G), BF),
+        pltpu.VMEM((2, n_dp, QKV, G), BF),
+        pltpu.VMEM((length, HEAD_DIM), BF),
+        pltpu.VMEM((2, n_ctx, HEAD_DIM, T), BF),
+        pltpu.VMEM((HEADS, HEAD_DIM, T), BF),
+        pltpu.VMEM((2, n_ctx, R, half), BF),
+        pltpu.VMEM((T, D), BF),
+    ]
+    DMA = pltpu.SemaphoreType.DMA
+    scratch += sem_shapes(3) + sem_shapes(n_dev)
+    scratch += sem_shapes(gather_sends(4, k, False, True))
+    scratch += sem_shapes(gather_sends(1, 2, True, False)) * 2
+    scratch += sem_shapes(gather_sends(4, k, False, True))
+    scratch += [DMA((2, HU)), DMA((2, n_dp)), DMA((2,))]
+    scratch += sem_shapes(gather_sends(1, k + 2, True, False))
+    scratch += sem_shapes(gather_sends(1, k, False, False))
+    scratch += [DMA((2, n_ctx)), DMA((HEADS,)), DMA((2,))]
+    scratch += sem_shapes(gather_sends(1, 2, True, False))
+    return call(
+        "forward", 0, body, (x, gains, biases, fc_bias, qkv, fc, out, proj, dy), [VM] * 9, outs, out_specs, scratch
+    )
+
+
 def norm_forward(values, gain, bias):
     centre = values - jnp.mean(values, axis=-1, keepdims=True)
     spread = lax.rsqrt(jnp.mean(centre * centre, axis=-1, keepdims=True) + EPS)
@@ -927,86 +1078,25 @@
     W = HU * HEAD_DIM
     length = n_ctx * T
 
-    def both(own, other, axis):
-        return jnp.where(
-            s == 0, jnp.concatenate([own, other], axis), jnp.concatenate([other, own], axis)
-        )
-
     def side(x, axis):
         return lax.dynamic_index_in_dim(x, s, axis, keepdims=False)
 
-    x = tokens.reshape(T, D).astype(F32)
+    x = tokens.reshape(T, D)
     dy = cotangent.reshape(T, D)
-
-    small = jnp.concatenate([gains.reshape(-1), biases.reshape(-1), fc_bias])
-    small = pad_to(small, 0, 2048).reshape(16, 128)
-    small_all, qkv_other, fc_other, out_other = exchange_start(
-        lay, small, qkv_weight, fc_weight, out_weight
-    )
-    small_all = small_all.reshape(n_ctx, 2, 2048)
-    gain_rows = jnp.transpose(small_all[:, :, :R], (1, 0, 2)).reshape(2, D).astype(F32)
-    bias_rows = (
-        jnp.transpose(small_all[:, :, R : 4 * R].reshape(n_ctx, 2, 3, R), (1, 2, 0, 3))
-        .reshape(6, D)
-        .astype(F32)
-    )
-    fcb = side(small_all[:, :, 4 * R : 4 * R + FH], 1)
-    fc_shift = lax.dynamic_index_in_dim(
-        lay.from_natural(fcb), t, 1, keepdims=False
-    ).reshape(n_dp * FH).astype(F32)
-
-    normed_one, hat_one, spread_one = norm_forward(x, gain_rows[0], bias_rows[0])
-    h1 = normed_one.astype(BF)
-
-    qkv_full = both(qkv_weight, qkv_other, 1).reshape(R, 3, D)
-    qkv_full = pad_to(qkv_full, 2, UNITS * W).reshape(R, 3, 4, 2, W)
-    qkv_src = jnp.transpose(side(qkv_full, 3), (2, 0, 1, 3)).reshape(4, R, 3 * W)
-    fc_full = side(both(fc_weight, fc_other, 1).reshape(R, n_ctx, 2, FH), 2)
-    fc_src = jnp.stack(
-        [
-            jnp.concatenate([fc_full[:, lay.compose(u, d)] for d in range(n_dp)], axis=1)
-            for u in range(4)
-        ]
-    )
-    out_src = side(both(out_weight, out_other, 1).reshape(2, FH, D), 0)
-
-    qkv_buf, fc_buf, out_buf, proj_buf, h1_all, dy_all = gather_weights(
-        lay, qkv_src, fc_src, out_src, proj_weight, h1, dy
-    )
-    w_qkv = qkv_buf.reshape(D, 3 * W)
+    n_dev = 2 * n_ctx
+    (h1_all, w_qkv, heads, o, lse, ob, w_proj, x1, h2_all, fc_buf, out_buf, dy_all, fc_shift, par) = forward(
+        lay, x, gains, biases, fc_bias.reshape(2, FH // 2), qkv_weight, fc_weight, out_weight, proj_weight, dy
+    )
+    q, k, v = heads[0], heads[1], heads[2]
     w_fc = fc_buf.reshape(D, n_dp * FH)
     w_out = out_buf.reshape(n_dp * FH, D)
-    w_proj = jnp.transpose(proj_buf, (1, 2, 0, 3)).reshape(D, D)
     h1_rows = h1_all.reshape(M, D)
+    h2_rows = h2_all.reshape(M, D)
     dy_rows = dy_all.reshape(M, D)
-
-    def unit_bias(row):
-        return lax.dynamic_slice_in_dim(pad_to(row, 0, UNITS * W), unit * W, W)
-
-    shift = jnp.concatenate([unit_bias(bias_rows[1]), jnp.zeros((W,), F32), unit_bias(bias_rows[2])])
-    qkv = (dot(w_qkv, h1_rows, ((0,), (1,))) + shift[:, None]).astype(BF)
-    qkv = jnp.transpose(qkv.reshape(3, HU, HEAD_DIM, M), (1, 0, 2, 3)).reshape(HU, QKV, M)
-    mine = exchange(
-        lay, "group_to_heads", 4, group_to_heads, data_partners, qkv, struct(n_dp, QKV, M), (HU, n_dp)
-    )
-    mine = jnp.transpose(mine.reshape(n_dp, 3, HEAD_DIM, 2, 4, T), (0, 4, 1, 3, 2, 5))
-    mine = jnp.transpose(lay.to_natural(mine), (1, 2, 3, 0, 4)).reshape(3, 2, HEAD_DIM, length)
-    q, k, v = mine[0], mine[1], mine[2]
-    o, o_low, lse = attend(lay, q, k, v, T)
-    n_dev = 2 * n_ctx
-    ob = exchange(
-        lay,
-        "heads_to_tokens",
-        5,
-        heads_to_tokens,
-        None,
-        o_low,
-        struct(HEADS, HEAD_DIM, T),
-        (n_dev, HEADS),
-    ).reshape(D, T)
-    x1 = x + dot(ob, w_proj, TN) + bias_rows[3]
-    normed_two, hat_two, spread_two = norm_forward(x1, gain_rows[1], bias_rows[4])
-    h2_rows = gather_rows(lay, normed_two.astype(BF)).reshape(M, D)
+    gain_rows = par[:, 0]
+    bias_rows = par[:, 1:4].reshape(6, D)
+    _, hat_one, spread_one = norm_forward(x.astype(F32), gain_rows[0], bias_rows[0])
+    _, hat_two, spread_two = norm_forward(x1, gain_rows[1], bias_rows[4])
     hidden_pre = dot(h2_rows, w_fc, NN) + fc_shift
     hidden, gelu_back = jax.vjp(gelu_tanh, hidden_pre)
     gb = hidden.astype(BF)
@@ -1021,9 +1111,11 @@
     back_two, gain_two_g, bias_two_g = norm_back(dh2.astype(F32), hat_two, spread_two, gain_rows[1])
     dx1 = dy.astype(F32) + back_two
     da = dx1.astype(BF)
-    proj_grad = jnp.transpose(dot(ob, da, NN).astype(BF).reshape(n_ctx, R, 2, D // 2), (2, 0, 1, 3))
+    proj_grad = jnp.stack([dot(ob, da[:, n * (D // 2) : (n + 1) * (D // 2)], TN) for n in range(2)])
+    proj_grad = proj_grad.astype(BF).reshape(2, n_ctx, R, D // 2)
     proj_bias_g = jnp.sum(da.astype(F32), axis=0)
-    dob = dot(w_proj, da, NT).astype(BF).reshape(HEADS, HEAD_DIM, T)
+    dob = dot(w_proj[0], da[:, : D // 2], NT) + dot(w_proj[1], da[:, D // 2 :], NT)
+    dob = dob.astype(BF).reshape(HEADS, HEAD_DIM, T)
     dob = exchange(
         lay,
         "tokens_to_heads",

time: 852 us -> 706 us (0.83)
  Pallas kernels: 554 us -> 482 us
  local copies, waits for them, and re-layouts: 164 us -> 97.8 us
    pallas_call x9 -> x5, Pallas kernels: 519 us -> 461 us  [call(): pl.pallas_call(body, out_shape=outs, in_specs=in_specs, out_specs=out_spe...]
    reshape x11 -> x2, local copies, waits for them, and re-layouts: 44.4 us -> 1.27 us  [the longest x1 1.25 us: shards(): fc_bias.reshape(2, FH // 2)]
    another operation x3 -> x7, local copies, waits for them, and re-layouts: 0.01 us -> 26.9 us  [the longest x4 26.9 us: shards(): jnp.stack([dot(ob, da[:, n * (D // 2):(n + 1) * (D // 2)], TN) for n in r...]
    transpose x4 -> x0, local copies, waits for them, and re-layouts: 23.8 us -> none  [the longest x1 23 us: shards(): w_proj = jnp.transpose(proj_buf, (1, 2, 0, 3)).reshape(D, D)]
    pallas_call x1 -> x0, Pallas kernels: 14.5 us -> none  [attend(): pl.pallas_call(body, grid=(2, n), in_specs=[tiled, whole, whole], out_spe...]
    concatenate x4 -> x0, local copies, waits for them, and re-layouts: 9.57 us -> none  [both(): jnp.concatenate([own, other], axis)]
where the time goes in v2:
time: 706 us; the launch traced here: 698 us
  Pallas kernels  482 us (68%)
  local copies, waits for them, and re-layouts  97.8 us (14%)
  matrix products  54.1 us (8%)
  blocking collectives  37.7 us (5%)
  other arithmetic  25.1 us (4%)
    pallas_call x5, Pallas kernels, call(): pl.pallas_call(body, out_shape=outs, in_specs=in_specs, out_specs=out_spe...  461 us
    dot_general x12, matrix products, dot(): lax.dot_general(left, right, (dims, ((), ())), preferred_element_type=F32)  54.1 us
    psum x1, blocking collectives, shards(): first_rows = lax.psum(first_rows, ('ctx', 'fsdp'))  37.7 us
    another operation x4, local copies, waits for them, and re-layouts, shards(): jnp.stack([dot(ob, da[:, n * (D // 2):(n + 1) * (D // 2)], TN) for n in r...  26.9 us
    pallas_call x1, Pallas kernels, attend_back(): pl.pallas_call(body, grid=(2, n), in_specs=[whole, tiled, tiled, whole, l...  20.9 us

profile of v2, /device:TPU:0, one launch (start us, length us, event | category | flops | bytes accessed | tf_op | source)
XLA Modules:
  0.0 698.1 jit_solution(3899606806275660943)
XLA Ops:
  3.9 2.0 copy.33
  5.9 209.6 %forward.1 = (bf16[2,4,128,1600]{3,2,1,0:T(8,128)(2,1)}, bf16[1600,768]{1,0:T(8,128)(2,1)}, bf16[3,2,64,2048]{3,2,1,0:T(8,128)(2,1)}, f32[2,64,2048]{2,1,0:T(8,1...) custom-call(bf16[128,1600]{1,0:T(8,128)(2,1)} %bitcast.185, ...), custom_call_target="tpu_custom_call" | custom-call | tf_op jit(solution)/shard_map/forward/pallas_call | solution.py:452
  215.5 1.4 reduce_sum.155
  220.9 2.5 slice_bitcast_fusion
  223.4 2.7 reshape.281
  226.1 6.2 fusion.48
  232.2 4.5 convert_reduce_fusion
  236.7 5.4 convolution_convert_fusion.4
  242.1 4.9 convolution_convert_fusion.2
  247.1 4.4 convolution_convert_fusion.3
  251.7 3.6 copy.34
  255.4 5.9 convolution_convert_fusion.1
  261.3 3.6 copy.35
  264.9 68.7 %reduce_rows.1 = (bf16[128,1600]{1,0:T(8,128)(2,1)}, bf16[128,1600]{1,0:T(8,128)(2,1)}) custom-call(bf16[2,4,128,1600]{3,2,1,0:T(8,128)(2,1)} %bitcast.189, bf16[2,4,128,1600]{3,2,1,0:T(8,128)(2,1)} %bitcast.190), custom_call_target="tpu_custom_call" | custom-call | tf_op jit(solution)/shard_map/reduce_rows/pallas_call | solution.py:452
  333.6 1.4 fusion.37
  335.1 2.9 convert_reduce_fusion.6
  339.0 8.2 %reshape.315 = bf16[16,100,800]{1,0,2:T(8,128)(2,1)S(1)} reshape(bf16[1600,800]{0,1:T(8,128)(2,1)} %convolution_convert_fusion.3) | data formatting | bytes 5120000 | tf_op jit(solution)/shard_map/reshape | solution.py:1107
  347.3 5.3 copy.51.fc_r
  352.5 2.9 fusion.7
  355.4 3.5 fusion.16
  358.9 16.8 %tokens_to_heads.1 = bf16[2,16,64,128]{3,2,1,0:T(8,128)(2,1)} custom-call(bf16[25,64,128]{2,1,0:T(8,128)(2,1)} %bitcast.205), custom_call_target="tpu_custom_call" | custom-call | tf_op jit(solution)/shard_map/tokens_to_heads/pallas_call | solution.py:452
  375.8 1.9 copy_bitcast_fusion.1.dob_ref
  377.7 20.9 %attend_back.1 = (bf16[2,64,2048]{2,1,0:T(8,128)(2,1)}, bf16[2,64,2048]{2,1,0:T(8,128)(2,1)}, bf16[2,64,2048]{2,1,0:T(8,128)(2,1)}) custom-call(bf16[2,64,2048]{2,1,0:T(8,128)(2,1)} %get-tuple-element.106.q_ref, bf16[2,64,2048]{2,1,0:T(8,128)(2,1)} %get-tuple-element.105.k_ref, bf16[2,64,2048]{2,1,0:T(8,128)(2,1)} %get-tuple-element.104.v_ref, ...), custom_call_target="tpu_custom_call" | custom-call | tf_op jit(solution)/shard_map/attend_back/pallas_call | solution.py:628
  403.6 2.4 reshape.292.src_r
  406.0 20.3 %heads_to_group.1 = bf16[4,192,1024]{2,1,0:T(8,128)(2,1)} custom-call(bf16[4,192,1024]{2,1,0:T(8,128)(2,1)} %reshape.292.src_r), custom_call_target="tpu_custom_call" | custom-call | tf_op jit(solution)/shard_map/heads_to_group/pallas_call | solution.py:452
  426.3 1.7 convert_reduce_fusion.1
  428.3 1.6 copy.38
  429.9 6.5 convolution_convert_fusion.7
  436.4 2.9 convolution_convert_fusion
  440.9 4.1 reshape.297.qkv_r
  445.0 3.7 copy.39
  448.7 3.6 convolution_convert_fusion.5
  452.3 8.4 %reshape.317 = bf16[1,16,100,800]{2,1,3,0:T(8,128)(2,1)S(1)} reshape(bf16[1600,800]{0,1:T(8,128)(2,1)} %convolution_convert_fusion.5) | data formatting | bytes 5120000 | tf_op jit(solution)/shard_map/stack | solution.py:1114
  460.7 5.1 copy.53
  465.8 3.4 convolution_convert_fusion.6
  469.3 8.2 %reshape.316 = bf16[1,16,100,800]{2,1,3,0:T(8,128)(2,1)S(1)} reshape(bf16[1600,800]{0,1:T(8,128)(2,1)} %convolution_convert_fusion.6) | data formatting | bytes 5120000 | tf_op jit(solution)/shard_map/stack | solution.py:1114
  477.5 5.1 copy.52
  482.7 6.1 pad_maximum_fusion.proj_r
  488.8 145.4 %reduce_grads.1 = (bf16[128,1600]{1,0:T(8,128)(2,1)}, bf16[2,4,100,768]{3,2,1,0:T(8,128)(2,1)}, bf16[2,4,100,800]{3,2,1,0:T(8,128)(2,1)}, bf16[2,200,1600]{2,1,0...) custom-call(bf16[2,4,128,1600]{3,2,1,0:T(8,128)(2,1)} %bitcast.188, ...), custom_call_target="tpu_custom_call" | custom-call | tf_op jit(solution)/shard_map/reduce_grads/pallas_call | solution.py:452
  636.0 1.4 fusion.38
  640.1 37.7 %psum.7 = f32[2,1600]{1,0:T(2,128)S(1)} all-reduce(f32[2,1600]{1,0:T(2,128)S(1)} %pad_maximum_fusion.3), channel_id=1, replica_groups=mesh['ctx'=16,'fsdp'=2] {'ctx','fsdp'}, use_global_device_ids=true, to_apply=%region_17.18 | all-reduce | flops 3200 | bytes 25600 | tf_op jit(solution)/shard_map/psum | solution.py:1177
  679.4 1.5 copy.45
  684.3 1.7 convert_element_type.105
  686.0 1.5 slice_bitcast_fusion.22
  688.5 1.6 concatenate.16
  690.2 2.2 concatenate.15
  693.5 1.4 reshape.309
  695.0 1.5 constant_dynamic-slice_fusion.1
  (110 shorter events, 28.1 us)
Async XLA Ops:
  3.5 2.4 copy-start
  215.5 8.0 %copy-start.5 = (bf16[16,100,800]{2,1,0:T(8,128)(2,1)S(1)}, bf16[16,100,800]{2,1,0:T(8,128)(2,1)}, u32[]{:S(2)}) copy-start(bf16[16,100,800]{2,1,0:T(8,128)(2,1)} %get-tuple-element.48) | copy-start | bytes 7680004
  226.1 6.2 copy-start.12
  226.1 6.2 copy-start.13
  236.7 10.4 %copy-start.15 = (bf16[1024,800]{0,1:T(8,128)(2,1)}, bf16[1024,800]{0,1:T(8,128)(2,1)S(1)}, u32[]{:S(2)}) copy-start(bf16[1024,800]{0,1:T(8,128)(2,1)S(1)} %get-tuple-element.103) | copy-start | bytes 4915204
  242.1 5.0 copy-start.11
  264.9 68.7 %copy-start.2 = (f32[128,1600]{1,0:T(8,128)S(1)}, f32[128,1600]{1,0:T(8,128)}, u32[]{:S(2)}) copy-start(f32[128,1600]{1,0:T(8,128)} %get-tuple-element.46) | copy-start | bytes 2457604
  264.9 70.2 %copy-start.3 = (bf16[1,128,1600]{2,1,0:T(8,128)(2,1)S(1)}, bf16[1,128,1600]{2,1,0:T(8,128)(2,1)}, u32[]{:S(2)}) copy-start(bf16[1,128,1600]{2,1,0:T(8,128)(2,1)} %copy.33) | copy-start | bytes 1228804
  352.5 2.9 copy-start.7
  429.9 6.5 copy-start.14
  488.8 147.3 %copy-start.1 = (bf16[1,128,1600]{2,1,0:T(8,128)(2,1)S(1)}, bf16[1,128,1600]{2,1,0:T(8,128)(2,1)}, u32[]{:S(2)}) copy-start(bf16[1,128,1600]{2,1,0:T(8,128)(2,1)} %copy-done) | copy-start | bytes 1228804
  488.8 148.7 %copy-start.4 = (f32[128,1600]{1,0:T(8,128)S(1)}, f32[128,1600]{1,0:T(8,128)}, u32[]{:S(2)}) copy-start(f32[128,1600]{1,0:T(8,128)} %get-tuple-element.101) | copy-start | bytes 2457604
  634.2 44.3 %copy-start.9 = (bf16[2,4,100,768]{3,2,1,0:T(8,128)(2,1)S(1)}, bf16[2,4,100,768]{3,2,1,0:T(8,128)(2,1)}, u32[]{:S(2)}) copy-start(bf16[2,4,100,768]{3,2,1,0:T(8,128)(2,1)} %get-tuple-element.66) | copy-start | bytes 3686404
  678.5 3.2 copy-start.10
  682.9 4.5 copy-start.6
  688.5 5.0 copy-start.8

commit v3 on v2

--- a/solution.py
+++ b/solution.py
@@ -19,7 +19,7 @@
 MESH = pl.DeviceIdType.MESH
 BF = jnp.bfloat16
 F32 = jnp.float32
-VMEM_LIMIT = 56 * 1024 * 1024
+VMEM_LIMIT = 60 * 1024 * 1024
 LOG2E = 1.0 / math.log(2.0)
 
 
@@ -296,7 +296,7 @@
         yield
         copy.wait_recv()
     else:
-        out[...] = now[0][...]
+        out[...] = now[0][...].astype(out.dtype)
     links.finish()
     yield
 
@@ -366,6 +366,7 @@
         return carry
 
     lax.fori_loop(0, HEADS, begin, 0)
+    yield
 
     @pl.when(active)
     def _():
@@ -402,42 +403,6 @@
 def data_partners(env):
     lay = env.lay
     return [(lay.compose(env.t, (env.d + i) % lay.n_dp), env.s) for i in range(1, lay.n_dp)]
-
-
-def heads_to_group(env, src, out, sems):
-    send_sems, recv_sems, local_sems = sems
-    lay = env.lay
-
-    def copy(there, j, target):
-        return pltpu.make_async_remote_copy(
-            src_ref=src.at[there],
-            dst_ref=out.at[j],
-            send_sem=send_sems.at[there],
-            recv_sem=recv_sems.at[j],
-            device_id=(lay.compose(env.t, target), env.s),
-            device_id_type=MESH,
-        )
-
-    @pl.when(env.d < HU)
-    def _():
-        for i in range(1, lay.n_dp):
-            there = (env.d + i) % lay.n_dp
-            copy(there, env.d, there).start()
-        local = pltpu.make_async_copy(src.at[env.d], out.at[env.d], local_sems.at[0])
-        local.start()
-        local.wait()
-
-    for j in range(HU):
-
-        @pl.when(j != env.d)
-        def _():
-            copy(0, j, j).wait_recv()
-
-    @pl.when(env.d < HU)
-    def _():
-        for i in range(1, lay.n_dp):
-            there = (env.d + i) % lay.n_dp
-            copy(there, env.d, there).wait_send()
 
 
 ANY = pl.BlockSpec(memory_space=pl.ANY)
@@ -462,110 +427,6 @@
     )(*args)
 
 
-def reduce_rows(lay, first, second):
-    block = first.shape[2:]
-
-    def body(a_r, b_r, a_o, b_o, *rest):
-        env = Env(lay)
-        meet(env, tp_partners(env) + [env.other()])
-        run(
-            [
-                reduce(env, a_r, a_o, rest[0:3], rest[6:9], lay.tp_order, lay.tp_index, core=True),
-                reduce(env, b_r, b_o, rest[3:6], rest[9:12], lay.tp_order, lay.tp_index, core=True),
-            ]
-        )
-
-    return call(
-        "reduce_rows",
-        3,
-        body,
-        (first, second),
-        [VM] * 2,
-        [struct(*block)] * 2,
-        [VM] * 2,
-        reduce_scratch(1, 2, True, block) * 2 + sem_shapes(reduce_sends(1, 2, True, False, False)) * 2,
-    )
-
-
-def exchange(lay, name, cid, op, partners, src, out, counts):
-    def body(src_r, out_r, *sems):
-        env = Env(lay)
-        if partners is None:
-            meet_all(env)
-        else:
-            meet(env, partners(env))
-        op(env, src_r, out_r, sems)
-
-    scratch = [
-        pltpu.SemaphoreType.DMA((counts[0],)),
-        pltpu.SemaphoreType.DMA((counts[1],)),
-        pltpu.SemaphoreType.DMA((1,)),
-    ]
-    return call(name, cid, body, (src,), [ANY], out, ANY, scratch)
-
-
-def reduce_grads(lay, rows, qkv, fc, out, proj, small):
-    n_ctx = lay.n_ctx
-    k = len(lay.dp_bits)
-    n_dev = 2 * n_ctx
-
-    def natural(c):
-        return c
-
-    plan = [
-        (rows.shape[2:], 1, 2, True, False, False),
-        (qkv.shape[1:], 4, k, False, True, False),
-        (fc.shape[1:], 4, k, False, True, False),
-        (out.shape[1:], 1, k, False, False, True),
-        (proj.shape[2:], 1, k + 2, True, False, False),
-    ]
-    scratch, spans = [], []
-    for block, have, bits, core, is_rows, halves in plan:
-        part = reduce_scratch(have, bits, core, block)
-        sems = sem_shapes(reduce_sends(have, bits, core, is_rows, halves))
-        spans.append((len(scratch), len(part)))
-        scratch = scratch + part + sems
-    scratch = scratch + sem_shapes(n_dev)
-
-    def body(rows_r, qkv_r, fc_r, out_r, proj_r, small_r, rows_o, qkv_o, fc_o, out_o, proj_o, small_o, *rest):
-        env = Env(lay)
-        meet_all(env)
-
-        def space(i):
-            first, n = spans[i]
-            return rest[first : first + n], rest[first + n : first + n + 3]
-
-        run(
-            [
-                to_everyone(env, small_r, small_o, rest[-3:], False),
-                reduce(env, qkv_r, qkv_o, *space(1), lay.dp_order, natural, rows=True),
-                reduce(env, rows_r, rows_o, *space(0), lay.tp_order, lay.tp_index, core=True),
-                reduce(env, proj_r, proj_o, *space(4), lay.tp_order + lay.dp_order, natural, core=True),
-                reduce(env, fc_r, fc_o, *space(2), lay.dp_order, natural, rows=True),
-                reduce(env, out_r, out_o, *space(3), lay.dp_order, lay.dp_index, halves=True),
-            ]
-        )
-
-    outs = [
-        struct(*rows.shape[2:]),
-        struct(2, 4, *qkv.shape[1:]),
-        struct(2, 4, *fc.shape[1:]),
-        struct(2, *out.shape[1:]),
-        struct(*proj.shape[2:]),
-        struct(*small.shape, dtype=F32),
-    ]
-    return call(
-        "reduce_grads",
-        8,
-        body,
-        (rows, qkv, fc, out, proj, small),
-        [VM] * 5 + [ANY],
-        outs,
-        [VM, ANY, ANY, ANY, VM, ANY],
-        scratch,
-    )
-
-
 def dot(left, right, dims):
     return lax.dot_general(left, right, (dims, ((), ())), preferred_element_type=F32)
 
@@ -575,71 +436,6 @@
 TN = ((0,), (0,))
 SCALE = 1.0 / math.sqrt(HEAD_DIM)
 TILE = 512
-
-
-def attend_back(lay, q, k, v, o, lse, dob):
-    length = q.shape[2]
-    tile = min(TILE, length)
-    n = length // tile
-
-    def body(q_ref, k_ref, v_ref, o_ref, lse_ref, dob_ref, dq_ref, dk_ref, dv_ref, qs, dobs, delta, dq_acc):
-        j = pl.program_id(1)
-
-        @pl.when(j == 0)
-        def _():
-            qs[...] = q_ref[0].T
-            dobs[...] = dob_ref[0].T
-            delta[...] = jnp.sum(dob_ref[0].astype(F32) * o_ref[0], axis=0, keepdims=True)
-            dq_acc[...] = jnp.zeros_like(dq_acc)
-
-        kt = k_ref[0]
-        keys = kt.T
-        values = v_ref[0].T
-
-        def step(i, carry, masked):
-            dk, dv = carry
-            at = pl.ds(pl.multiple_of(i * tile, tile), tile)
-            st = dot(keys, q_ref[0, :, at], NN) * (SCALE * LOG2E)
-            p = jnp.exp2(st - lse_ref[0, :, at])
-            if masked:
-                row = lax.broadcasted_iota(jnp.int32, (tile, tile), 0)
-                col = lax.broadcasted_iota(jnp.int32, (tile, tile), 1)
-                p = jnp.where(row <= col, p, 0.0)
-            dp = dot(values, dob_ref[0, :, at], NN)
-            ds = (p * (dp - delta[:, at])).astype(BF)
-            dv = dv + dot(p.astype(BF), dobs[at, :], NN)
-            dk = dk + dot(ds, qs[at, :], NN)
-            dq_acc[:, at] += dot(kt, ds, NN)
-            return dk, dv
-
-        zero = jnp.zeros((tile, HEAD_DIM), F32)
-        carry = step(j, (zero, zero), True)
-        dk, dv = lax.fori_loop(j + 1, n, functools.partial(step, masked=False), carry)
-        dk_ref[0] = (dk * SCALE).T.astype(BF)
-        dv_ref[0] = dv.T.astype(BF)
-
-        @pl.when(j == n - 1)
-        def _():
-            dq_ref[0] = (dq_acc[...] * SCALE).astype(BF)
-
-    whole = pl.BlockSpec((1, HEAD_DIM, length), lambda b, i: (b, 0, 0))
-    tiled = pl.BlockSpec((1, HEAD_DIM, tile), lambda b, i: (b, 0, i))
-    line = pl.BlockSpec((1, 1, length), lambda b, i: (b, 0, 0))
-    return pl.pallas_call(
-        body,
-        grid=(2, n),
-        in_specs=[whole, tiled, tiled, whole, line, whole],
-        out_specs=[whole, tiled, tiled],
-        out_shape=[struct(2, HEAD_DIM, length)] * 3,
-        scratch_shapes=[
-            pltpu.VMEM((length, HEAD_DIM), BF),
-            pltpu.VMEM((length, HEAD_DIM), BF),
-            pltpu.VMEM((1, length), F32),
-            pltpu.VMEM((HEAD_DIM, length), F32),
-        ],
-        compiler_params=pltpu.CompilerParams(vmem_limit_bytes=VMEM_LIMIT),
-        name="attend_back",
-    )(q, k, v, o, lse, dob)
 
 
 class Background:
@@ -1035,178 +831,493 @@
     )
 
 
-def norm_forward(values, gain, bias):
-    centre = values - jnp.mean(values, axis=-1, keepdims=True)
-    spread = lax.rsqrt(jnp.mean(centre * centre, axis=-1, keepdims=True) + EPS)
-    normed = centre * spread
-    return (normed * gain + bias, normed, spread)
-
-
-def norm_back(grad_out, normed, spread, gain):
-    scaled = grad_out * gain
-    grad_in = spread * (
-        scaled
-        - jnp.mean(scaled, axis=-1, keepdims=True)
-        - normed * jnp.mean(scaled * normed, axis=-1, keepdims=True)
-    )
-    return (grad_in, jnp.sum(grad_out * normed, axis=0), jnp.sum(grad_out, axis=0))
-
-
-def gelu_tanh(values):
-    return jax.nn.gelu(values, approximate=True)
-
-
-def pad_to(x, axis, size):
-    if x.shape[axis] == size:
-        return x
-    widths = [(0, 0)] * x.ndim
-    widths[axis] = (0, size - x.shape[axis])
-    return jnp.pad(x, widths)
-
-
-def shards(lay, tokens, qkv_weight, proj_weight, fc_weight, out_weight, gains, biases, fc_bias, cotangent):
+def drive(generator, background):
+    for _ in generator:
+        background.step()
+
+
+def by_side(s, f):
+    for side in range(2):
+
+        @pl.when(s == side)
+        def _():
+            f(side)
+
+
+def middle(lay, x, h2, dy_all, fc, out, shift, x1, dy, pj, par):
     n_ctx, n_dp = lay.n_ctx, lay.n_dp
-    c = lax.axis_index("ctx")
-    s = lax.axis_index("fsdp")
-    t = lay.tp_index(c)
-    unit = 2 * t + s
-    T = tokens.shape[1]
-    M = 8 * T
-    R = D // n_ctx
-    FB = FF // n_ctx
+    n_dev = 2 * n_ctx
+    k = len(lay.dp_bits)
+    T = x.shape[0]
+    R, FB = D // n_ctx, FF // n_ctx
+    FH = FB // 2
+    U = n_dp * FH
+    G = 4 * T
+    half = D // 2
+    chunk = 2 * T
+
+    def natural(c):
+        return c
+
+    def body(*refs):
+        (h2_r, dya_r, fc_r, out_r, pj_r, shift_r, x1_r, dy_r, par_r) = refs[:9]
+        (mixed_o, dx1_o, dob_o, fc_o, out_o, vec_o, fcb_o) = refs[9:16]
+        (
+            h2_v, dy_v, fc_b, fc_w, out_b, out_w, pj_v, gb_v, du_v, back_p, dh2_v, mix_v, dob_s, fc_v, out_v,
+        ) = refs[16:31]
+        rest = refs[31:]
+        plan = [
+            (0, 3, 3),
+            (1, 3, 3),
+            (2, k, 3),
+            (3, k, 3),
+        ]
+        spans, first = [], 0
+        for _, n, m in plan:
+            spans.append((rest[first : first + n], rest[first + n : first + n + m]))
+            first += n + m
+        sems = rest[first:]
+        env = Env(lay)
+        s = env.s
+        loads = Links((None, None, sems[3]))
+        load = {}
+        for name, a, b in (
+            ("h2", h2_r, h2_v),
+            ("fc", fc_r, fc_b),
+            ("dy", dya_r, dy_v),
+            ("out", out_r, out_b),
+            ("pj", pj_r, pj_v),
+        ):
+            load[name] = loads.local(a, b)
+        meet_all(env)
+        load["fc"].wait()
+        for c in range(n_ctx):
+            fc_w[c * R : (c + 1) * R, :] = fc_b[c]
+        load["out"].wait()
+        for d in range(n_dp):
+            out_w[d * FH : (d + 1) * FH, :] = out_b[d]
+        load["h2"].wait()
+        load["dy"].wait()
+
+        def forth_and_back(q):
+            @pl.loop(0, G // chunk)
+            def _(i):
+                rows = h2_v[q, pl.ds(2 * i, 2)].reshape(chunk, D)
+                u = dot(rows, fc_w[...], NN) + shift_r[...]
+                square = u * u
+                th = jnp.tanh(math.sqrt(2 / math.pi) * (u + 0.044715 * square * u))
+                up = 0.5 * (1.0 + th)
+                at = pl.ds(pl.multiple_of(i * chunk, chunk), chunk)
+                gb_v[q, at, :] = (u * up).astype(BF)
+                slope = up + (0.5 * math.sqrt(2 / math.pi)) * u * (1.0 - th * th) * (
+                    1.0 + (3 * 0.044715) * square
+                )
+                dact = dot(dy_v[q, pl.ds(2 * i, 2)].reshape(chunk, D), out_w[...], NT)
+                du = (dact * slope).astype(BF)
+                du_v[q, at, :] = du
+                back = dot(du, fc_w[...], NT).astype(BF)
+                back_p[q, pl.ds(2 * i, 2)] = back.reshape(2, T, D)
+
+        forth_and_back(1 - s)
+        rows = reduce(env, back_p, dh2_v, *spans[0], lay.tp_order, lay.tp_index, core=True)
+        next(rows)
+        forth_and_back(s)
+        next(rows)
+        bg = Background()
+        for d in range(n_dp):
+            left = gb_v[:, :, d * FH : (d + 1) * FH].reshape(2 * G, FH)
+            out_b[d] = dot(left, dy_v[...].reshape(2 * G, D), TN).astype(BF)
+        bg.add(reduce(env, out_b, out_v, *spans[3], lay.dp_order, lay.dp_index, halves=True))
+        bg.step()
+        next(rows)
+        for c in range(0, n_ctx, 4):
+            left = h2_v[:, :, :, c * R : (c + 4) * R].reshape(2 * G, 4 * R)
+            made = dot(left, du_v[...].reshape(2 * G, U), TN).astype(BF)
+            for i in range(4):
+                fc_b[c + i] = made[i * R : (i + 1) * R, :]
+        bg.add(reduce(env, fc_b, fc_v, *spans[2], lay.dp_order, natural, rows=True))
+        bg.step()
+        for _ in range(2):
+            next(rows)
+        fcb_o[...] = jnp.sum(du_v[...].reshape(2 * G, U).astype(F32), axis=0, keepdims=True)
+        x1 = x1_r[...]
+        hat, spread = norm_stats(x1)
+        dy_own = dy_r[...].astype(F32)
+        vec_o[...] = jnp.zeros_like(vec_o)
+        vec_o[3:4, :] = jnp.sum(dy_own, axis=0, keepdims=True)
+        for _ in range(2):
+            next(rows)
+        for q in range(2):
+
+            @pl.loop(0, G // chunk)
+            def _(i):
+                at = pl.ds(pl.multiple_of(i * chunk, chunk), chunk)
+                part = dot(gb_v[q, at, :], out_w[...], NN).astype(BF)
+                h2_v[q, pl.ds(2 * i, 2)] = part.reshape(2, T, D)
+
+        finish(rows)
+        dh2 = dh2_v[...].astype(F32)
+        scaled = dh2 * par_r[1, 0:1, :]
+        dx1 = dy_own + spread * (
+            scaled
+            - jnp.mean(scaled, axis=-1, keepdims=True)
+            - hat * jnp.mean(scaled * hat, axis=-1, keepdims=True)
+        )
+        dx1_o[...] = dx1
+        da = dx1.astype(BF)
+        load["pj"].wait()
+        dob = dot(da[:, :half], pj_v[0], NT) + dot(da[:, half:], pj_v[1], NT)
+        dob_s[...] = dob.astype(BF).T.reshape(HEADS, HEAD_DIM, T)
+        heads = tokens_to_heads(env, dob_s, dob_o, sems[0:3])
+        next(heads)
+        mixing = reduce(env, h2_v, mix_v, *spans[1], lay.tp_order, lay.tp_index, core=True)
+        next(mixing)
+        bg.add(mixing)
+        vec_o[0:1, :] = jnp.sum(dh2 * hat, axis=0, keepdims=True)
+        vec_o[1:2, :] = jnp.sum(da.astype(F32), axis=0, keepdims=True)
+        vec_o[2:3, :] = jnp.sum(dh2, axis=0, keepdims=True)
+        bg.finish()
+        finish(heads)
+        mixed_o[...] = (x1 + mix_v[...].astype(F32) + par_r[1, 3:4, :]).astype(BF)
+
+        def last(side):
+            pieces = []
+            for c in range(n_ctx // 2 * side, n_ctx // 2 * (side + 1)):
+                for h in range(2):
+                    first = lay.dp_index(c) * FH
+                    pieces.append(fc_v[h, lay.tp_index(c)][:, first : first + FH])
+            fc_o[...] = jnp.concatenate(pieces, axis=1).astype(F32)
+            out_o[...] = jnp.concatenate(
+                [out_v[h][:, side * half : (side + 1) * half] for h in range(2)], axis=0
+            ).astype(F32)
+
+        by_side(s, last)
+
+    outs = [
+        struct(T, D),
+        struct(T, D, dtype=F32),
+        struct(2, n_ctx, HEAD_DIM, T),
+        struct(R, FF // 2, dtype=F32),
+        struct(FB, half, dtype=F32),
+        struct(8, D, dtype=F32),
+        struct(1, U, dtype=F32),
+    ]
+    scratch = [
+        pltpu.VMEM((2, 4, T, D), BF),
+        pltpu.VMEM((2, 4, T, D), BF),
+        pltpu.VMEM((n_ctx, R, U), BF),
+        pltpu.VMEM((D, U), BF),
+        pltpu.VMEM((n_dp, FH, D), BF),
+        pltpu.VMEM((U, D), BF),
+        pltpu.VMEM((2, D, half), BF),
+        pltpu.VMEM((2, G, U), BF),
+        pltpu.VMEM((2, G, U), BF),
+        pltpu.VMEM((2, 4, T, D), BF),
+        pltpu.VMEM((T, D), BF),
+        pltpu.VMEM((T, D), BF),
+        pltpu.VMEM((HEADS, HEAD_DIM, T), BF),
+        pltpu.VMEM((2, 4, R, U), BF),
+        pltpu.VMEM((2, FH, D), BF),
+    ]
+    for _ in range(2):
+        scratch += reduce_scratch(1, 2, True, (T, D)) + sem_shapes(reduce_sends(1, 2, True, False, False))
+    scratch += reduce_scratch(4, k, False, (R, U)) + sem_shapes(reduce_sends(4, k, False, True, False))
+    scratch += reduce_scratch(1, k, False, (FH, D)) + sem_shapes(reduce_sends(1, k, False, False, True))
+    DMA = pltpu.SemaphoreType.DMA
+    scratch += [DMA((HEADS,)), DMA((n_dev,)), DMA((1,)), DMA((5,))]
+    args = (h2, dy_all, fc, out, pj, shift, x1, dy, par)
+    out_specs = [VM] * 2 + [ANY] + [VM] * 4
+    return call("middle", 1, body, args, [ANY] * 5 + [VM] * 4, outs, out_specs, scratch)
+
+
+def heads_to_group(env, src, out, sems, q):
+    send_sems, recv_sems, local_sems = sems
+    lay = env.lay
+
+    def copy(there, j, target):
+        return pltpu.make_async_remote_copy(
+            src_ref=src.at[q, there],
+            dst_ref=out.at[q, j],
+            send_sem=send_sems.at[q, there],
+            recv_sem=recv_sems.at[q, j],
+            device_id=(lay.compose(env.t, target), env.s),
+            device_id_type=MESH,
+        )
+
+    local = pltpu.make_async_copy(src.at[q, env.d], out.at[q, env.d % HU], local_sems.at[q])
+
+    @pl.when(env.d < HU)
+    def _():
+        for i in range(1, lay.n_dp):
+            there = (env.d + i) % lay.n_dp
+            copy(there, env.d, there).start()
+        local.start()
+
+    yield
+
+    @pl.when(env.d < HU)
+    def _():
+        local.wait()
+
+    for j in range(HU):
+
+        @pl.when(j != env.d)
+        def _():
+            copy(0, j, j).wait_recv()
+
+    yield
+
+    @pl.when(env.d < HU)
+    def _():
+        for i in range(1, lay.n_dp):
+            there = (env.d + i) % lay.n_dp
+            copy(there, env.d, there).wait_send()
+
+
+def backward(lay, x, heads, o, lse, dob, wq, h1, ob, vec, fcb, dx1, par):
+    n_ctx, n_dp = lay.n_ctx, lay.n_dp
+    n_dev = 2 * n_ctx
+    k = len(lay.dp_bits)
+    T = x.shape[0]
+    R, FB = D // n_ctx, FF // n_ctx
     FH = FB // 2
     W = HU * HEAD_DIM
+    G = 4 * T
+    half = D // 2
     length = n_ctx * T
-
-    def side(x, axis):
-        return lax.dynamic_index_in_dim(x, s, axis, keepdims=False)
-
+    tile = TILE if length <= 4 * TILE else TILE // 2
+    n_tiles = length // tile
+    wide = UNITS * W
+
+    def natural(c):
+        return c
+
+    def body(*refs):
+        (x_r, heads_r, o_r, lse_r, dob_r, wq_r, h1_r, ob_r, vec_r, fcb_r, dx1_r, par_r) = refs[:12]
+        (grad_o, qkv_o, proj_o, small_o) = refs[12:16]
+        (
+            heads_v, o_v, dob_n, qs, dobs, delta, dq_acc, parts, land, dqkv, dh1_p, dh1_v, q_g, q_v, wide_v,
+            small_s, small_v, pg,
+        ) = refs[16:34]
+        rest = refs[34:]
+        spans, first = [], 0
+        for n in (3, k, k + 3):
+            spans.append((rest[first : first + n], rest[first + n : first + n + 3]))
+            first += n + 3
+        sems = rest[first:]
+        env = Env(lay)
+        s = env.s
+        meet_all(env)
+        bg = Background()
+        for n in range(2):
+            right = dx1_r[:, n * half : (n + 1) * half].astype(BF)
+            for c in range(0, n_ctx, 4):
+                made = dot(ob_r[:, c * R : (c + 4) * R], right, TN).astype(BF)
+                for i in range(4):
+                    pg[n, c + i] = made[i * R : (i + 1) * R, :]
+        bg.add(reduce(env, pg, proj_o, *spans[2], lay.tp_order + lay.dp_order, natural, core=True))
+        bg.step()
+        small_s[...] = jnp.zeros_like(small_s)
+        wide_v[...] = jnp.zeros_like(wide_v)
+        moving = []
+        _, active = own_head(env)
+
+        def loads(q):
+            copies = [pltpu.make_async_copy(heads_r.at[n, q], heads_v.at[n], sems[6].at[n]) for n in range(3)]
+            copies.append(pltpu.make_async_copy(o_r.at[q], o_v, sems[6].at[3]))
+            for c in range(n_ctx):
+                copies.append(
+                    pltpu.make_async_copy(
+                        dob_r.at[q, c], dob_n.at[:, pl.ds(c * T, T)], sems[6].at[4 + c]
+                    )
+                )
+            return copies
+
+        for copy in loads(0):
+            copy.start()
+        for q in range(2):
+            for copy in loads(q):
+                copy.wait()
+
+            @pl.when(jnp.logical_not(active))
+            def _():
+                dob_n[...] = jnp.zeros_like(dob_n)
+
+            qs[...] = heads_v[0].T
+            dobs[...] = dob_n[...].T
+            delta[...] = jnp.sum(dob_n[...].astype(F32) * o_v[...], axis=0, keepdims=True)
+            dq_acc[...] = jnp.zeros_like(dq_acc)
+
+            def put(n, first, block):
+                for b in range(block.shape[1] // T):
+                    c = first // T + b
+                    tc, dc = lay.tp_index(c), lay.dp_index(c)
+                    parts[q, dc, n * HEAD_DIM : (n + 1) * HEAD_DIM, tc * T : (tc + 1) * T] = block[
+                        :, b * T : (b + 1) * T
+                    ]
+
+            for j in range(n_tiles):
+                here = slice(j * tile, (j + 1) * tile)
+                kt = heads_v[1, :, here]
+                keys = kt.T
+                values = heads_v[2, :, here].T
+
+                def step(i, carry, masked):
+                    dk, dv = carry
+                    at = pl.ds(pl.multiple_of(i * tile, tile), tile)
+                    st = dot(keys, heads_v[0, :, at], NN) * (SCALE * LOG2E)
+                    p = jnp.exp2(st - lse_r[q, :, at])
+                    if masked:
+                        row = lax.broadcasted_iota(jnp.int32, (tile, tile), 0)
+                        col = lax.broadcasted_iota(jnp.int32, (tile, tile), 1)
+                        p = jnp.where(row <= col, p, 0.0)
+                    dp = dot(values, dob_n[:, at], NN)
+                    ds = (p * (dp - delta[:, at])).astype(BF)
+                    dv = dv + dot(p.astype(BF), dobs[at, :], NN)
+                    dk = dk + dot(ds, qs[at, :], NN)
+                    dq_acc[:, at] += dot(kt, ds, NN)
+                    return dk, dv
+
+                zero = jnp.zeros((tile, HEAD_DIM), F32)
+                carry = step(j, (zero, zero), True)
+                if j + 1 < n_tiles:
+                    carry = lax.fori_loop(j + 1, n_tiles, functools.partial(step, masked=False), carry)
+                put(1, j * tile, (carry[0] * SCALE).T.astype(BF))
+                put(2, j * tile, carry[1].T.astype(BF))
+                bg.step(4)
+            put(0, 0, (dq_acc[...] * SCALE).astype(BF))
+            if q == 0:
+                for copy in loads(1):
+                    copy.start()
+            g = heads_to_group(env, parts, land, sems[0:3], q)
+            next(g)
+            moving.append(g)
+        for q in range(2):
+            next(moving[q])
+            rows = []
+            for n in range(3):
+                for j in range(HU):
+                    rows.append(land[q, j, n * HEAD_DIM : (n + 1) * HEAD_DIM, :])
+            dqkv[q] = jnp.concatenate(rows, axis=0).T
+            dh1_p[q] = dot(dqkv[q], wq_r[...], NT).astype(BF).reshape(4, T, D)
+        rows_h1 = reduce(env, dh1_p, dh1_v, *spans[0], lay.tp_order, lay.tp_index, core=True)
+        next(rows_h1)
+        for c in range(0, n_ctx, 4):
+            left = h1_r[:, :, :, c * R : (c + 4) * R].reshape(2 * G, 4 * R)
+            made = dot(left, dqkv[...].reshape(2 * G, 3 * W), TN).astype(BF)
+            for i in range(4):
+                q_g[c + i] = made[i * R : (i + 1) * R, :]
+        grads = reduce(env, q_g, q_v, *spans[1], lay.dp_order, natural, rows=True)
+        next(grads)
+        bg.add(grads)
+        unit = 2 * env.t + s
+        sums = jnp.sum(dqkv[0].astype(F32), axis=0, keepdims=True) + jnp.sum(
+            dqkv[1].astype(F32), axis=0, keepdims=True
+        )
+        cols = pl.ds(pl.multiple_of(unit * W, W), W)
+        wide_v[2:3, cols] = sums[:, :W]
+        wide_v[3:4, cols] = sums[:, 2 * W :]
+        hat, spread = norm_stats(x_r[...].astype(F32))
+        drive(rows_h1, bg)
+        dh1 = dh1_v[...].astype(F32)
+        scaled = dh1 * par_r[0, 0:1, :]
+        grad_o[...] = dx1_r[...] + spread * (
+            scaled
+            - jnp.mean(scaled, axis=-1, keepdims=True)
+            - hat * jnp.mean(scaled * hat, axis=-1, keepdims=True)
+        )
+        wide_v[0:1, :D] = jnp.sum(dh1 * hat, axis=0, keepdims=True)
+        wide_v[1:2, :D] = jnp.sum(dh1, axis=0, keepdims=True)
+        for c in range(n_ctx):
+            small_s[2 * c, 0:4, :R] = wide_v[0:4, c * R : (c + 1) * R]
+            small_s[2 * c + 1, 0:4, :R] = vec_r[0:4, c * R : (c + 1) * R]
+        for d in range(n_dp):
+            owner = lay.compose(env.t, d) * 2 + s
+            for h in range(2):
+                first = d * FH + h * (FH // 2)
+                small_s[owner, 4 + h : 5 + h, : FH // 2] = fcb_r[:, first : first + FH // 2]
+        everyone = to_everyone(env, small_s, small_v, sems[3:6], False)
+        next(everyone)
+        bg.finish()
+        for g in moving:
+            finish(g)
+
+        def last(side):
+            parts_all = []
+            for n in range(3):
+                pieces = [q_v[h, u][:, n * W : (n + 1) * W] for u in range(4) for h in range(2)]
+                parts_all.append(jnp.concatenate(pieces, axis=1)[:, :D])
+            whole = jnp.concatenate(parts_all, axis=1)
+            qkv_o[...] = whole[:, side * (3 * half) : (side + 1) * (3 * half)].astype(F32)
+
+        by_side(s, last)
+        finish(everyone)
+        total = small_v[0]
+        for r in range(1, n_dev):
+            total = total + small_v[r]
+        small_o[...] = total
+
+    outs = [
+        struct(T, D, dtype=F32),
+        struct(R, 3 * half, dtype=F32),
+        struct(R, half, dtype=F32),
+        struct(8, 128, dtype=F32),
+    ]
+    scratch = [
+        pltpu.VMEM((3, HEAD_DIM, length), BF),
+        pltpu.VMEM((HEAD_DIM, length), F32),
+        pltpu.VMEM((HEAD_DIM, length), BF),
+        pltpu.VMEM((length, HEAD_DIM), BF),
+        pltpu.VMEM((length, HEAD_DIM), BF),
+        pltpu.VMEM((1, length), F32),
+        pltpu.VMEM((HEAD_DIM, length), F32),
+        pltpu.VMEM((2, n_dp, QKV, G), BF),
+        pltpu.VMEM((2, HU, QKV, G), BF),
+        pltpu.VMEM((2, G, 3 * W), BF),
+        pltpu.VMEM((2, 4, T, D), BF),
+        pltpu.VMEM((T, D), BF),
+        pltpu.VMEM((n_ctx, R, 3 * W), BF),
+        pltpu.VMEM((2, 4, R, 3 * W), BF),
+        pltpu.VMEM((8, wide), F32),
+        pltpu.VMEM((n_dev, 8, 128), F32),
+        pltpu.VMEM((n_dev, 8, 128), F32),
+        pltpu.VMEM((2, n_ctx, R, half), BF),
+    ]
+    scratch += reduce_scratch(1, 2, True, (T, D)) + sem_shapes(reduce_sends(1, 2, True, False, False))
+    scratch += reduce_scratch(4, k, False, (R, 3 * W)) + sem_shapes(reduce_sends(4, k, False, True, False))
+    scratch += reduce_scratch(1, k + 2, True, (R, half)) + sem_shapes(
+        reduce_sends(1, k + 2, True, False, False)
+    )
+    DMA = pltpu.SemaphoreType.DMA
+    scratch += [DMA((2, n_dp)), DMA((2, HU)), DMA((2,))] + sem_shapes(n_dev) + [DMA((4 + n_ctx,))]
+    args = (x, heads, o, lse, dob, wq, h1, ob, vec, fcb, dx1, par)
+    in_specs = [VM, ANY, ANY, VM, ANY] + [VM] * 7
+    return call("backward", 2, body, args, in_specs, outs, [VM] * 4, scratch)
+
+
+def shards(lay, tokens, qkv_weight, proj_weight, fc_weight, out_weight, gains, biases, fc_bias, cotangent):
+    T = tokens.shape[1]
+    R = D // lay.n_ctx
+    FH = FF // lay.n_ctx // 2
     x = tokens.reshape(T, D)
     dy = cotangent.reshape(T, D)
-    n_dev = 2 * n_ctx
-    (h1_all, w_qkv, heads, o, lse, ob, w_proj, x1, h2_all, fc_buf, out_buf, dy_all, fc_shift, par) = forward(
+    (h1, wq, heads, o, lse, ob, pj, x1, h2, fc, out, dy_all, shift, par) = forward(
         lay, x, gains, biases, fc_bias.reshape(2, FH // 2), qkv_weight, fc_weight, out_weight, proj_weight, dy
     )
-    q, k, v = heads[0], heads[1], heads[2]
-    w_fc = fc_buf.reshape(D, n_dp * FH)
-    w_out = out_buf.reshape(n_dp * FH, D)
-    h1_rows = h1_all.reshape(M, D)
-    h2_rows = h2_all.reshape(M, D)
-    dy_rows = dy_all.reshape(M, D)
-    gain_rows = par[:, 0]
-    bias_rows = par[:, 1:4].reshape(6, D)
-    _, hat_one, spread_one = norm_forward(x.astype(F32), gain_rows[0], bias_rows[0])
-    _, hat_two, spread_two = norm_forward(x1, gain_rows[1], bias_rows[4])
-    hidden_pre = dot(h2_rows, w_fc, NN) + fc_shift
-    hidden, gelu_back = jax.vjp(gelu_tanh, hidden_pre)
-    gb = hidden.astype(BF)
-    mixed_part = dot(gb, w_out, NN).astype(BF).reshape(2, 4, T, D)
-    du = gelu_back(dot(dy_rows, w_out, NT))[0].astype(BF)
-    dh2_part = dot(du, w_fc, NT).astype(BF).reshape(2, 4, T, D)
-    mixed_sum, dh2 = reduce_rows(lay, mixed_part, dh2_part)
-    fc_grad = dot(h2_rows, du, TN).astype(BF).reshape(n_ctx, R, n_dp * FH)
-    out_grad = dot(gb, dy_rows, TN).astype(BF).reshape(n_dp, FH, D)
-    fc_bias_part = jnp.sum(du.astype(F32), axis=0)
-    mixed = (x1 + mixed_sum.astype(F32) + bias_rows[5]).astype(BF)
-    back_two, gain_two_g, bias_two_g = norm_back(dh2.astype(F32), hat_two, spread_two, gain_rows[1])
-    dx1 = dy.astype(F32) + back_two
-    da = dx1.astype(BF)
-    proj_grad = jnp.stack([dot(ob, da[:, n * (D // 2) : (n + 1) * (D // 2)], TN) for n in range(2)])
-    proj_grad = proj_grad.astype(BF).reshape(2, n_ctx, R, D // 2)
-    proj_bias_g = jnp.sum(da.astype(F32), axis=0)
-    dob = dot(w_proj[0], da[:, : D // 2], NT) + dot(w_proj[1], da[:, D // 2 :], NT)
-    dob = dob.astype(BF).reshape(HEADS, HEAD_DIM, T)
-    dob = exchange(
-        lay,
-        "tokens_to_heads",
-        6,
-        tokens_to_heads,
-        None,
-        dob,
-        struct(2, n_ctx, HEAD_DIM, T),
-        (HEADS, n_dev),
+    mixed, dx1, dob, fc_grad, out_grad, vec, fcb = middle(
+        lay, x, h2, dy_all, fc, out, shift, x1, dy, pj, par
     )
-    dob = jnp.transpose(dob, (0, 2, 1, 3)).reshape(2, HEAD_DIM, length)
-    dq, dk, dv = attend_back(lay, q, k, v, o, lse, dob)
-    grads = jnp.stack([dq, dk, dv]).reshape(3, 2, HEAD_DIM, n_ctx, T)
-    grads = lay.from_natural(jnp.transpose(grads, (3, 0, 2, 1, 4)))
-    grads = jnp.transpose(grads, (0, 2, 3, 4, 1, 5)).reshape(n_dp, QKV, M)
-    dqkv = exchange(
-        lay, "heads_to_group", 7, heads_to_group, data_partners, grads, struct(HU, QKV, M), (n_dp, HU)
-    )
-    dqkv = jnp.transpose(dqkv.reshape(HU, 3, HEAD_DIM, M), (1, 0, 2, 3)).reshape(3 * W, M)
-    dh1_part = dot(dqkv, w_qkv, ((0,), (1,))).astype(BF).reshape(2, 4, T, D)
-    qkv_grad = dot(h1_rows, dqkv, ((0,), (1,))).astype(BF).reshape(n_ctx, R, 3 * W)
-    qkv_bias_part = jnp.sum(dqkv.astype(F32), axis=1)
-
-    def unit_row(part):
-        row = lax.dynamic_update_slice_in_dim(jnp.zeros((UNITS * W,), F32), part, unit * W, 0)
-        return row[:D]
-
-    dy_sum = jnp.sum(dy.astype(F32), axis=0)
-    gains_part = jnp.stack([jnp.zeros((D,), F32), gain_two_g])
-    biases_part = jnp.stack(
-        [
-            jnp.zeros((D,), F32),
-            unit_row(qkv_bias_part[:W]),
-            unit_row(qkv_bias_part[2 * W :]),
-            proj_bias_g,
-            bias_two_g,
-            dy_sum,
-        ]
-    )
-    parts = lay.from_natural(jnp.zeros((n_ctx, 2, FH), F32))
-    mask = (jnp.arange(4)[None, :, None, None] == t) & (jnp.arange(2)[None, None, :, None] == s)
-    parts = jnp.where(mask, fc_bias_part.reshape(n_dp, 1, 1, FH), parts)
-    fc_bias_full = lay.to_natural(parts)
-    small_parts = jnp.concatenate(
-        [
-            jnp.transpose(gains_part.reshape(2, n_ctx, R), (1, 0, 2)),
-            jnp.transpose(biases_part.reshape(2, 3, n_ctx, R), (2, 0, 1, 3)).reshape(n_ctx, 2, 3 * R),
-            fc_bias_full,
-        ],
-        axis=2,
-    )
-    small_parts = pad_to(small_parts, 2, 1024).reshape(n_dev, 8, 128)
-    dh1, qkv_sum, fc_sum, out_sum, proj_sum, small_sum = reduce_grads(
-        lay, dh1_part, qkv_grad, fc_grad, out_grad, proj_grad, small_parts
-    )
-    back_one, gain_one_g, bias_one_g = norm_back(dh1.astype(F32), hat_one, spread_one, gain_rows[0])
-    input_grad = (dx1 + back_one).reshape(tokens.shape)
-    first_rows = jnp.stack([gain_one_g, bias_one_g])
-    first_rows = lax.psum(first_rows, ("ctx", "fsdp"))
-    small_sum = jnp.sum(small_sum.reshape(n_dev, 1024), axis=0)
-    own_cols = lax.dynamic_slice_in_dim(first_rows, c * R, R, 1)
-    first_side = (s == 0).astype(F32)
-    gains_out = (small_sum[:R] + own_cols[0] * first_side).reshape(1, R)
-    biases_out = small_sum[R : 4 * R].reshape(3, R)
-    biases_out = biases_out.at[0].add(own_cols[1] * first_side)
-    fc_bias_out = small_sum[4 * R : 4 * R + FH]
-
-    qkv_out = jnp.transpose(qkv_sum.reshape(2, 4, R, 3, W), (2, 3, 1, 0, 4))
-    qkv_out = qkv_out.reshape(R, 3, UNITS * W)[:, :, :D].reshape(R, 2, 3 * D // 2)
-    qkv_out = side(qkv_out, 1).astype(F32)
-    fc_out = fc_sum.reshape(2, 4, R, n_dp, FH)
-    fc_cols = []
-    for b in range(n_ctx):
-        for half in range(2):
-            fc_cols.append(fc_sum[half, lay.tp_index(b), :, lay.dp_index(b) * FH : (lay.dp_index(b) + 1) * FH])
-    half = n_ctx
-    fc_out = jnp.where(
-        s == 0, jnp.concatenate(fc_cols[:half], axis=1), jnp.concatenate(fc_cols[half:], axis=1)
-    ).astype(F32)
-    out_out = side(out_sum.reshape(FB, 2, D // 2), 1).astype(F32)
-    proj_out = proj_sum.astype(F32)
+    input_grad, qkv_grad, proj_grad, small = backward(lay, x, heads, o, lse, dob, wq, h1, ob, vec, fcb, dx1, par)
     return (
         mixed.reshape(tokens.shape),
-        input_grad,
-        qkv_out,
-        proj_out,
-        fc_out,
-        out_out,
-        gains_out,
-        biases_out,
-        fc_bias_out,
+        input_grad.reshape(tokens.shape),
+        qkv_grad,
+        proj_grad,
+        fc_grad,
+        out_grad,
+        small[0:1, :R],
+        small[1:4, :R],
+        small[4:6, : FH // 2].reshape(FH),
     )
 
 

time: 706 us -> 478 us (0.68)
  local copies, waits for them, and re-layouts: 97.8 us -> 16.1 us
  matrix products: 54.1 us -> 0 us
  blocking collectives: 37.7 us -> 0 us
  Pallas kernels: 482 us -> 452 us
  other arithmetic: 25.1 us -> 0 us
    dot_general x12 -> x0, matrix products: 54.1 us -> none  [dot(): lax.dot_general(left, right, (dims, ((), ())), preferred_element_type=F32)]
    psum x1 -> x0, blocking collectives: 37.7 us -> none  [shards(): first_rows = lax.psum(first_rows, ('ctx', 'fsdp'))]
    reshape x17 -> x1, local copies, waits for them, and re-layouts: 31.7 us -> 0.64 us  [shards(): small[4:6, :FH // 2].reshape(FH)]
    another operation x17 -> x0, local copies, waits for them, and re-layouts: 27.1 us -> none  [the longest x4 26.9 us: shards(): jnp.stack([dot(ob, da[:, n * (D // 2):(n + 1) * (D // 2)], TN) for n in r...]
    pallas_call x1 -> x0, Pallas kernels: 20.9 us -> none  [attend_back(): pl.pallas_call(body, grid=(2, n), in_specs=[whole, tiled, tiled, whole, l...]
    reduce_sum x9 -> x0, other arithmetic: 11.7 us -> none  [the longest x1 2.86 us: shards(): proj_bias_g = jnp.sum(da.astype(F32), axis=0)]
    convert_element_type x3 -> x0, local copies, waits for them, and re-layouts: 10.9 us -> none  [the longest x1 3.66 us: shards(): dh1_part = dot(dqkv, w_qkv, ((0,), (1,))).astype(BF).reshape(2, 4, T, D)]
    pallas_call x5 -> x3, Pallas kernels: 461 us -> 452 us  [call(): pl.pallas_call(body, out_shape=outs, in_specs=in_specs, out_specs=out_spe...]
where the time goes in v3:
time: 478 us; the launch traced here: 469 us
  Pallas kernels  452 us (95%)
  local copies, waits for them, and re-layouts  16.1 us (3%)
    pallas_call x3, Pallas kernels, call(): pl.pallas_call(body, out_shape=outs, in_specs=in_specs, out_specs=out_spe...  452 us
    unnamed x18, local copies, waits for them, and re-layouts  11.1 us

profile of v3, /device:TPU:0, one launch (start us, length us, event | category | flops | bytes accessed | tf_op | source)
XLA Modules:
  0.0 469.0 jit_solution(17370506293084043447)
XLA Ops:
  0.6 1.2 reshape.37.refs_3_
  1.9 2.0 copy.18
  3.9 2.0 copy.19
  5.8 210.2 %forward.1 = (bf16[2,4,128,1600]{3,2,1,0:T(8,128)(2,1)}, bf16[1600,768]{1,0:T(8,128)(2,1)}, bf16[3,2,64,2048]{3,2,1,0:T(8,128)(2,1)}, f32[2,64,2048]{2,1,0:T(8,1...) custom-call(bf16[128,1600]{1,0:T(8,128)(2,1)} %bitcast.4, ...), custom_call_target="tpu_custom_call" | custom-call | tf_op jit(solution)/shard_map/forward/pallas_call | solution.py:417
  216.0 116.6 %middle.1 = (bf16[128,1600]{1,0:T(8,128)(2,1)}, f32[128,1600]{1,0:T(8,128)}, bf16[2,16,64,128]{3,2,1,0:T(8,128)(2,1)}, f32[100,3200]{1,0:T(8,128)}, f32[400,800]...) custom-call(bf16[2,4,128,1600]{3,2,1,0:T(8,128)(2,1)} %get-tuple-element.34.refs_0_, ...), custom_call_target="tpu_custom_call" | custom-call | tf_op jit(solution)/shard_map/middle/pallas_call | solution.py:417
  332.6 0.0 copy-start.3
  332.6 124.9 %backward.1 = (f32[128,1600]{1,0:T(8,128)}, f32[100,2400]{1,0:T(8,128)}, f32[100,800]{1,0:T(8,128)}, f32[8,128]{1,0:T(8,128)}) custom-call(bf16[128,1600]{1,0:T(8,128)(2,1)} %bitcast.5, bf16[3,2,64,2048]{3,2,1,0:T(8,128)(2,1)} %get-tuple-element.43.refs_1_, f32[2,64,2048]{2,1,0:T(8,128)} %get-tuple-element.44.refs_2_, ...), custom_call_target="tpu_custom_call" | custom-call | tf_op jit(solution)/shard_map/backward/pallas_call | solution.py:417
  457.5 0.0 copy-start.2
  457.5 0.0 copy-start.4
  457.5 0.0 copy-start.1
  457.6 0.0 copy-done.3
  457.6 0.9 copy.20
  458.5 2.3 copy.21
  460.8 1.2 slice.9
  462.0 0.7 slice.11
  462.7 1.3 slice.10
  464.0 0.6 reshape.41
  464.6 0.0 copy-done.2
  464.6 0.0 copy-start
  464.6 1.0 copy.26
  465.6 0.0 copy-done.4
  465.6 0.7 copy.27
  466.3 0.0 copy-done.1
  466.3 1.1 copy.28
  467.4 0.0 copy-done
  467.4 1.1 copy.29
Async XLA Ops:
  332.6 124.9 %copy-start.3 = (bf16[128,1600]{1,0:T(8,128)(2,1)S(1)}, bf16[128,1600]{1,0:T(8,128)(2,1)}, u32[]{:S(2)}) copy-start(bf16[128,1600]{1,0:T(8,128)(2,1)} %get-tuple-element.42) | copy-start | bytes 1228804
  457.5 7.1 %copy-start.2 = (f32[100,2400]{1,0:T(8,128)S(1)}, f32[100,2400]{1,0:T(8,128)}, u32[]{:S(2)}) copy-start(f32[100,2400]{1,0:T(8,128)} %get-tuple-element.79) | copy-start | bytes 2880004
  457.5 8.0 %copy-start.4 = (f32[100,800]{1,0:T(8,128)S(1)}, f32[100,800]{1,0:T(8,128)}, u32[]{:S(2)}) copy-start(f32[100,800]{1,0:T(8,128)} %get-tuple-element.80) | copy-start | bytes 960004
  457.5 8.8 %copy-start.1 = (f32[100,3200]{1,0:T(8,128)S(1)}, f32[100,3200]{1,0:T(8,128)}, u32[]{:S(2)}) copy-start(f32[100,3200]{1,0:T(8,128)} %get-tuple-element.81) | copy-start | bytes 3840004
  464.6 2.8 copy-start

commit v4 on v3

--- a/solution.py
+++ b/solution.py
@@ -150,7 +150,7 @@
     pl.semaphore_wait(barrier, len(devices))
 
 
-def meet_all(env):
+def hail_all(env):
     barrier = pltpu.get_barrier_semaphore()
 
     def hail(i, carry):
@@ -159,7 +159,10 @@
         return carry
 
     lax.fori_loop(1, env.n_dev, hail, 0)
-    pl.semaphore_wait(barrier, env.n_dev - 1)
+
+
+def meet_all(env):
+    pl.semaphore_wait(pltpu.get_barrier_semaphore(), env.n_dev - 1)
 
 
 def tp_partners(env):
@@ -187,7 +190,7 @@
     return (3 if rows else 0) + have * ((1 << bits) - 1) + (have << bits if core else 0)
 
 
-def gather(env, src, buf, sems, bits, slot, core=False, rows=False):
+def gather(env, src, buf, sems, bits, slot, core=False, rows=False, half=None):
     c, s = env.c, env.s
     links = Links(sems)
 
@@ -216,6 +219,9 @@
                 levels[j + 1].append((masks + [bits[j]], forward))
             if core:
                 crossing.append(links.send(ref, place(masks), env.other()))
+            if half is not None:
+                there = half.at[slot(flips(c, masks, s))]
+                crossing.append(links.send(ref.at[1 - s], there, env.other()))
             yield
     for copy in crossing:
         copy.wait_recv()
@@ -232,7 +238,7 @@
     return [pltpu.VMEM((n,) + block, BF) for n in counts]
 
 
-def reduce(env, inp, out, parts, sems, bits, slot, core=False, rows=False, halves=False):
+def reduce(env, inp, out, parts, sems, bits, slot, core=False, rows=False, halves=False, own=None):
     c, s = env.c, env.s
     links = Links(sems)
     levels = [list(env.lay.tp_masks) if rows else [[]]]
@@ -244,7 +250,10 @@
         return inp.at[side, index] if core else inp.at[index]
 
     last = levels[-1]
-    now = [at(s, m) for m in last]
+    if own is None:
+        now = [at(s, m) for m in last]
+    else:
+        now = [own.at[slot(flips(c, m, s))] for m in last]
     copies = {}
     if core:
         stage = len(bits)
@@ -637,28 +646,34 @@
 
     def body(*refs):
         (x_r, gains_r, biases_r, fcb_r, qkv_r, fc_r, out_r, proj_r, dy_r) = refs[:9]
-        (h1_o, wq_o, heads_o, o_o, lse_o, ob_o, pj_o, x1_o, h2_o, fc_o, out_o, dy_o, shift_o, par_o) = refs[9:23]
+        (h1_o, wq_o, heads_o, o_o, pj_o, h2_o, fc_o, out_o, outx_o, dy_o, lse_o, ob_o, x1_o, shift_o, par_o) = refs[9:24]
         (
-            pack, small, qkv_x, fc_x, out_x, qkv_s, fc_s, out_s, wq_b, h1_s, par_w,
-            parts, mine, keys, o_low, ob_b, proj_b, h2_s,
-        ) = refs[23:41]
-        sems = refs[41:]
+            pack, small, qkv_x, fc_x, qkv_s, fc_s, out_s, wq_b, wq_v, x_v, h1_v, par_w,
+            parts, mine, keys, heads_v, o_v, o_low, ob_b, proj_b, pj_v, h2_s,
+        ) = refs[24:46]
+        sems = refs[46:]
         groups = [sems[3 * i : 3 * i + 3] for i in range(len(sems) // 3)]
         env = Env(lay)
         s = env.s
 
+        hail_all(env)
         pack[...] = jnp.zeros_like(pack)
         pack[0:1, :R] = gains_r[...].astype(F32)
         pack[1:4, :R] = biases_r[...].astype(F32)
         pack[4:6, : FH // 2] = fcb_r[...].astype(F32)
+        for h in range(2):
+            out_s[h] = out_r[h * FH : (h + 1) * FH, :]
+        par_w[...] = jnp.zeros_like(par_w)
         meet_all(env)
         links = Links(groups[0])
-        crossing = [
-            links.send(a, b, env.other()) for a, b in ((qkv_r, qkv_x), (fc_r, fc_x), (out_r, out_x))
-        ]
+        crossing = [links.send(a, b, env.other()) for a, b in ((qkv_r, qkv_x), (fc_r, fc_x))]
+        rows_x = gather(env, x_r, x_v, groups[3], lay.tp_order, lay.tp_index, core=True)
+        next(rows_x)
         everyone = to_everyone(env, pack, small, groups[1], True)
         next(everyone)
-        hat, _ = norm_stats(x_r[...].astype(F32))
+        bg = Background()
+        bg.add(gather(env, out_s, out_o, groups[8], lay.dp_order, lay.dp_index, half=outx_o))
+        bg.step()
 
         def fill_qkv(a, b, side):
             q = a[:, :D]
@@ -673,55 +688,51 @@
                     if width > 0:
                         qkv_s[u, :, n * W : n * W + width] = part[:, first : first + width]
 
-        def fill_rest(a, b, oa, ob, side):
+        def fill_fc(a, b, side):
             for u in range(4):
                 for d in range(n_dp):
                     first = lay.compose(u, d) * FB + side * FH
                     source, first = (a, first) if first < FF // 2 else (b, first - FF // 2)
                     fc_s[u, :, d * FH : (d + 1) * FH] = source[:, first : first + FH]
-            out_s[:, :half] = oa[side * FH : (side + 1) * FH, :]
-            out_s[:, half:] = ob[side * FH : (side + 1) * FH, :]
-
-        def by_side(f, own, other):
-            @pl.when(s == 0)
-            def _():
-                f(*own_other(own, other), 0)
-
-            @pl.when(s == 1)
-            def _():
-                f(*own_other(other, own), 1)
-
-        def own_other(first, second):
-            return [r for pair in zip(first, second) for r in pair]
 
         crossing[0].wait_recv()
-        by_side(fill_qkv, (qkv_r,), (qkv_x,))
+        by_side(s, lambda side: fill_qkv(*((qkv_r, qkv_x) if side == 0 else (qkv_x, qkv_r)), side))
         weights = gather(env, qkv_s, wq_b, groups[2], lay.dp_order, natural, rows=True)
         next(weights)
+        crossing[1].wait_recv()
+        by_side(s, lambda side: fill_fc(*((fc_r, fc_x) if side == 0 else (fc_x, fc_r)), side))
         finish(everyone)
         for f in range(2):
             rows = jnp.concatenate([small[2 * c + f][:, :R] for c in range(n_ctx)], axis=1)
             par_o[f] = rows
-        par_w[...] = jnp.zeros_like(par_w)
         par_w[:, :D] = par_o[0]
-        h1_s[...] = (hat * par_o[0, 0:1, :] + par_o[0, 1:2, :]).astype(BF)
-        rows_h1 = gather(env, h1_s, h1_o, groups[3], lay.tp_order, lay.tp_index, core=True)
-        next(rows_h1)
         shift_parts = []
         for d in range(n_dp):
             block = small[lay.compose(env.t, d) * 2 + s]
             shift_parts += [block[4:5, : FH // 2], block[5:6, : FH // 2]]
         shift_o[...] = jnp.concatenate(shift_parts, axis=1)
-        run([weights, rows_h1])
-        crossing[1].wait_recv()
-        crossing[2].wait_recv()
-        by_side(fill_rest, (fc_r, out_r), (fc_x, out_x))
-        bg = Background()
-        bg.add(gather(env, dy_r, dy_o, groups[4], lay.tp_order, lay.tp_index, core=True))
+        steps(weights, 3)
+        bg.step()
+        steps(rows_x, 1)
+        steps(weights, 4)
+        bg.step(2)
+        finish(rows_x)
+        proj = gather(env, proj_r, proj_b, groups[7], lay.tp_order + lay.dp_order, natural, core=True)
+        next(proj)
         bg.add(gather(env, fc_s, fc_o, groups[5], lay.dp_order, natural, rows=True))
         bg.step(2)
+
+        @pl.loop(0, 8)
+        def _(i):
+            hat, _ = norm_stats(x_v[i // 4, i % 4].astype(F32))
+            h1_v[i // 4, i % 4] = (hat * par_o[0, 0:1, :] + par_o[0, 1:2, :]).astype(BF)
+
+        finish(weights)
         for c in range(n_ctx):
-            wq_o[c * R : (c + 1) * R, :] = wq_b[c]
+            wq_v[c * R : (c + 1) * R, :] = wq_b[c]
+        leave = Links((None, None, groups[11][2]))
+        leave.local(h1_v, h1_o)
+        leave.local(wq_v, wq_o)
         unit = 2 * env.t + s
         cols = pl.ds(pl.multiple_of(unit * W, W), W)
         shift = jnp.concatenate(
@@ -729,8 +740,8 @@
         )
         moving = []
         for q in range(2):
-            rows = h1_o[q].reshape(G, D)
-            made = (dot(rows, wq_o[...], NN) + shift).astype(BF).T
+            rows = h1_v[q].reshape(G, D)
+            made = (dot(rows, wq_v[...], NN) + shift).astype(BF).T
             for n in range(3):
                 for j in range(HU):
                     first = n * W + j * HEAD_DIM
@@ -738,45 +749,57 @@
             g = group_to_heads(env, parts, mine, groups[6], q)
             next(g)
             moving.append(g)
-        bg.add(gather(env, proj_r, proj_b, groups[7], lay.tp_order + lay.dp_order, natural, core=True))
-        bg.add(gather(env, out_s, out_o, groups[8], lay.dp_order, lay.dp_index))
+        steps(proj, 1)
         bg.step(4)
+        bg.add(gather(env, dy_r, dy_o, groups[4], lay.tp_order, lay.tp_index, core=True))
         leaving = []
         for q in range(2):
             next(moving[q])
             for c in range(n_ctx):
                 tc, dc = lay.tp_index(c), lay.dp_index(c)
                 for n in range(3):
-                    heads_o[n, q, :, c * T : (c + 1) * T] = mine[
+                    heads_v[n, q, :, c * T : (c + 1) * T] = mine[
                         q, dc, n * HEAD_DIM : (n + 1) * HEAD_DIM, tc * T : (tc + 1) * T
                     ]
-            keys[...] = heads_o[1, q].T
+            keys[...] = heads_v[1, q].T
             for i in range(n_tiles):
                 at = slice(i * tile, (i + 1) * tile)
-                o, lse = attend_tile(i, tile, heads_o[0, q, :, at], keys, heads_o.at[2, q])
-                o_o[q, :, at] = o
+                o, lse = attend_tile(i, tile, heads_v[0, q, :, at], keys, heads_v.at[2, q])
+                o_v[q, :, at] = o
                 lse_o[q, :, at] = lse
                 low = o.astype(BF)
                 for b in range(tile // T):
                     o_low[q, i * (tile // T) + b] = low[:, b * T : (b + 1) * T]
-                bg.step(3)
+                steps(proj, 2)
+                bg.step(2)
             g = heads_out(env, o_low, ob_b, groups[9], q)
             next(g)
             leaving.append(g)
-        bg.finish()
-        for g in moving + leaving:
-            finish(g)
+        leave.local(heads_v, heads_o)
+        leave.local(o_v, o_o)
+        finish(proj)
         for n in range(2):
             for c in range(n_ctx):
-                pj_o[n, c * R : (c + 1) * R, :] = proj_b[n, c]
+                pj_v[n, c * R : (c + 1) * R, :] = proj_b[n, c]
+        leave.local(pj_v, pj_o)
+        for g in leaving:
+            finish(g)
         heads_in(env, o_low, ob_b, groups[9])
         ob_o[...] = ob_b[...].reshape(D, T).T
-        branch = jnp.concatenate([dot(ob_o[...], pj_o[n], NN) for n in range(2)], axis=1)
+        branch = jnp.concatenate([dot(ob_o[...], pj_v[n], NN) for n in range(2)], axis=1)
         x1 = x_r[...].astype(F32) + branch + par_o[1, 1:2, :]
         x1_o[...] = x1
         hat, _ = norm_stats(x1)
         h2_s[...] = (hat * par_o[1, 0:1, :] + par_o[1, 2:3, :]).astype(BF)
-        finish(gather(env, h2_s, h2_o, groups[10], lay.tp_order, lay.tp_index, core=True))
+        rows_h2 = gather(env, h2_s, h2_o, groups[10], lay.tp_order, lay.tp_index, core=True)
+        next(rows_h2)
+        bg.step(4)
+        next(rows_h2)
+        bg.finish()
+        finish(rows_h2)
+        for g in moving:
+            finish(g)
+        leave.finish()
         links.finish()
 
     outs = [
@@ -784,56 +807,63 @@
         struct(D, 3 * W),
         struct(3, 2, HEAD_DIM, length),
         struct(2, HEAD_DIM, length, dtype=F32),
+        struct(2, D, half),
+        struct(2, 4, T, D),
+        struct(n_ctx, R, n_dp * FH),
+        struct(n_dp, 2, FH, half),
+        struct(n_dp, FH, half),
+        struct(2, 4, T, D),
         struct(2, 1, length, dtype=F32),
         struct(T, D),
-        struct(2, D, half),
         struct(T, D, dtype=F32),
-        struct(2, 4, T, D),
-        struct(n_ctx, R, n_dp * FH),
-        struct(n_dp, FH, D),
-        struct(2, 4, T, D),
         struct(1, n_dp * FH, dtype=F32),
         struct(2, 8, D, dtype=F32),
     ]
-    out_specs = [VM] * 8 + [ANY] * 4 + [VM] * 2
+    out_specs = [ANY] * 10 + [VM] * 5
     scratch = [
         pltpu.VMEM((8, 128), F32),
         pltpu.VMEM((n_dev, 8, 128), F32),
         pltpu.VMEM(qkv.shape, BF),
         pltpu.VMEM(fc.shape, BF),
-        pltpu.VMEM(out.shape, BF),
         pltpu.VMEM((4, R, 3 * W), BF),
         pltpu.VMEM((4, R, n_dp * FH), BF),
-        pltpu.VMEM((FH, D), BF),
+        pltpu.VMEM((2, FH, half), BF),
         pltpu.VMEM((n_ctx, R, 3 * W), BF),
-        pltpu.VMEM((T, D), BF),
+        pltpu.VMEM((D, 3 * W), BF),
+        pltpu.VMEM((2, 4, T, D), BF),
+        pltpu.VMEM((2, 4, T, D), BF),
         pltpu.VMEM((8, wide), F32),
         pltpu.VMEM((2, HU, QKV, G), BF),
         pltpu.VMEM((2, n_dp, QKV, G), BF),
         pltpu.VMEM((length, HEAD_DIM), BF),
+        pltpu.VMEM((3, 2, HEAD_DIM, length), BF),
+        pltpu.VMEM((2, HEAD_DIM, length), F32),
         pltpu.VMEM((2, n_ctx, HEAD_DIM, T), BF),
         pltpu.VMEM((HEADS, HEAD_DIM, T), BF),
         pltpu.VMEM((2, n_ctx, R, half), BF),
+        pltpu.VMEM((2, D, half), BF),
         pltpu.VMEM((T, D), BF),
     ]
     DMA = pltpu.SemaphoreType.DMA
-    scratch += sem_shapes(3) + sem_shapes(n_dev)
+    scratch += sem_shapes(2) + sem_shapes(n_dev)
     scratch += sem_shapes(gather_sends(4, k, False, True))
     scratch += sem_shapes(gather_sends(1, 2, True, False)) * 2
     scratch += sem_shapes(gather_sends(4, k, False, True))
     scratch += [DMA((2, HU)), DMA((2, n_dp)), DMA((2,))]
     scratch += sem_shapes(gather_sends(1, k + 2, True, False))
-    scratch += sem_shapes(gather_sends(1, k, False, False))
+    scratch += sem_shapes(gather_sends(1, k, True, False))
     scratch += [DMA((2, n_ctx)), DMA((HEADS,)), DMA((2,))]
     scratch += sem_shapes(gather_sends(1, 2, True, False))
+    scratch += sem_shapes(1, 5)
+    in_specs = [VM] * 7 + [ANY] * 2
     return call(
-        "forward", 0, body, (x, gains, biases, fc_bias, qkv, fc, out, proj, dy), [VM] * 9, outs, out_specs, scratch
+        "forward", 0, body, (x, gains, biases, fc_bias, qkv, fc, out, proj, dy), in_specs, outs, out_specs, scratch
     )
 
 
-def drive(generator, background):
-    for _ in generator:
-        background.step()
+def steps(generator, count):
+    for _ in range(count):
+        next(generator, None)
 
 
 def by_side(s, f):
@@ -844,7 +874,7 @@
             f(side)
 
 
-def middle(lay, x, h2, dy_all, fc, out, shift, x1, dy, pj, par):
+def middle(lay, x, h2, dy_all, fc, out, out_x, shift, x1, dy, pj, par):
     n_ctx, n_dp = lay.n_ctx, lay.n_dp
     n_dev = 2 * n_ctx
     k = len(lay.dp_bits)
@@ -860,44 +890,40 @@
         return c
 
     def body(*refs):
-        (h2_r, dya_r, fc_r, out_r, pj_r, shift_r, x1_r, dy_r, par_r) = refs[:9]
-        (mixed_o, dx1_o, dob_o, fc_o, out_o, vec_o, fcb_o) = refs[9:16]
-        (
-            h2_v, dy_v, fc_b, fc_w, out_b, out_w, pj_v, gb_v, du_v, back_p, dh2_v, mix_v, dob_s, fc_v, out_v,
-        ) = refs[16:31]
-        rest = refs[31:]
-        plan = [
-            (0, 3, 3),
-            (1, 3, 3),
-            (2, k, 3),
-            (3, k, 3),
-        ]
+        (h2_r, dya_r, fc_r, out_r, outx_r, pj_r, shift_r, x1_r, dy_r, par_r) = refs[:10]
+        (mix_o, dob_o, fc_o, out_o, dx1_o, vec_o, fcb_o) = refs[10:17]
+        (h2_v, dy_v, fc_b, fc_w, out_b, out_w, out_g, pj_v, gb_v, du_v, back_p, dh2_v, dob_s) = refs[17:30]
+        rest = refs[30:]
         spans, first = [], 0
-        for _, n, m in plan:
-            spans.append((rest[first : first + n], rest[first + n : first + n + m]))
-            first += n + m
+        for n in (3, k, k):
+            spans.append((rest[first : first + n], rest[first + n : first + n + 3]))
+            first += n + 3
         sems = rest[first:]
         env = Env(lay)
         s = env.s
+        hail_all(env)
         loads = Links((None, None, sems[3]))
-        load = {}
-        for name, a, b in (
-            ("h2", h2_r, h2_v),
-            ("fc", fc_r, fc_b),
-            ("dy", dya_r, dy_v),
-            ("out", out_r, out_b),
-            ("pj", pj_r, pj_v),
-        ):
-            load[name] = loads.local(a, b)
-        meet_all(env)
-        load["fc"].wait()
+        load_fc = loads.local(fc_r, fc_b)
+        load_h2 = loads.local(h2_r, h2_v)
+        load_out = [loads.local(out_r.at[d, s], out_b.at[0, d]) for d in range(n_dp)]
+        load_out += [loads.local(outx_r.at[d], out_b.at[1, d]) for d in range(n_dp)]
+        load_dy = loads.local(dya_r, dy_v)
+        load_pj = loads.local(pj_r, pj_v)
+        load_fc.wait()
         for c in range(n_ctx):
             fc_w[c * R : (c + 1) * R, :] = fc_b[c]
-        load["out"].wait()
-        for d in range(n_dp):
-            out_w[d * FH : (d + 1) * FH, :] = out_b[d]
-        load["h2"].wait()
-        load["dy"].wait()
+        for copy in load_out:
+            copy.wait()
+
+        def fill_out(side):
+            for d in range(n_dp):
+                at = slice(d * FH, (d + 1) * FH)
+                pair = (out_b[0, d], out_b[1, d]) if side == 0 else (out_b[1, d], out_b[0, d])
+                out_w[at, :] = jnp.concatenate(pair, axis=1)
+
+        by_side(s, fill_out)
+        load_h2.wait()
+        load_dy.wait()
 
         def forth_and_back(q):
             @pl.loop(0, G // chunk)
@@ -919,34 +945,29 @@
                 back_p[q, pl.ds(2 * i, 2)] = back.reshape(2, T, D)
 
         forth_and_back(1 - s)
+        meet_all(env)
         rows = reduce(env, back_p, dh2_v, *spans[0], lay.tp_order, lay.tp_index, core=True)
         next(rows)
         forth_and_back(s)
-        next(rows)
-        bg = Background()
-        for d in range(n_dp):
-            left = gb_v[:, :, d * FH : (d + 1) * FH].reshape(2 * G, FH)
-            out_b[d] = dot(left, dy_v[...].reshape(2 * G, D), TN).astype(BF)
-        bg.add(reduce(env, out_b, out_v, *spans[3], lay.dp_order, lay.dp_index, halves=True))
-        bg.step()
-        next(rows)
+        steps(rows, 4)
         for c in range(0, n_ctx, 4):
             left = h2_v[:, :, :, c * R : (c + 4) * R].reshape(2 * G, 4 * R)
             made = dot(left, du_v[...].reshape(2 * G, U), TN).astype(BF)
             for i in range(4):
                 fc_b[c + i] = made[i * R : (i + 1) * R, :]
-        bg.add(reduce(env, fc_b, fc_v, *spans[2], lay.dp_order, natural, rows=True))
-        bg.step()
-        for _ in range(2):
-            next(rows)
+        fc_sum = reduce(env, fc_b, fc_o, *spans[1], lay.dp_order, natural, rows=True)
+        next(fc_sum)
+        for d in range(n_dp):
+            left = gb_v[:, :, d * FH : (d + 1) * FH].reshape(2 * G, FH)
+            out_g[d] = dot(left, dy_v[...].reshape(2 * G, D), TN).astype(BF)
+        out_sum = reduce(env, out_g, out_o, *spans[2], lay.dp_order, lay.dp_index, halves=True)
+        next(out_sum)
         fcb_o[...] = jnp.sum(du_v[...].reshape(2 * G, U).astype(F32), axis=0, keepdims=True)
         x1 = x1_r[...]
         hat, spread = norm_stats(x1)
         dy_own = dy_r[...].astype(F32)
         vec_o[...] = jnp.zeros_like(vec_o)
         vec_o[3:4, :] = jnp.sum(dy_own, axis=0, keepdims=True)
-        for _ in range(2):
-            next(rows)
         for q in range(2):
 
             @pl.loop(0, G // chunk)
@@ -955,6 +976,9 @@
                 part = dot(gb_v[q, at, :], out_w[...], NN).astype(BF)
                 h2_v[q, pl.ds(2 * i, 2)] = part.reshape(2, T, D)
 
+        leave = loads.local(h2_v, mix_o)
+        steps(rows, 2)
+        steps(fc_sum, 8)
         finish(rows)
         dh2 = dh2_v[...].astype(F32)
         scaled = dh2 * par_r[1, 0:1, :]
@@ -965,40 +989,26 @@
         )
         dx1_o[...] = dx1
         da = dx1.astype(BF)
-        load["pj"].wait()
+        load_pj.wait()
         dob = dot(da[:, :half], pj_v[0], NT) + dot(da[:, half:], pj_v[1], NT)
         dob_s[...] = dob.astype(BF).T.reshape(HEADS, HEAD_DIM, T)
         heads = tokens_to_heads(env, dob_s, dob_o, sems[0:3])
         next(heads)
-        mixing = reduce(env, h2_v, mix_v, *spans[1], lay.tp_order, lay.tp_index, core=True)
-        next(mixing)
-        bg.add(mixing)
         vec_o[0:1, :] = jnp.sum(dh2 * hat, axis=0, keepdims=True)
         vec_o[1:2, :] = jnp.sum(da.astype(F32), axis=0, keepdims=True)
         vec_o[2:3, :] = jnp.sum(dh2, axis=0, keepdims=True)
-        bg.finish()
+        steps(fc_sum, 4)
+        steps(out_sum, 2)
+        run([fc_sum, out_sum])
         finish(heads)
-        mixed_o[...] = (x1 + mix_v[...].astype(F32) + par_r[1, 3:4, :]).astype(BF)
-
-        def last(side):
-            pieces = []
-            for c in range(n_ctx // 2 * side, n_ctx // 2 * (side + 1)):
-                for h in range(2):
-                    first = lay.dp_index(c) * FH
-                    pieces.append(fc_v[h, lay.tp_index(c)][:, first : first + FH])
-            fc_o[...] = jnp.concatenate(pieces, axis=1).astype(F32)
-            out_o[...] = jnp.concatenate(
-                [out_v[h][:, side * half : (side + 1) * half] for h in range(2)], axis=0
-            ).astype(F32)
-
-        by_side(s, last)
+        leave.wait()
 
     outs = [
-        struct(T, D),
+        struct(2, 4, T, D),
+        struct(2, n_ctx, HEAD_DIM, T),
+        struct(2, 4, R, U),
+        struct(2, FH, D),
         struct(T, D, dtype=F32),
-        struct(2, n_ctx, HEAD_DIM, T),
-        struct(R, FF // 2, dtype=F32),
-        struct(FB, half, dtype=F32),
         struct(8, D, dtype=F32),
         struct(1, U, dtype=F32),
     ]
@@ -1007,36 +1017,34 @@
         pltpu.VMEM((2, 4, T, D), BF),
         pltpu.VMEM((n_ctx, R, U), BF),
         pltpu.VMEM((D, U), BF),
+        pltpu.VMEM((2, n_dp, FH, half), BF),
+        pltpu.VMEM((U, D), BF),
         pltpu.VMEM((n_dp, FH, D), BF),
-        pltpu.VMEM((U, D), BF),
         pltpu.VMEM((2, D, half), BF),
         pltpu.VMEM((2, G, U), BF),
         pltpu.VMEM((2, G, U), BF),
         pltpu.VMEM((2, 4, T, D), BF),
         pltpu.VMEM((T, D), BF),
-        pltpu.VMEM((T, D), BF),
         pltpu.VMEM((HEADS, HEAD_DIM, T), BF),
-        pltpu.VMEM((2, 4, R, U), BF),
-        pltpu.VMEM((2, FH, D), BF),
     ]
-    for _ in range(2):
-        scratch += reduce_scratch(1, 2, True, (T, D)) + sem_shapes(reduce_sends(1, 2, True, False, False))
+    scratch += reduce_scratch(1, 2, True, (T, D)) + sem_shapes(reduce_sends(1, 2, True, False, False))
     scratch += reduce_scratch(4, k, False, (R, U)) + sem_shapes(reduce_sends(4, k, False, True, False))
     scratch += reduce_scratch(1, k, False, (FH, D)) + sem_shapes(reduce_sends(1, k, False, False, True))
     DMA = pltpu.SemaphoreType.DMA
-    scratch += [DMA((HEADS,)), DMA((n_dev,)), DMA((1,)), DMA((5,))]
-    args = (h2, dy_all, fc, out, pj, shift, x1, dy, par)
-    out_specs = [VM] * 2 + [ANY] + [VM] * 4
-    return call("middle", 1, body, args, [ANY] * 5 + [VM] * 4, outs, out_specs, scratch)
+    scratch += [DMA((HEADS,)), DMA((n_dev,)), DMA((1,)), DMA((2 * n_dp + 5,))]
+    args = (h2, dy_all, fc, out, out_x, pj, shift, x1, dy, par)
+    out_specs = [ANY] * 4 + [VM] * 3
+    return call("middle", 1, body, args, [ANY] * 6 + [VM] * 4, outs, out_specs, scratch)
 
 
 def heads_to_group(env, src, out, sems, q):
     send_sems, recv_sems, local_sems = sems
     lay = env.lay
+    held = q % src.shape[0]
 
     def copy(there, j, target):
         return pltpu.make_async_remote_copy(
-            src_ref=src.at[q, there],
+            src_ref=src.at[held, there],
             dst_ref=out.at[q, j],
             send_sem=send_sems.at[q, there],
             recv_sem=recv_sems.at[q, j],
@@ -1044,7 +1052,7 @@
             device_id_type=MESH,
         )
 
-    local = pltpu.make_async_copy(src.at[q, env.d], out.at[q, env.d % HU], local_sems.at[q])
+    local = pltpu.make_async_copy(src.at[held, env.d], out.at[q, env.d % HU], local_sems.at[q])
 
     @pl.when(env.d < HU)
     def _():
@@ -1074,7 +1082,7 @@
             copy(there, env.d, there).wait_send()
 
 
-def backward(lay, x, heads, o, lse, dob, wq, h1, ob, vec, fcb, dx1, par):
+def backward(lay, x, heads, o, lse, dob, wq, h1, ob, vec, fcb, dx1, par, mix):
     n_ctx, n_dp = lay.n_ctx, lay.n_dp
     n_dev = 2 * n_ctx
     k = len(lay.dp_bits)
@@ -1093,32 +1101,40 @@
         return c
 
     def body(*refs):
-        (x_r, heads_r, o_r, lse_r, dob_r, wq_r, h1_r, ob_r, vec_r, fcb_r, dx1_r, par_r) = refs[:12]
-        (grad_o, qkv_o, proj_o, small_o) = refs[12:16]
+        (x_r, heads_r, o_r, lse_r, dob_r, wqh_r, h1h_r, ob_r, vec_r, fcb_r, dx1_r, par_r, mix_r) = refs[:13]
+        (grad_o, q_v, proj_o, small_o, mix_s) = refs[13:18]
         (
-            heads_v, o_v, dob_n, qs, dobs, delta, dq_acc, parts, land, dqkv, dh1_p, dh1_v, q_g, q_v, wide_v,
-            small_s, small_v, pg,
-        ) = refs[16:34]
-        rest = refs[34:]
+            heads_v, o_v, dob_n, qs, dobs, delta, dq_acc, parts, land, dqkv, dh1_p, dh1_v, q_g, wide_v,
+            small_s, small_v, pg, wq_r, h1_r,
+        ) = refs[18:37]
+        rest = refs[37:]
         spans, first = [], 0
-        for n in (3, k, k + 3):
+        for n in (3, k, k + 3, 3):
             spans.append((rest[first : first + n], rest[first + n : first + n + 3]))
             first += n + 3
         sems = rest[first:]
         env = Env(lay)
         s = env.s
-        meet_all(env)
-        bg = Background()
+        hail_all(env)
+        early = Links((None, None, sems[7]))
+        mix_v = dh1_p.at[0]
+        load_mix = early.local(mix_r.at[s], mix_v)
+        load_wq = early.local(wqh_r, wq_r)
+        load_h1 = early.local(h1h_r, h1_r)
         for n in range(2):
             right = dx1_r[:, n * half : (n + 1) * half].astype(BF)
             for c in range(0, n_ctx, 4):
                 made = dot(ob_r[:, c * R : (c + 4) * R], right, TN).astype(BF)
                 for i in range(4):
                     pg[n, c + i] = made[i * R : (i + 1) * R, :]
-        bg.add(reduce(env, pg, proj_o, *spans[2], lay.tp_order + lay.dp_order, natural, core=True))
-        bg.step()
         small_s[...] = jnp.zeros_like(small_s)
         wide_v[...] = jnp.zeros_like(wide_v)
+        meet_all(env)
+        proj = reduce(env, pg, proj_o, *spans[2], lay.tp_order + lay.dp_order, natural, core=True)
+        next(proj)
+        mixing = reduce(env, mix_r, mix_s, *spans[3], lay.tp_order, lay.tp_index, core=True, own=mix_v)
+        next(mixing)
+        load_mix.wait()
         moving = []
         _, active = own_head(env)
 
@@ -1148,11 +1164,14 @@
             delta[...] = jnp.sum(dob_n[...].astype(F32) * o_v[...], axis=0, keepdims=True)
             dq_acc[...] = jnp.zeros_like(dq_acc)
 
+            if q == 1 and parts.shape[0] == 1:
+                finish(moving[0])
+
             def put(n, first, block):
                 for b in range(block.shape[1] // T):
                     c = first // T + b
                     tc, dc = lay.tp_index(c), lay.dp_index(c)
-                    parts[q, dc, n * HEAD_DIM : (n + 1) * HEAD_DIM, tc * T : (tc + 1) * T] = block[
+                    parts[q % parts.shape[0], dc, n * HEAD_DIM : (n + 1) * HEAD_DIM, tc * T : (tc + 1) * T] = block[
                         :, b * T : (b + 1) * T
                     ]
 
@@ -1184,7 +1203,12 @@
                     carry = lax.fori_loop(j + 1, n_tiles, functools.partial(step, masked=False), carry)
                 put(1, j * tile, (carry[0] * SCALE).T.astype(BF))
                 put(2, j * tile, carry[1].T.astype(BF))
-                bg.step(4)
+                if q == 0:
+                    steps(proj, n_ctx // n_tiles)
+                    steps(mixing, 1)
+                else:
+                    steps(proj, n_ctx // 2 // n_tiles)
+                    steps(mixing, 1)
             put(0, 0, (dq_acc[...] * SCALE).astype(BF))
             if q == 0:
                 for copy in loads(1):
@@ -1192,8 +1216,10 @@
             g = heads_to_group(env, parts, land, sems[0:3], q)
             next(g)
             moving.append(g)
+        load_wq.wait()
+        load_h1.wait()
         for q in range(2):
-            next(moving[q])
+            next(moving[q], None)
             rows = []
             for n in range(3):
                 for j in range(HU):
@@ -1209,7 +1235,7 @@
                 q_g[c + i] = made[i * R : (i + 1) * R, :]
         grads = reduce(env, q_g, q_v, *spans[1], lay.dp_order, natural, rows=True)
         next(grads)
-        bg.add(grads)
+        steps(rows_h1, 4)
         unit = 2 * env.t + s
         sums = jnp.sum(dqkv[0].astype(F32), axis=0, keepdims=True) + jnp.sum(
             dqkv[1].astype(F32), axis=0, keepdims=True
@@ -1218,7 +1244,12 @@
         wide_v[2:3, cols] = sums[:, :W]
         wide_v[3:4, cols] = sums[:, 2 * W :]
         hat, spread = norm_stats(x_r[...].astype(F32))
-        drive(rows_h1, bg)
+        finish(mixing)
+        steps(proj, n_ctx // 4)
+        steps(grads, n_ctx // 2)
+        steps(rows_h1, 2)
+        steps(grads, n_ctx // 4)
+        finish(rows_h1)
         dh1 = dh1_v[...].astype(F32)
         scaled = dh1 * par_r[0, 0:1, :]
         grad_o[...] = dx1_r[...] + spread * (
@@ -1238,19 +1269,10 @@
                 small_s[owner, 4 + h : 5 + h, : FH // 2] = fcb_r[:, first : first + FH // 2]
         everyone = to_everyone(env, small_s, small_v, sems[3:6], False)
         next(everyone)
-        bg.finish()
+        finish(grads)
+        finish(proj)
         for g in moving:
             finish(g)
-
-        def last(side):
-            parts_all = []
-            for n in range(3):
-                pieces = [q_v[h, u][:, n * W : (n + 1) * W] for u in range(4) for h in range(2)]
-                parts_all.append(jnp.concatenate(pieces, axis=1)[:, :D])
-            whole = jnp.concatenate(parts_all, axis=1)
-            qkv_o[...] = whole[:, side * (3 * half) : (side + 1) * (3 * half)].astype(F32)
-
-        by_side(s, last)
         finish(everyone)
         total = small_v[0]
         for r in range(1, n_dev):
@@ -1259,9 +1281,10 @@
 
     outs = [
         struct(T, D, dtype=F32),
-        struct(R, 3 * half, dtype=F32),
-        struct(R, half, dtype=F32),
+        struct(2, 4, R, 3 * W),
+        struct(R, half),
         struct(8, 128, dtype=F32),
+        struct(T, D),
     ]
     scratch = [
         pltpu.VMEM((3, HEAD_DIM, length), BF),
@@ -1271,28 +1294,88 @@
         pltpu.VMEM((length, HEAD_DIM), BF),
         pltpu.VMEM((1, length), F32),
         pltpu.VMEM((HEAD_DIM, length), F32),
-        pltpu.VMEM((2, n_dp, QKV, G), BF),
+        pltpu.VMEM((2 if n_ctx <= 16 else 1, n_dp, QKV, G), BF),
         pltpu.VMEM((2, HU, QKV, G), BF),
         pltpu.VMEM((2, G, 3 * W), BF),
         pltpu.VMEM((2, 4, T, D), BF),
         pltpu.VMEM((T, D), BF),
         pltpu.VMEM((n_ctx, R, 3 * W), BF),
-        pltpu.VMEM((2, 4, R, 3 * W), BF),
         pltpu.VMEM((8, wide), F32),
         pltpu.VMEM((n_dev, 8, 128), F32),
         pltpu.VMEM((n_dev, 8, 128), F32),
         pltpu.VMEM((2, n_ctx, R, half), BF),
+        pltpu.VMEM((D, 3 * W), BF),
+        pltpu.VMEM((2, 4, T, D), BF),
     ]
     scratch += reduce_scratch(1, 2, True, (T, D)) + sem_shapes(reduce_sends(1, 2, True, False, False))
     scratch += reduce_scratch(4, k, False, (R, 3 * W)) + sem_shapes(reduce_sends(4, k, False, True, False))
     scratch += reduce_scratch(1, k + 2, True, (R, half)) + sem_shapes(
         reduce_sends(1, k + 2, True, False, False)
     )
+    scratch += reduce_scratch(1, 2, True, (T, D)) + sem_shapes(reduce_sends(1, 2, True, False, False))
     DMA = pltpu.SemaphoreType.DMA
-    scratch += [DMA((2, n_dp)), DMA((2, HU)), DMA((2,))] + sem_shapes(n_dev) + [DMA((4 + n_ctx,))]
-    args = (x, heads, o, lse, dob, wq, h1, ob, vec, fcb, dx1, par)
-    in_specs = [VM, ANY, ANY, VM, ANY] + [VM] * 7
-    return call("backward", 2, body, args, in_specs, outs, [VM] * 4, scratch)
+    scratch += [DMA((2, n_dp)), DMA((2, HU)), DMA((2,))] + sem_shapes(n_dev) + [DMA((4 + n_ctx,)), DMA((3,))]
+    args = (x, heads, o, lse, dob, wq, h1, ob, vec, fcb, dx1, par, mix)
+    in_specs = [VM, ANY, ANY, VM, ANY, ANY, ANY] + [VM] * 5 + [ANY]
+    return call("backward", 2, body, args, in_specs, outs, [VM, ANY, VM, VM, VM], scratch)
+
+
+def assemble(lay, q, fc, out, proj, grad, mix, x1, par, small):
+    n_ctx, n_dp = lay.n_ctx, lay.n_dp
+    T = grad.shape[0]
+    R, FB = D // n_ctx, FF // n_ctx
+    FH = FB // 2
+    W = HU * HEAD_DIM
+    half = D // 2
+
+    def body(*refs):
+        (q_r, fc_r, out_r, proj_r, grad_r, mix_r, x1_r, par_r, small_r) = refs[:9]
+        (mixed_o, grad_o, qkv_o, proj_o, fc_o, out_o, gains_o, biases_o, fcb_o) = refs[9:]
+        mixed_o[...] = (x1_r[...] + mix_r[...].astype(F32) + par_r[1, 3:4, :]).astype(BF)
+        grad_o[...] = grad_r[...]
+        proj_o[...] = proj_r[...].astype(F32)
+        gains_o[...] = small_r[0:1, :R]
+        biases_o[...] = small_r[1:4, :R]
+        fcb_o[...] = small_r[4:6, : FH // 2]
+
+        def last(side):
+            thirds = []
+            for n in range(3):
+                pieces = [q_r[h, u][:, n * W : (n + 1) * W] for u in range(4) for h in range(2)]
+                thirds.append(jnp.concatenate(pieces, axis=1)[:, :D])
+            whole = jnp.concatenate(thirds, axis=1)
+            qkv_o[...] = whole[:, side * (3 * half) : (side + 1) * (3 * half)].astype(F32)
+            pieces = []
+            for c in range(n_ctx // 2 * side, n_ctx // 2 * (side + 1)):
+                for h in range(2):
+                    first = lay.dp_index(c) * FH
+                    pieces.append(fc_r[h, lay.tp_index(c)][:, first : first + FH])
+            fc_o[...] = jnp.concatenate(pieces, axis=1).astype(F32)
+            out_o[...] = jnp.concatenate(
+                [out_r[h][:, side * half : (side + 1) * half] for h in range(2)], axis=0
+            ).astype(F32)
+
+        by_side(lax.axis_index("fsdp"), last)
+
+    outs = [
+        struct(T, D),
+        struct(T, D, dtype=F32),
+        struct(R, 3 * half, dtype=F32),
+        struct(R, half, dtype=F32),
+        struct(R, FF // 2, dtype=F32),
+        struct(FB, half, dtype=F32),
+        struct(1, R, dtype=F32),
+        struct(3, R, dtype=F32),
+        struct(2, FH // 2, dtype=F32),
+    ]
+    return pl.pallas_call(
+        body,
+        out_shape=outs,
+        in_specs=[VM] * 9,
+        out_specs=[VM] * 9,
+        compiler_params=pltpu.CompilerParams(vmem_limit_bytes=VMEM_LIMIT),
+        name="assemble",
+    )(q, fc, out, proj, grad, mix, x1, par, small)
 
 
 def shards(lay, tokens, qkv_weight, proj_weight, fc_weight, out_weight, gains, biases, fc_bias, cotangent):
@@ -1301,23 +1384,28 @@
     FH = FF // lay.n_ctx // 2
     x = tokens.reshape(T, D)
     dy = cotangent.reshape(T, D)
-    (h1, wq, heads, o, lse, ob, pj, x1, h2, fc, out, dy_all, shift, par) = forward(
+    (h1, wq, heads, o, pj, h2, fc, out, out_x, dy_all, lse, ob, x1, shift, par) = forward(
         lay, x, gains, biases, fc_bias.reshape(2, FH // 2), qkv_weight, fc_weight, out_weight, proj_weight, dy
     )
-    mixed, dx1, dob, fc_grad, out_grad, vec, fcb = middle(
-        lay, x, h2, dy_all, fc, out, shift, x1, dy, pj, par
+    mix, dob, fc_sum, out_sum, dx1, vec, fcb = middle(
+        lay, x, h2, dy_all, fc, out, out_x, shift, x1, dy, pj, par
     )
-    input_grad, qkv_grad, proj_grad, small = backward(lay, x, heads, o, lse, dob, wq, h1, ob, vec, fcb, dx1, par)
+    grad, q_sum, proj_sum, small, mix_sum = backward(
+        lay, x, heads, o, lse, dob, wq, h1, ob, vec, fcb, dx1, par, mix
+    )
+    (mixed, grad, qkv_grad, proj_grad, fc_grad, out_grad, gains_grad, biases_grad, fc_bias_grad) = assemble(
+        lay, q_sum, fc_sum, out_sum, proj_sum, grad, mix_sum, x1, par, small
+    )
     return (
         mixed.reshape(tokens.shape),
-        input_grad.reshape(tokens.shape),
+        grad.reshape(tokens.shape),
         qkv_grad,
         proj_grad,
         fc_grad,
         out_grad,
-        small[0:1, :R],
-        small[1:4, :R],
-        small[4:6, : FH // 2].reshape(FH),
+        gains_grad,
+        biases_grad,
+        fc_bias_grad.reshape(FH),
     )
 
 

time: 478 us -> 428 us (0.90)
  Pallas kernels: 452 us -> 408 us
  local copies, waits for them, and re-layouts: 16.1 us -> 10.1 us
    pallas_call x3, Pallas kernels: 452 us -> 402 us  [call(): pl.pallas_call(body, out_shape=outs, in_specs=in_specs, out_specs=out_spe...]
    pallas_call x0 -> x1, Pallas kernels: none -> 5.97 us  [assemble(): pl.pallas_call(body, out_shape=outs, in_specs=[VM] * 9, out_specs=[VM] *...]
    unnamed x18 -> x6, local copies, waits for them, and re-layouts: 11.1 us -> 8.22 us
where the time goes in v4:
time: 428 us; the launch traced here: 419 us
  Pallas kernels  408 us (95%)
  local copies, waits for them, and re-layouts  10.1 us (2%)
    pallas_call x3, Pallas kernels, call(): pl.pallas_call(body, out_shape=outs, in_specs=in_specs, out_specs=out_spe...  402 us

profile of v4, /device:TPU:0, one launch (start us, length us, event | category | flops | bytes accessed | tf_op | source)
XLA Modules:
  0.0 419.2 jit_solution(6575539368190899748)
XLA Ops:
  0.6 1.2 reshape.37.refs_3_
  1.9 2.0 copy.18
  3.9 2.0 copy.19
  5.8 171.2 %forward.1 = (bf16[2,4,128,1600]{3,2,1,0:T(8,128)(2,1)}, bf16[1600,768]{1,0:T(8,128)(2,1)}, bf16[3,2,64,2048]{3,2,1,0:T(8,128)(2,1)}, f32[2,64,2048]{2,1,0:T(8,1...) custom-call(bf16[128,1600]{1,0:T(8,128)(2,1)} %bitcast.4, ...), custom_call_target="tpu_custom_call" | custom-call | tf_op jit(solution)/shard_map/forward/pallas_call | solution.py:426
  177.0 91.4 %middle.1 = (bf16[2,4,128,1600]{3,2,1,0:T(8,128)(2,1)}, bf16[2,16,64,128]{3,2,1,0:T(8,128)(2,1)}, bf16[2,4,100,800]{3,2,1,0:T(8,128)(2,1)}, bf16[2,200,1600]{2,1...) custom-call(bf16[2,4,128,1600]{3,2,1,0:T(8,128)(2,1)} %get-tuple-element.48.refs_0_, ...), custom_call_target="tpu_custom_call" | custom-call | tf_op jit(solution)/shard_map/middle/pallas_call | solution.py:426
  268.5 139.3 %backward.1 = (f32[128,1600]{1,0:T(8,128)}, bf16[2,4,100,768]{3,2,1,0:T(8,128)(2,1)}, bf16[100,800]{1,0:T(8,128)(2,1)}, f32[8,128]{1,0:T(8,128)}, bf16[128,1600]{1,0:T(8,128)(2,1)}) custom-call(bf16[128,1600]{1,0:T(8,128)(2,1)} %bitcast.5, bf16[3,2,64,2048]{3,2,1,0:T(8,128)(2,1)} %get-tuple-element.45.refs_1_, f32[2,64,2048]{2,1,0:T(8,128)} %get-tuple-element.46.refs_2_, ...), custom_call_target="tpu_custom_call" | custom-call | tf_op jit(solution)/shard_map/backward/pallas_call | solution.py:426
  407.8 6.0 %assemble.1 = (bf16[128,1600]{1,0:T(8,128)(2,1)}, f32[128,1600]{1,0:T(8,128)}, f32[100,2400]{1,0:T(8,128)}, f32[100,800]{1,0:T(8,128)}, f32[100,3200]{1,0:T(8,12...) custom-call(bf16[2,4,100,768]{3,2,1,0:T(8,128)(2,1)} %get-tuple-element.65.refs_0_, ...), custom_call_target="tpu_custom_call" | custom-call | tf_op jit(solution)/shard_map/assemble/pallas_call | solution.py:1371
  413.7 0.0 copy-start
  413.8 2.0 copy.20
  415.7 2.3 copy.21
  418.0 0.0 copy-done
  418.0 0.6 reshape.41
Async XLA Ops:
  413.7 4.3 %copy-start = (f32[2,100]{1,0:T(2,128)S(1)}, f32[2,100]{1,0:T(2,128)}, u32[]{:S(2)}) copy-start(f32[2,100]{1,0:T(2,128)} %get-tuple-element.80) | copy-start | bytes 2404

commit v5 on v4

--- a/solution.py
+++ b/solution.py
@@ -27,7 +27,7 @@
     def __init__(self, n_ctx):
         self.n_ctx = n_ctx
         a, b = n_ctx // 4, n_ctx // 2
-        self.tp_bits = (a, b)
+        self.tp_bits = (b, a)
         self.dp_bits = tuple(1 << i for i in range(n_ctx.bit_length() - 3))
         self.n_dp = n_ctx // 4
         self.dp_order = list(zip(self.dp_bits, self.dp_bits[::-1]))
@@ -93,14 +93,21 @@
         self.d = layout.dp_index(self.c)
         self.rank = self.c * 2 + self.s
         self.n_dev = layout.n_ctx * 2
+        self.opened = []
 
     def other(self):
         return (self.c, 1 - self.s)
 
+    def drain(self):
+        for links in self.opened:
+            links.drain()
+
 
 class Links:
-    def __init__(self, sems):
+    def __init__(self, sems, env=None):
         self.send_sems, self.recv_sems, self.local_sems = sems
+        if env is not None:
+            env.opened.append(self)
         self.count = 0
         self.local_count = 0
         self.sent = []
@@ -127,9 +134,13 @@
         self.locals.append(copy)
         return copy
 
-    def finish(self):
+    def settle(self):
         for copy in self.locals:
             copy.wait()
+        self.locals = []
+
+    def drain(self):
+        self.settle()
         for copy in self.sent:
             copy.wait_send()
 
@@ -159,6 +170,25 @@
         return carry
 
     lax.fori_loop(1, env.n_dev, hail, 0)
+
+
+def near(env):
+    lay = env.lay
+    return (
+        [(flips(env.c, m, env.s), env.s) for m in lay.tp_masks[1:]]
+        + [(lay.compose(env.t, (env.d + i) % lay.n_dp), env.s) for i in range(1, lay.n_dp)]
+        + [env.other()]
+    )
+
+
+def hail_near(env):
+    barrier = pltpu.get_barrier_semaphore()
+    for device in near(env):
+        pl.semaphore_signal(barrier, inc=1, device_id=device, device_id_type=MESH)
+
+
+def meet_near(env):
+    pl.semaphore_wait(pltpu.get_barrier_semaphore(), len(near(env)))
 
 
 def meet_all(env):
@@ -186,31 +216,24 @@
         active = left
 
 
-def gather_sends(have, bits, core, rows):
-    return (3 if rows else 0) + have * ((1 << bits) - 1) + (have << bits if core else 0)
-
-
-def gather(env, src, buf, sems, bits, slot, core=False, rows=False, half=None):
+def gather_sends(bits, core):
+    return (1 << bits) - 1 + (1 << bits if core else 0)
+
+
+def gather(env, links, src, buf, bits, slot, core=False, half=None, placed=False):
     c, s = env.c, env.s
-    links = Links(sems)
 
     def place(masks):
-        index = slot(flips(c, masks, s))
-        return buf.at[s, index] if core else buf.at[index]
-
-    own = src.at[env.t] if rows else src
-    links.local(own, place([]))
+        return buf.at[slot(flips(c, masks, s))]
+
+    if not placed:
+        links.local(src, place([]))
     levels = [[([], None)]] + [[] for _ in bits]
-    if rows:
-        for m in env.lay.tp_masks[1:]:
-            there = flips(c, m, s)
-            copy = links.send(src.at[env.lay.tp_index(there)], place([]), (there, s))
-            levels[0].append((m, copy))
     crossing = []
     for k in range(len(bits) + 1):
         for masks, copy in levels[k]:
             if copy is None:
-                ref = own
+                ref = src
             else:
                 copy.wait_recv()
                 ref = place(masks)
@@ -225,23 +248,63 @@
             yield
     for copy in crossing:
         copy.wait_recv()
-    links.finish()
-    yield
-
-
-def reduce_sends(have, bits, core, rows, halves):
-    return (have << bits if core else 0) + have * ((1 << bits) - 1) + (3 + 4 if rows else 0) + (1 if halves else 0)
-
-
-def reduce_scratch(have, bits, core, block):
-    counts = [have << j for j in range(bits + (1 if core else 0))]
-    return [pltpu.VMEM((n,) + block, BF) for n in counts]
-
-
-def reduce(env, inp, out, parts, sems, bits, slot, core=False, rows=False, halves=False, own=None):
+
+
+def gather_blocks(env, src, buf, sems, bits, slot, core=False, half=None):
+    links = Links(sems, env)
+    yield from gather(env, links, src, buf.at[env.s] if core else buf, bits, slot, core, half)
+    links.settle()
+    yield
+
+
+def gather_columns(env, src, buf, sems):
+    lay = env.lay
+    links = Links(sems, env)
+    own = buf.at[env.d]
+    copies = [links.local(src.at[env.t], own.at[env.t])]
+    for m in lay.tp_masks[1:]:
+        there = flips(env.c, m, env.s)
+        copies.append(links.send(src.at[lay.tp_index(there)], own.at[env.t], (there, env.s)))
+    yield
+    links.settle()
+    for copy in copies[1:]:
+        copy.wait_recv()
+    yield from gather(env, links, own, buf, lay.dp_order, lay.dp_index, placed=True)
+    links.settle()
+    yield
+
+
+def gather_all(env, src, buf, sems):
+    lay = env.lay
+    links = Links(sems, env)
+    mine = buf.at[env.s]
+    own = mine.at[env.d]
+    yield from gather(env, links, src, own, lay.tp_order, lay.tp_index)
+    links.settle()
+    yield from gather(env, links, own, mine, lay.dp_order, lay.dp_index, core=True, placed=True)
+    links.settle()
+    yield
+
+
+def reduce_sends(bits, core):
+    return (1 << bits) - 1 + (1 << bits if core else 0)
+
+
+def reduce_scratch(bits, core, block, dtype=BF):
+    return [pltpu.VMEM((1 << j,) + block, dtype) for j in range(bits + (1 if core else 0))]
+
+
+def add_into(total, term):
+    if len(total.shape) == 2:
+        total[...] = total[...] + term[...]
+    else:
+        for i in range(total.shape[0]):
+            add_into(total.at[i], term.at[i])
+
+
+def reduce(env, links, inp, parts, bits, slot, core=False, own=None):
     c, s = env.c, env.s
-    links = Links(sems)
-    levels = [list(env.lay.tp_masks) if rows else [[]]]
+    levels = [[[]]]
     for sym in bits:
         levels.append(levels[-1] + [m + [sym] for m in levels[-1]])
 
@@ -271,7 +334,7 @@
         after = {}
         for i in reversed(range(n)):
             copies[i].wait_recv()
-            got[i] = got[i] + now[i][...]
+            add_into(got.at[i], now[i])
             if stage > 0 and i >= n // 2:
                 after[i - n // 2] = links.send(
                     got.at[i], parts[stage - 1].at[i - n // 2], (flip(c, bits[stage - 1], s), s)
@@ -280,67 +343,57 @@
         now = [got.at[i] for i in range(n)]
         copies = after
         stage -= 1
-    if rows:
-        arrivals = []
-        links.local(now[0], out.at[s, env.t])
-        arrivals.append((env.t, None, now[0]))
-        for i, m in enumerate(env.lay.tp_masks):
-            if i > 0:
-                there = flips(c, m, s)
-                copy = links.send(now[i], out.at[s, env.t], (there, s))
-                index = env.lay.tp_index(there)
-                arrivals.append((index, copy, out.at[s, index]))
-        yield
-        crossing = []
-        for index, copy, ref in arrivals:
-            if copy is not None:
-                copy.wait_recv()
-            crossing.append(links.send(ref, out.at[s, index], env.other()))
-            yield
-        for copy in crossing:
-            copy.wait_recv()
-    elif halves:
-        links.local(now[0], out.at[s])
-        copy = links.send(now[0], out.at[s], env.other())
-        yield
+    return now[0]
+
+
+def reduce_blocks(env, inp, out, parts, sems, own=None):
+    links = Links(sems, env)
+    total = yield from reduce(env, links, inp, parts, env.lay.tp_order, env.lay.tp_index, core=True, own=own)
+    out[...] = total[...].astype(out.dtype)
+    links.settle()
+    yield
+
+
+def reduce_columns(env, inp, out, parts, sems):
+    lay = env.lay
+    links = Links(sems, env)
+    total = yield from reduce(env, links, inp, parts, lay.dp_order, lay.dp_index)
+    local = links.local(total.at[env.t], out.at[env.s, env.t])
+    copies = []
+    for m in lay.tp_masks[1:]:
+        there = flips(env.c, m, env.s)
+        copies.append(links.send(total.at[lay.tp_index(there)], out.at[env.s, env.t], (there, env.s)))
+    yield
+    links.settle()
+    for copy in copies:
         copy.wait_recv()
-    else:
-        out[...] = now[0][...].astype(out.dtype)
-    links.finish()
-    yield
-
-
-def to_everyone(env, src, out, sems, same):
-    send_sems, recv_sems, local_sems = sems
-
-    def own(ref):
-        return ref if same else ref.at[env.rank]
-
-    def copy(i):
-        rank = (env.rank + i) % env.n_dev
-        return pltpu.make_async_remote_copy(
-            src_ref=src if same else src.at[rank],
-            dst_ref=out.at[env.rank],
-            send_sem=send_sems.at[i],
-            recv_sem=recv_sems.at[i],
-            device_id=(rank // 2, rank % 2),
-            device_id_type=MESH,
-        )
-
-    def begin(i, carry):
-        copy(i).start()
-        return carry
-
-    def end(i, carry):
-        copy(i).wait()
-        return carry
-
-    lax.fori_loop(1, env.n_dev, begin, 0)
-    local = pltpu.make_async_copy(own(src), out.at[env.rank], local_sems.at[0])
-    local.start()
-    yield
-    lax.fori_loop(1, env.n_dev, end, 0)
-    local.wait()
+    copy = links.send(out.at[env.s], out.at[env.s], env.other())
+    yield
+    copy.wait_recv()
+    links.settle()
+    yield
+
+
+def reduce_halves(env, inp, out, parts, sems):
+    lay = env.lay
+    links = Links(sems, env)
+    total = yield from reduce(env, links, inp, parts, lay.dp_order, lay.dp_index)
+    links.local(total, out.at[env.s])
+    copy = links.send(total, out.at[env.s], env.other())
+    yield
+    copy.wait_recv()
+    links.settle()
+    yield
+
+
+def reduce_all(env, inp, out, parts, sems):
+    lay = env.lay
+    links = Links(sems, env)
+    n = len(lay.dp_bits) + 1
+    total = yield from reduce(env, links, inp, parts[:n], lay.dp_order, lay.dp_index, core=True)
+    total = yield from reduce(env, links, total, parts[n:], lay.tp_order, lay.tp_index)
+    out[...] = total[...].astype(out.dtype)
+    links.settle()
     yield
 
 
@@ -349,28 +402,42 @@
     return h, jnp.logical_and(env.d < HU, h < HEADS)
 
 
+def wait_pieces(env, ref, count, send=None, recv=None):
+    part = ref.at[pl.ds(0, count)]
+    copy = pltpu.make_async_remote_copy(
+        src_ref=part,
+        dst_ref=part,
+        send_sem=recv if send is None else send,
+        recv_sem=send if recv is None else recv,
+        device_id=env.other(),
+        device_id_type=MESH,
+    )
+    if send is not None:
+        copy.wait_send()
+    if recv is not None:
+        copy.wait_recv()
+
+
 def tokens_to_heads(env, src, out, sems):
-    send_sems, recv_sems, local_sems = sems
+    send_sem, recv_sem, local_sem = sems[0].at[0], sems[1].at[0], sems[2].at[0]
     h, active = own_head(env)
     lay = env.lay
-
-    def copy(j):
+    place = env.s * lay.n_ctx + env.c
+
+    def begin(i, carry):
+        j = (env.rank + i) % HEADS
         rank = lay.head_rank(j)
-        return rank, pltpu.make_async_remote_copy(
-            src_ref=src.at[j],
-            dst_ref=out.at[env.s, env.c],
-            send_sem=send_sems.at[j],
-            recv_sem=recv_sems.at[(rank - env.rank + env.n_dev) % env.n_dev],
-            device_id=(rank // 2, rank % 2),
-            device_id_type=MESH,
-        )
-
-    def begin(i, carry):
-        rank, cp = copy((env.rank + i) % HEADS)
 
         @pl.when(rank != env.rank)
         def _():
-            cp.start()
+            pltpu.make_async_remote_copy(
+                src_ref=src.at[j],
+                dst_ref=out.at[place],
+                send_sem=send_sem,
+                recv_sem=recv_sem,
+                device_id=(rank // 2, rank % 2),
+                device_id_type=MESH,
+            ).start()
 
         return carry
 
@@ -379,39 +446,15 @@
 
     @pl.when(active)
     def _():
-        local = pltpu.make_async_copy(src.at[h], out.at[env.s, env.c], local_sems.at[0])
+        local = pltpu.make_async_copy(src.at[h], out.at[place], local_sem)
         local.start()
         local.wait()
-
-        def receive(i, carry):
-            rank = (env.rank - i + env.n_dev) % env.n_dev
-            pltpu.make_async_remote_copy(
-                src_ref=src.at[0],
-                dst_ref=out.at[rank % 2, rank // 2],
-                send_sem=send_sems.at[0],
-                recv_sem=recv_sems.at[i],
-                device_id=env.other(),
-                device_id_type=MESH,
-            ).wait_recv()
-            return carry
-
-        lax.fori_loop(1, env.n_dev, receive, 0)
-
-    def end(j, carry):
-        rank, cp = copy(j)
-
-        @pl.when(rank != env.rank)
-        def _():
-            cp.wait_send()
-
-        return carry
-
-    lax.fori_loop(0, HEADS, end, 0)
-
-
-def data_partners(env):
-    lay = env.lay
-    return [(lay.compose(env.t, (env.d + i) % lay.n_dp), env.s) for i in range(1, lay.n_dp)]
+        wait_pieces(env, out, env.n_dev - 1, recv=recv_sem)
+        wait_pieces(env, src, HEADS - 1, send=send_sem)
+
+    @pl.when(jnp.logical_not(active))
+    def _():
+        wait_pieces(env, src, HEADS, send=send_sem)
 
 
 ANY = pl.BlockSpec(memory_space=pl.ANY)
@@ -520,7 +563,7 @@
 
 
 def heads_out(env, src, out, sems, q):
-    send_sems, recv_sems, local_sems = sems
+    send_sem, recv_sem = sems[0].at[q], sems[1].at[0]
     h, active = own_head(env)
     n_ctx = env.lay.n_ctx
 
@@ -529,13 +572,13 @@
         return pltpu.make_async_remote_copy(
             src_ref=src.at[q, there],
             dst_ref=out.at[h],
-            send_sem=send_sems.at[q, i],
-            recv_sem=recv_sems.at[h],
+            send_sem=send_sem,
+            recv_sem=recv_sem,
             device_id=(there, q),
             device_id_type=MESH,
         )
 
-    local = pltpu.make_async_copy(src.at[q, env.c], out.at[h], local_sems.at[q])
+    local = pltpu.make_async_copy(src.at[q, env.c], out.at[h], sems[2].at[q])
     mine = jnp.logical_and(active, env.s == q)
     theirs = jnp.logical_and(active, env.s != q)
 
@@ -543,10 +586,6 @@
         copy(i).start()
         return carry
 
-    def end(i, carry):
-        copy(i).wait_send()
-        return carry
-
     @pl.when(mine)
     def _():
         local.start()
@@ -565,31 +604,27 @@
     def _():
         local.wait()
 
+    yield
+
+    @pl.when(mine)
+    def _():
+        wait_pieces(env, src.at[q], n_ctx - 1, send=send_sem)
+
     @pl.when(theirs)
     def _():
-        copy(0).wait_send()
+        wait_pieces(env, src.at[q], n_ctx, send=send_sem)
+
+
+def heads_in(env, out, sems):
+    _, active = own_head(env)
 
     @pl.when(active)
     def _():
-        lax.fori_loop(1, n_ctx, end, 0)
-
-
-def heads_in(env, src, out, sems):
-    def receive(j, carry):
-        @pl.when(env.lay.head_rank(j) != env.rank)
-        def _():
-            pltpu.make_async_remote_copy(
-                src_ref=src.at[0, 0],
-                dst_ref=out.at[j],
-                send_sem=sems[0].at[0, 0],
-                recv_sem=sems[1].at[j],
-                device_id=env.other(),
-                device_id_type=MESH,
-            ).wait_recv()
-
-        return carry
-
-    lax.fori_loop(0, HEADS, receive, 0)
+        wait_pieces(env, out, HEADS - 1, recv=sems[1].at[0])
+
+    @pl.when(jnp.logical_not(active))
+    def _():
+        wait_pieces(env, out, HEADS, recv=sems[1].at[0])
 
 
 def norm_stats(values):
@@ -630,7 +665,7 @@
     n_ctx, n_dp = lay.n_ctx, lay.n_dp
     n_dev = 2 * n_ctx
     k = len(lay.dp_bits)
-    T = x.shape[0]
+    T = x.shape[1]
     R, FB = D // n_ctx, FF // n_ctx
     FH = FB // 2
     W = HU * HEAD_DIM
@@ -649,14 +684,15 @@
         (h1_o, wq_o, heads_o, o_o, pj_o, h2_o, fc_o, out_o, outx_o, dy_o, lse_o, ob_o, x1_o, shift_o, par_o) = refs[9:24]
         (
             pack, small, qkv_x, fc_x, qkv_s, fc_s, out_s, wq_b, wq_v, x_v, h1_v, par_w,
-            parts, mine, keys, heads_v, o_v, o_low, ob_b, proj_b, pj_v, h2_s,
-        ) = refs[24:46]
-        sems = refs[46:]
+            parts, mine, keys, heads_v, o_v, o_low, ob_b, proj_b, pj_v, h2_s, x_s, dy_s, h1_t,
+        ) = refs[24:49]
+        sems = refs[49:]
         groups = [sems[3 * i : 3 * i + 3] for i in range(len(sems) // 3)]
         env = Env(lay)
         s = env.s
 
         hail_all(env)
+        x_s[...] = x_r[...].T
         pack[...] = jnp.zeros_like(pack)
         pack[0:1, :R] = gains_r[...].astype(F32)
         pack[1:4, :R] = biases_r[...].astype(F32)
@@ -665,15 +701,10 @@
             out_s[h] = out_r[h * FH : (h + 1) * FH, :]
         par_w[...] = jnp.zeros_like(par_w)
         meet_all(env)
-        links = Links(groups[0])
+        links = Links(groups[0], env)
         crossing = [links.send(a, b, env.other()) for a, b in ((qkv_r, qkv_x), (fc_r, fc_x))]
-        rows_x = gather(env, x_r, x_v, groups[3], lay.tp_order, lay.tp_index, core=True)
-        next(rows_x)
-        everyone = to_everyone(env, pack, small, groups[1], True)
-        next(everyone)
-        bg = Background()
-        bg.add(gather(env, out_s, out_o, groups[8], lay.dp_order, lay.dp_index, half=outx_o))
-        bg.step()
+        params = gather_all(env, pack, small, groups[1])
+        next(params)
 
         def fill_qkv(a, b, side):
             q = a[:, :D]
@@ -697,41 +728,49 @@
 
         crossing[0].wait_recv()
         by_side(s, lambda side: fill_qkv(*((qkv_r, qkv_x) if side == 0 else (qkv_x, qkv_r)), side))
-        weights = gather(env, qkv_s, wq_b, groups[2], lay.dp_order, natural, rows=True)
+        weights = gather_columns(env, qkv_s, wq_b, groups[2])
         next(weights)
+        steps(params, 4)
+        rows_x = gather_blocks(env, x_s, x_v, groups[3], lay.tp_order, lay.tp_index, core=True)
+        next(rows_x)
+        proj = gather_all(env, proj_r, proj_b, groups[7])
+        next(proj)
+        out_all = gather_blocks(env, out_s, out_o, groups[8], lay.dp_order, lay.dp_index, half=outx_o)
+        next(out_all)
+        dy_s[...] = dy_r[...].T
         crossing[1].wait_recv()
         by_side(s, lambda side: fill_fc(*((fc_r, fc_x) if side == 0 else (fc_x, fc_r)), side))
-        finish(everyone)
+        steps(weights, 1)
+        steps(params, 2)
+        steps(rows_x, 1)
+        steps(proj, 1)
+        steps(weights, 1)
+        steps(out_all, 1)
+        finish(params)
         for f in range(2):
-            rows = jnp.concatenate([small[2 * c + f][:, :R] for c in range(n_ctx)], axis=1)
-            par_o[f] = rows
+            par_o[f] = jnp.concatenate(
+                [small[f, lay.dp_index(c), lay.tp_index(c)][:, :R] for c in range(n_ctx)], axis=1
+            )
         par_w[:, :D] = par_o[0]
         shift_parts = []
         for d in range(n_dp):
-            block = small[lay.compose(env.t, d) * 2 + s]
+            block = small[s, d, env.t]
             shift_parts += [block[4:5, : FH // 2], block[5:6, : FH // 2]]
         shift_o[...] = jnp.concatenate(shift_parts, axis=1)
-        steps(weights, 3)
-        bg.step()
-        steps(rows_x, 1)
-        steps(weights, 4)
-        bg.step(2)
         finish(rows_x)
-        proj = gather(env, proj_r, proj_b, groups[7], lay.tp_order + lay.dp_order, natural, core=True)
-        next(proj)
-        bg.add(gather(env, fc_s, fc_o, groups[5], lay.dp_order, natural, rows=True))
-        bg.step(2)
 
         @pl.loop(0, 8)
         def _(i):
             hat, _ = norm_stats(x_v[i // 4, i % 4].astype(F32))
-            h1_v[i // 4, i % 4] = (hat * par_o[0, 0:1, :] + par_o[0, 1:2, :]).astype(BF)
+            low = (hat * par_o[0, 0:1, :] + par_o[0, 1:2, :]).astype(BF)
+            h1_v[i // 4, i % 4] = low
+            h1_t[:, pl.ds(pl.multiple_of(i * T, T), T)] = low.T
 
         finish(weights)
         for c in range(n_ctx):
-            wq_v[c * R : (c + 1) * R, :] = wq_b[c]
+            wq_v[c * R : (c + 1) * R, :] = wq_b[lay.dp_index(c), lay.tp_index(c)]
         leave = Links((None, None, groups[11][2]))
-        leave.local(h1_v, h1_o)
+        leave.local(h1_t, h1_o)
         leave.local(wq_v, wq_o)
         unit = 2 * env.t + s
         cols = pl.ds(pl.multiple_of(unit * W, W), W)
@@ -749,9 +788,11 @@
             g = group_to_heads(env, parts, mine, groups[6], q)
             next(g)
             moving.append(g)
-        steps(proj, 1)
-        bg.step(4)
-        bg.add(gather(env, dy_r, dy_o, groups[4], lay.tp_order, lay.tp_index, core=True))
+        steps(proj, 3)
+        fc_all = gather_columns(env, fc_s, fc_o, groups[5])
+        next(fc_all)
+        dy_all = gather_blocks(env, dy_s, dy_o, groups[4], lay.tp_order, lay.tp_index, core=True)
+        next(dy_all)
         leaving = []
         for q in range(2):
             next(moving[q])
@@ -770,8 +811,8 @@
                 low = o.astype(BF)
                 for b in range(tile // T):
                     o_low[q, i * (tile // T) + b] = low[:, b * T : (b + 1) * T]
-                steps(proj, 2)
-                bg.step(2)
+                if i == n_tiles - 1:
+                    steps(proj, 1 if q == 0 else n_dp // 2)
             g = heads_out(env, o_low, ob_b, groups[9], q)
             next(g)
             leaving.append(g)
@@ -780,36 +821,40 @@
         finish(proj)
         for n in range(2):
             for c in range(n_ctx):
-                pj_v[n, c * R : (c + 1) * R, :] = proj_b[n, c]
+                pj_v[n, c * R : (c + 1) * R, :] = proj_b[n, lay.dp_index(c), lay.tp_index(c)]
         leave.local(pj_v, pj_o)
         for g in leaving:
-            finish(g)
-        heads_in(env, o_low, ob_b, groups[9])
+            next(g)
+        heads_in(env, ob_b, groups[9])
         ob_o[...] = ob_b[...].reshape(D, T).T
         branch = jnp.concatenate([dot(ob_o[...], pj_v[n], NN) for n in range(2)], axis=1)
-        x1 = x_r[...].astype(F32) + branch + par_o[1, 1:2, :]
+        x1 = x_s[...].astype(F32) + branch + par_o[1, 1:2, :]
         x1_o[...] = x1
         hat, _ = norm_stats(x1)
         h2_s[...] = (hat * par_o[1, 0:1, :] + par_o[1, 2:3, :]).astype(BF)
-        rows_h2 = gather(env, h2_s, h2_o, groups[10], lay.tp_order, lay.tp_index, core=True)
+        rows_h2 = gather_blocks(env, h2_s, h2_o, groups[10], lay.tp_order, lay.tp_index, core=True)
         next(rows_h2)
-        bg.step(4)
-        next(rows_h2)
-        bg.finish()
+        steps(fc_all, 1)
+        steps(dy_all, 1)
+        steps(rows_h2, 1)
+        steps(fc_all, 1)
+        finish(out_all)
+        finish(fc_all)
+        finish(dy_all)
         finish(rows_h2)
-        for g in moving:
+        for g in moving + leaving:
             finish(g)
-        leave.finish()
-        links.finish()
+        leave.settle()
+        env.drain()
 
     outs = [
-        struct(2, 4, T, D),
+        struct(D, 2 * G),
         struct(D, 3 * W),
         struct(3, 2, HEAD_DIM, length),
         struct(2, HEAD_DIM, length, dtype=F32),
         struct(2, D, half),
         struct(2, 4, T, D),
-        struct(n_ctx, R, n_dp * FH),
+        struct(n_dp, 4, R, n_dp * FH),
         struct(n_dp, 2, FH, half),
         struct(n_dp, FH, half),
         struct(2, 4, T, D),
@@ -822,13 +867,13 @@
     out_specs = [ANY] * 10 + [VM] * 5
     scratch = [
         pltpu.VMEM((8, 128), F32),
-        pltpu.VMEM((n_dev, 8, 128), F32),
+        pltpu.VMEM((2, n_dp, 4, 8, 128), F32),
         pltpu.VMEM(qkv.shape, BF),
         pltpu.VMEM(fc.shape, BF),
         pltpu.VMEM((4, R, 3 * W), BF),
         pltpu.VMEM((4, R, n_dp * FH), BF),
         pltpu.VMEM((2, FH, half), BF),
-        pltpu.VMEM((n_ctx, R, 3 * W), BF),
+        pltpu.VMEM((n_dp, 4, R, 3 * W), BF),
         pltpu.VMEM((D, 3 * W), BF),
         pltpu.VMEM((2, 4, T, D), BF),
         pltpu.VMEM((2, 4, T, D), BF),
@@ -840,22 +885,25 @@
         pltpu.VMEM((2, HEAD_DIM, length), F32),
         pltpu.VMEM((2, n_ctx, HEAD_DIM, T), BF),
         pltpu.VMEM((HEADS, HEAD_DIM, T), BF),
-        pltpu.VMEM((2, n_ctx, R, half), BF),
+        pltpu.VMEM((2, n_dp, 4, R, half), BF),
         pltpu.VMEM((2, D, half), BF),
         pltpu.VMEM((T, D), BF),
+        pltpu.VMEM((T, D), BF),
+        pltpu.VMEM((T, D), BF),
+        pltpu.VMEM((D, 2 * G), BF),
     ]
     DMA = pltpu.SemaphoreType.DMA
-    scratch += sem_shapes(2) + sem_shapes(n_dev)
-    scratch += sem_shapes(gather_sends(4, k, False, True))
-    scratch += sem_shapes(gather_sends(1, 2, True, False)) * 2
-    scratch += sem_shapes(gather_sends(4, k, False, True))
+    columns = sem_shapes(3 + gather_sends(k, False))
+    blocks = sem_shapes(gather_sends(2, True))
+    every = sem_shapes(gather_sends(2, False) + gather_sends(k, True))
+    scratch += sem_shapes(2) + every + columns + blocks * 2 + columns
     scratch += [DMA((2, HU)), DMA((2, n_dp)), DMA((2,))]
-    scratch += sem_shapes(gather_sends(1, k + 2, True, False))
-    scratch += sem_shapes(gather_sends(1, k, True, False))
-    scratch += [DMA((2, n_ctx)), DMA((HEADS,)), DMA((2,))]
-    scratch += sem_shapes(gather_sends(1, 2, True, False))
+    scratch += every
+    scratch += sem_shapes(gather_sends(k, True))
+    scratch += [DMA((2,)), DMA((1,)), DMA((2,))]
+    scratch += blocks
     scratch += sem_shapes(1, 5)
-    in_specs = [VM] * 7 + [ANY] * 2
+    in_specs = [VM] * 7 + [ANY, VM]
     return call(
         "forward", 0, body, (x, gains, biases, fc_bias, qkv, fc, out, proj, dy), in_specs, outs, out_specs, scratch
     )
@@ -872,13 +920,23 @@
         @pl.when(s == side)
         def _():
             f(side)
+
+
+def spread_rows(made, first, size, block):
+    end = first + made.shape[0]
+    at = first
+    while at < end:
+        i = at // size
+        stop = min(end, (i + 1) * size)
+        block(i)[at - i * size : stop - i * size] = made[at - first : stop - first]
+        at = stop
 
 
 def middle(lay, x, h2, dy_all, fc, out, out_x, shift, x1, dy, pj, par):
     n_ctx, n_dp = lay.n_ctx, lay.n_dp
     n_dev = 2 * n_ctx
     k = len(lay.dp_bits)
-    T = x.shape[0]
+    T = x.shape[1]
     R, FB = D // n_ctx, FF // n_ctx
     FH = FB // 2
     U = n_dp * FH
@@ -905,13 +963,12 @@
         loads = Links((None, None, sems[3]))
         load_fc = loads.local(fc_r, fc_b)
         load_h2 = loads.local(h2_r, h2_v)
-        load_out = [loads.local(out_r.at[d, s], out_b.at[0, d]) for d in range(n_dp)]
-        load_out += [loads.local(outx_r.at[d], out_b.at[1, d]) for d in range(n_dp)]
+        load_out = [loads.local(out_r.at[:, s], out_b.at[0]), loads.local(outx_r, out_b.at[1])]
         load_dy = loads.local(dya_r, dy_v)
         load_pj = loads.local(pj_r, pj_v)
         load_fc.wait()
         for c in range(n_ctx):
-            fc_w[c * R : (c + 1) * R, :] = fc_b[c]
+            fc_w[c * R : (c + 1) * R, :] = fc_b[lay.dp_index(c), lay.tp_index(c)]
         for copy in load_out:
             copy.wait()
 
@@ -941,31 +998,29 @@
                 dact = dot(dy_v[q, pl.ds(2 * i, 2)].reshape(chunk, D), out_w[...], NT)
                 du = (dact * slope).astype(BF)
                 du_v[q, at, :] = du
-                back = dot(du, fc_w[...], NT).astype(BF)
-                back_p[q, pl.ds(2 * i, 2)] = back.reshape(2, T, D)
+                back_p[q, pl.ds(2 * i, 2)] = dot(du, fc_w[...], NT).astype(BF).reshape(2, T, D)
 
         forth_and_back(1 - s)
         meet_all(env)
-        rows = reduce(env, back_p, dh2_v, *spans[0], lay.tp_order, lay.tp_index, core=True)
+        rows = reduce_blocks(env, back_p, dh2_v, *spans[0])
         next(rows)
         forth_and_back(s)
         steps(rows, 4)
-        for c in range(0, n_ctx, 4):
-            left = h2_v[:, :, :, c * R : (c + 4) * R].reshape(2 * G, 4 * R)
+        for first in range(0, D, TILE):
+            left = h2_v[:, :, :, first : min(D, first + TILE)].reshape(2 * G, -1)
             made = dot(left, du_v[...].reshape(2 * G, U), TN).astype(BF)
-            for i in range(4):
-                fc_b[c + i] = made[i * R : (i + 1) * R, :]
-        fc_sum = reduce(env, fc_b, fc_o, *spans[1], lay.dp_order, natural, rows=True)
+            spread_rows(made, first, R, lambda c: fc_b.at[lay.dp_index(c), lay.tp_index(c)])
+        fc_sum = reduce_columns(env, fc_b, fc_o, *spans[1])
         next(fc_sum)
-        for d in range(n_dp):
-            left = gb_v[:, :, d * FH : (d + 1) * FH].reshape(2 * G, FH)
-            out_g[d] = dot(left, dy_v[...].reshape(2 * G, D), TN).astype(BF)
-        out_sum = reduce(env, out_g, out_o, *spans[2], lay.dp_order, lay.dp_index, halves=True)
-        next(out_sum)
+        for first in range(0, U, TILE):
+            left = gb_v[:, :, first : min(U, first + TILE)].reshape(2 * G, -1)
+            made = dot(left, dy_v[...].reshape(2 * G, D), TN).astype(BF)
+            spread_rows(made, first, FH, lambda d: out_g.at[d])
+        out_sum = reduce_halves(env, out_g, out_o, *spans[2])
         fcb_o[...] = jnp.sum(du_v[...].reshape(2 * G, U).astype(F32), axis=0, keepdims=True)
         x1 = x1_r[...]
         hat, spread = norm_stats(x1)
-        dy_own = dy_r[...].astype(F32)
+        dy_own = dy_r[...].T.astype(F32)
         vec_o[...] = jnp.zeros_like(vec_o)
         vec_o[3:4, :] = jnp.sum(dy_own, axis=0, keepdims=True)
         for q in range(2):
@@ -977,8 +1032,9 @@
                 h2_v[q, pl.ds(2 * i, 2)] = part.reshape(2, T, D)
 
         leave = loads.local(h2_v, mix_o)
-        steps(rows, 2)
-        steps(fc_sum, 8)
+        steps(rows, 1)
+        steps(fc_sum, n_dp // 2)
+        next(out_sum)
         finish(rows)
         dh2 = dh2_v[...].astype(F32)
         scaled = dh2 * par_r[1, 0:1, :]
@@ -990,22 +1046,22 @@
         dx1_o[...] = dx1
         da = dx1.astype(BF)
         load_pj.wait()
-        dob = dot(da[:, :half], pj_v[0], NT) + dot(da[:, half:], pj_v[1], NT)
-        dob_s[...] = dob.astype(BF).T.reshape(HEADS, HEAD_DIM, T)
+        dob = dot(pj_v[0], da[:, :half], NT) + dot(pj_v[1], da[:, half:], NT)
+        dob_s[...] = dob.astype(BF).reshape(HEADS, HEAD_DIM, T)
         heads = tokens_to_heads(env, dob_s, dob_o, sems[0:3])
         next(heads)
         vec_o[0:1, :] = jnp.sum(dh2 * hat, axis=0, keepdims=True)
         vec_o[1:2, :] = jnp.sum(da.astype(F32), axis=0, keepdims=True)
         vec_o[2:3, :] = jnp.sum(dh2, axis=0, keepdims=True)
-        steps(fc_sum, 4)
-        steps(out_sum, 2)
+        steps(fc_sum, n_dp // 4)
         run([fc_sum, out_sum])
         finish(heads)
         leave.wait()
+        env.drain()
 
     outs = [
         struct(2, 4, T, D),
-        struct(2, n_ctx, HEAD_DIM, T),
+        struct(n_dev, HEAD_DIM, T),
         struct(2, 4, R, U),
         struct(2, FH, D),
         struct(T, D, dtype=F32),
@@ -1015,7 +1071,7 @@
     scratch = [
         pltpu.VMEM((2, 4, T, D), BF),
         pltpu.VMEM((2, 4, T, D), BF),
-        pltpu.VMEM((n_ctx, R, U), BF),
+        pltpu.VMEM((n_dp, 4, R, U), BF),
         pltpu.VMEM((D, U), BF),
         pltpu.VMEM((2, n_dp, FH, half), BF),
         pltpu.VMEM((U, D), BF),
@@ -1027,11 +1083,11 @@
         pltpu.VMEM((T, D), BF),
         pltpu.VMEM((HEADS, HEAD_DIM, T), BF),
     ]
-    scratch += reduce_scratch(1, 2, True, (T, D)) + sem_shapes(reduce_sends(1, 2, True, False, False))
-    scratch += reduce_scratch(4, k, False, (R, U)) + sem_shapes(reduce_sends(4, k, False, True, False))
-    scratch += reduce_scratch(1, k, False, (FH, D)) + sem_shapes(reduce_sends(1, k, False, False, True))
+    scratch += reduce_scratch(2, True, (T, D)) + sem_shapes(reduce_sends(2, True))
+    scratch += reduce_scratch(k, False, (4, R, U)) + sem_shapes(reduce_sends(k, False) + 4)
+    scratch += reduce_scratch(k, False, (FH, D)) + sem_shapes(reduce_sends(k, False) + 1)
     DMA = pltpu.SemaphoreType.DMA
-    scratch += [DMA((HEADS,)), DMA((n_dev,)), DMA((1,)), DMA((2 * n_dp + 5,))]
+    scratch += sem_shapes(1) + [DMA((7,))]
     args = (h2, dy_all, fc, out, out_x, pj, shift, x1, dy, par)
     out_specs = [ANY] * 4 + [VM] * 3
     return call("middle", 1, body, args, [ANY] * 6 + [VM] * 4, outs, out_specs, scratch)
@@ -1086,7 +1142,7 @@
     n_ctx, n_dp = lay.n_ctx, lay.n_dp
     n_dev = 2 * n_ctx
     k = len(lay.dp_bits)
-    T = x.shape[0]
+    T = x.shape[1]
     R, FB = D // n_ctx, FF // n_ctx
     FH = FB // 2
     W = HU * HEAD_DIM
@@ -1105,18 +1161,18 @@
         (grad_o, q_v, proj_o, small_o, mix_s) = refs[13:18]
         (
             heads_v, o_v, dob_n, qs, dobs, delta, dq_acc, parts, land, dqkv, dh1_p, dh1_v, q_g, wide_v,
-            small_s, small_v, pg, wq_r, h1_r,
-        ) = refs[18:37]
-        rest = refs[37:]
+            small_s, pg, wq_r, h1_r,
+        ) = refs[18:36]
+        rest = refs[36:]
         spans, first = [], 0
-        for n in (3, k, k + 3, 3):
+        for n in (3, k, k + 3, 3, k + 3):
             spans.append((rest[first : first + n], rest[first + n : first + n + 3]))
             first += n + 3
         sems = rest[first:]
         env = Env(lay)
         s = env.s
-        hail_all(env)
-        early = Links((None, None, sems[7]))
+        hail_near(env)
+        early = Links((None, None, sems[4]))
         mix_v = dh1_p.at[0]
         load_mix = early.local(mix_r.at[s], mix_v)
         load_wq = early.local(wqh_r, wq_r)
@@ -1126,27 +1182,24 @@
             for c in range(0, n_ctx, 4):
                 made = dot(ob_r[:, c * R : (c + 4) * R], right, TN).astype(BF)
                 for i in range(4):
-                    pg[n, c + i] = made[i * R : (i + 1) * R, :]
+                    pg[n, lay.dp_index(c + i), lay.tp_index(c + i)] = made[i * R : (i + 1) * R, :]
         small_s[...] = jnp.zeros_like(small_s)
         wide_v[...] = jnp.zeros_like(wide_v)
-        meet_all(env)
-        proj = reduce(env, pg, proj_o, *spans[2], lay.tp_order + lay.dp_order, natural, core=True)
+        meet_near(env)
+        proj = reduce_all(env, pg, proj_o, *spans[2])
         next(proj)
-        mixing = reduce(env, mix_r, mix_s, *spans[3], lay.tp_order, lay.tp_index, core=True, own=mix_v)
+        mixing = reduce_blocks(env, mix_r, mix_s, *spans[3], own=mix_v)
         next(mixing)
         load_mix.wait()
         moving = []
         _, active = own_head(env)
 
         def loads(q):
-            copies = [pltpu.make_async_copy(heads_r.at[n, q], heads_v.at[n], sems[6].at[n]) for n in range(3)]
-            copies.append(pltpu.make_async_copy(o_r.at[q], o_v, sems[6].at[3]))
+            copies = [pltpu.make_async_copy(heads_r.at[n, q], heads_v.at[n], sems[3].at[n]) for n in range(3)]
+            copies.append(pltpu.make_async_copy(o_r.at[q], o_v, sems[3].at[3]))
             for c in range(n_ctx):
-                copies.append(
-                    pltpu.make_async_copy(
-                        dob_r.at[q, c], dob_n.at[:, pl.ds(c * T, T)], sems[6].at[4 + c]
-                    )
-                )
+                there = dob_n.at[:, pl.ds(c * T, T)]
+                copies.append(pltpu.make_async_copy(dob_r.at[q * n_ctx + c], there, sems[3].at[4 + c]))
             return copies
 
         for copy in loads(0):
@@ -1203,11 +1256,13 @@
                     carry = lax.fori_loop(j + 1, n_tiles, functools.partial(step, masked=False), carry)
                 put(1, j * tile, (carry[0] * SCALE).T.astype(BF))
                 put(2, j * tile, carry[1].T.astype(BF))
-                if q == 0:
-                    steps(proj, n_ctx // n_tiles)
-                    steps(mixing, 1)
-                else:
-                    steps(proj, n_ctx // 2 // n_tiles)
+                if q == 0 and j == 0:
+                    steps(proj, n_dp)
+                if q == 0 and j == 1:
+                    steps(mixing, 4)
+                if q == 1 and j == 0:
+                    steps(proj, n_dp // 2)
+                if q == 1 and j >= n_tiles - 2:
                     steps(mixing, 1)
             put(0, 0, (dq_acc[...] * SCALE).astype(BF))
             if q == 0:
@@ -1216,6 +1271,7 @@
             g = heads_to_group(env, parts, land, sems[0:3], q)
             next(g)
             moving.append(g)
+        steps(proj, n_dp // 4 + 1)
         load_wq.wait()
         load_h1.wait()
         for q in range(2):
@@ -1226,29 +1282,49 @@
                     rows.append(land[q, j, n * HEAD_DIM : (n + 1) * HEAD_DIM, :])
             dqkv[q] = jnp.concatenate(rows, axis=0).T
             dh1_p[q] = dot(dqkv[q], wq_r[...], NT).astype(BF).reshape(4, T, D)
-        rows_h1 = reduce(env, dh1_p, dh1_v, *spans[0], lay.tp_order, lay.tp_index, core=True)
+        rows_h1 = reduce_blocks(env, dh1_p, dh1_v, *spans[0])
         next(rows_h1)
-        for c in range(0, n_ctx, 4):
-            left = h1_r[:, :, :, c * R : (c + 4) * R].reshape(2 * G, 4 * R)
-            made = dot(left, dqkv[...].reshape(2 * G, 3 * W), TN).astype(BF)
-            for i in range(4):
-                q_g[c + i] = made[i * R : (i + 1) * R, :]
-        grads = reduce(env, q_g, q_v, *spans[1], lay.dp_order, natural, rows=True)
-        next(grads)
-        steps(rows_h1, 4)
-        unit = 2 * env.t + s
         sums = jnp.sum(dqkv[0].astype(F32), axis=0, keepdims=True) + jnp.sum(
             dqkv[1].astype(F32), axis=0, keepdims=True
         )
+        for c in range(0, n_ctx, 4):
+            at = slice(c * R, (c + 4) * R)
+            made = dot(h1_r[at, :], dqkv[...].reshape(2 * G, 3 * W), NN)
+            low = made.astype(BF)
+            for i in range(4):
+                q_g[lay.dp_index(c + i), lay.tp_index(c + i)] = low[i * R : (i + 1) * R, :]
+            weight = wq_r[at, :].astype(F32)
+            for n, product in enumerate((made * weight, weight * sums)):
+                folded = product[:, :128]
+                for lane in range(128, 3 * W, 128):
+                    folded = folded + product[:, lane : lane + 128]
+                wide_v[n : n + 1, at] = jnp.sum(folded.T, axis=0, keepdims=True)
+            if c == n_ctx // 2:
+                steps(rows_h1, 4)
+        grads = reduce_columns(env, q_g, q_v, *spans[1])
+        next(grads)
+        unit = 2 * env.t + s
         cols = pl.ds(pl.multiple_of(unit * W, W), W)
         wide_v[2:3, cols] = sums[:, :W]
         wide_v[3:4, cols] = sums[:, 2 * W :]
-        hat, spread = norm_stats(x_r[...].astype(F32))
+        wide_v[0:1, :D] = (wide_v[0:1, :D] - par_r[0, 1:2, :] * wide_v[1:2, :D]) / par_r[0, 0:1, :]
+        for c in range(n_ctx):
+            small_s[0, lay.dp_index(c), lay.tp_index(c), 0:4, :R] = wide_v[0:4, c * R : (c + 1) * R]
+            small_s[1, lay.dp_index(c), lay.tp_index(c), 0:4, :R] = vec_r[0:4, c * R : (c + 1) * R]
+        for d in range(n_dp):
+            for h in range(2):
+                first = d * FH + h * (FH // 2)
+                small_s[s, d, env.t, 4 + h : 5 + h, : FH // 2] = fcb_r[:, first : first + FH // 2]
+        small = reduce_all(env, small_s, small_o, *spans[4])
+        next(small)
+        hat, spread = norm_stats(x_r[...].T.astype(F32))
+        steps(rows_h1, 1)
         finish(mixing)
-        steps(proj, n_ctx // 4)
-        steps(grads, n_ctx // 2)
-        steps(rows_h1, 2)
-        steps(grads, n_ctx // 4)
+        steps(small, n_dp)
+        steps(grads, n_dp // 2)
+        steps(rows_h1, 1)
+        steps(small, n_dp // 2)
+        steps(grads, n_dp // 4)
         finish(rows_h1)
         dh1 = dh1_v[...].astype(F32)
         scaled = dh1 * par_r[0, 0:1, :]
@@ -1257,27 +1333,12 @@
             - jnp.mean(scaled, axis=-1, keepdims=True)
             - hat * jnp.mean(scaled * hat, axis=-1, keepdims=True)
         )
-        wide_v[0:1, :D] = jnp.sum(dh1 * hat, axis=0, keepdims=True)
-        wide_v[1:2, :D] = jnp.sum(dh1, axis=0, keepdims=True)
-        for c in range(n_ctx):
-            small_s[2 * c, 0:4, :R] = wide_v[0:4, c * R : (c + 1) * R]
-            small_s[2 * c + 1, 0:4, :R] = vec_r[0:4, c * R : (c + 1) * R]
-        for d in range(n_dp):
-            owner = lay.compose(env.t, d) * 2 + s
-            for h in range(2):
-                first = d * FH + h * (FH // 2)
-                small_s[owner, 4 + h : 5 + h, : FH // 2] = fcb_r[:, first : first + FH // 2]
-        everyone = to_everyone(env, small_s, small_v, sems[3:6], False)
-        next(everyone)
+        finish(proj)
+        finish(small)
         finish(grads)
-        finish(proj)
         for g in moving:
             finish(g)
-        finish(everyone)
-        total = small_v[0]
-        for r in range(1, n_dev):
-            total = total + small_v[r]
-        small_o[...] = total
+        env.drain()
 
     outs = [
         struct(T, D, dtype=F32),
@@ -1299,22 +1360,23 @@
         pltpu.VMEM((2, G, 3 * W), BF),
         pltpu.VMEM((2, 4, T, D), BF),
         pltpu.VMEM((T, D), BF),
-        pltpu.VMEM((n_ctx, R, 3 * W), BF),
+        pltpu.VMEM((n_dp, 4, R, 3 * W), BF),
         pltpu.VMEM((8, wide), F32),
-        pltpu.VMEM((n_dev, 8, 128), F32),
-        pltpu.VMEM((n_dev, 8, 128), F32),
-        pltpu.VMEM((2, n_ctx, R, half), BF),
+        pltpu.VMEM((2, n_dp, 4, 8, 128), F32),
+        pltpu.VMEM((2, n_dp, 4, R, half), BF),
         pltpu.VMEM((D, 3 * W), BF),
-        pltpu.VMEM((2, 4, T, D), BF),
+        pltpu.VMEM((D, 2 * G), BF),
     ]
-    scratch += reduce_scratch(1, 2, True, (T, D)) + sem_shapes(reduce_sends(1, 2, True, False, False))
-    scratch += reduce_scratch(4, k, False, (R, 3 * W)) + sem_shapes(reduce_sends(4, k, False, True, False))
-    scratch += reduce_scratch(1, k + 2, True, (R, half)) + sem_shapes(
-        reduce_sends(1, k + 2, True, False, False)
-    )
-    scratch += reduce_scratch(1, 2, True, (T, D)) + sem_shapes(reduce_sends(1, 2, True, False, False))
+    blocks = reduce_scratch(2, True, (T, D)) + sem_shapes(reduce_sends(2, True))
+    scratch += blocks
+    scratch += reduce_scratch(k, False, (4, R, 3 * W)) + sem_shapes(reduce_sends(k, False) + 4)
+    scratch += reduce_scratch(k, True, (4, R, half)) + reduce_scratch(2, False, (R, half))
+    scratch += sem_shapes(reduce_sends(k, True) + reduce_sends(2, False))
+    scratch += blocks
+    scratch += reduce_scratch(k, True, (4, 8, 128), F32) + reduce_scratch(2, False, (8, 128), F32)
+    scratch += sem_shapes(reduce_sends(k, True) + reduce_sends(2, False))
     DMA = pltpu.SemaphoreType.DMA
-    scratch += [DMA((2, n_dp)), DMA((2, HU)), DMA((2,))] + sem_shapes(n_dev) + [DMA((4 + n_ctx,)), DMA((3,))]
+    scratch += [DMA((2, n_dp)), DMA((2, HU)), DMA((2,)), DMA((4 + n_ctx,)), DMA((3,))]
     args = (x, heads, o, lse, dob, wq, h1, ob, vec, fcb, dx1, par, mix)
     in_specs = [VM, ANY, ANY, VM, ANY, ANY, ANY] + [VM] * 5 + [ANY]
     return call("backward", 2, body, args, in_specs, outs, [VM, ANY, VM, VM, VM], scratch)
@@ -1331,8 +1393,8 @@
     def body(*refs):
         (q_r, fc_r, out_r, proj_r, grad_r, mix_r, x1_r, par_r, small_r) = refs[:9]
         (mixed_o, grad_o, qkv_o, proj_o, fc_o, out_o, gains_o, biases_o, fcb_o) = refs[9:]
-        mixed_o[...] = (x1_r[...] + mix_r[...].astype(F32) + par_r[1, 3:4, :]).astype(BF)
-        grad_o[...] = grad_r[...]
+        mixed_o[...] = (x1_r[...] + mix_r[...].astype(F32) + par_r[1, 3:4, :]).astype(BF).T
+        grad_o[...] = grad_r[...].T
         proj_o[...] = proj_r[...].astype(F32)
         gains_o[...] = small_r[0:1, :R]
         biases_o[...] = small_r[1:4, :R]
@@ -1358,8 +1420,8 @@
         by_side(lax.axis_index("fsdp"), last)
 
     outs = [
-        struct(T, D),
-        struct(T, D, dtype=F32),
+        struct(D, T),
+        struct(D, T, dtype=F32),
         struct(R, 3 * half, dtype=F32),
         struct(R, half, dtype=F32),
         struct(R, FF // 2, dtype=F32),
@@ -1382,8 +1444,8 @@
     T = tokens.shape[1]
     R = D // lay.n_ctx
     FH = FF // lay.n_ctx // 2
-    x = tokens.reshape(T, D)
-    dy = cotangent.reshape(T, D)
+    x = jnp.transpose(tokens, (0, 2, 1)).reshape(D, T)
+    dy = jnp.transpose(cotangent, (0, 2, 1)).reshape(D, T)
     (h1, wq, heads, o, pj, h2, fc, out, out_x, dy_all, lse, ob, x1, shift, par) = forward(
         lay, x, gains, biases, fc_bias.reshape(2, FH // 2), qkv_weight, fc_weight, out_weight, proj_weight, dy
     )
@@ -1397,8 +1459,8 @@
         lay, q_sum, fc_sum, out_sum, proj_sum, grad, mix_sum, x1, par, small
     )
     return (
-        mixed.reshape(tokens.shape),
-        grad.reshape(tokens.shape),
+        jnp.transpose(mixed.reshape(1, D, T), (0, 2, 1)),
+        jnp.transpose(grad.reshape(1, D, T), (0, 2, 1)),
         qkv_grad,
         proj_grad,
         fc_grad,

time: 428 us -> 389 us (0.909); the launches traced: 419 us -> 386 us
  Pallas kernels: 408 us -> 382 us
  local copies, waits for them, and re-layouts: 10.1 us -> 2.57 us
    pallas_call x3, Pallas kernels: 402 us -> 376 us  [call(): pl.pallas_call(body, out_shape=outs, in_specs=in_specs, out_specs=out_spe...]
    unnamed x6 -> x0, local copies, waits for them, and re-layouts: 8.22 us -> none
where the time goes in v5:
time: 389 us; the launch traced here: 386 us
  Pallas kernels  382 us (98%)
    pallas_call x3, Pallas kernels, call(): pl.pallas_call(body, out_shape=outs, in_specs=in_specs, out_specs=out_spe...  376 us

profile of v5, /device:TPU:0, one launch (start us, length us, event | category | flops | bytes accessed | tf_op | source)
XLA Modules:
  0.0 385.6 jit_solution(10036873431404069289)
XLA Ops:
  0.6 1.2 reshape.37.refs_3_
  1.9 169.9 %forward.1 = (bf16[1600,1024]{1,0:T(8,128)(2,1)}, bf16[1600,768]{1,0:T(8,128)(2,1)}, bf16[3,2,64,2048]{3,2,1,0:T(8,128)(2,1)}, f32[2,64,2048]{2,1,0:T(8,128)}, b...) custom-call(bf16[1600,128]{1,0:T(8,128)(2,1)} %bitcast.14, ...), custom_call_target="tpu_custom_call" | custom-call | tf_op jit(solution)/shard_map/forward/pallas_call | solution.py:469
  171.8 84.2 %middle.1 = (bf16[2,4,128,1600]{3,2,1,0:T(8,128)(2,1)}, bf16[32,64,128]{2,1,0:T(8,128)(2,1)}, bf16[2,4,100,800]{3,2,1,0:T(8,128)(2,1)}, bf16[2,200,1600]{2,1,0:T...) custom-call(bf16[2,4,128,1600]{3,2,1,0:T(8,128)(2,1)} %get-tuple-element.48.refs_0_, ...), custom_call_target="tpu_custom_call" | custom-call | tf_op jit(solution)/shard_map/middle/pallas_call | solution.py:469
  256.0 121.9 %backward.1 = (f32[128,1600]{1,0:T(8,128)}, bf16[2,4,100,768]{3,2,1,0:T(8,128)(2,1)}, bf16[100,800]{1,0:T(8,128)(2,1)}, f32[8,128]{1,0:T(8,128)}, bf16[128,1600]{1,0:T(8,128)(2,1)}) custom-call(bf16[1600,128]{1,0:T(8,128)(2,1)} %bitcast.15, bf16[3,2,64,2048]{3,2,1,0:T(8,128)(2,1)} %get-tuple-element.45.refs_1_, f32[2,64,2048]{2,1,0:T(8,128)} %get-tuple-element.46.refs_2_, ...), custom_call_target="tpu_custom_call" | custom-call | tf_op jit(solution)/shard_map/backward/pallas_call | solution.py:469
  377.9 6.2 %assemble.1 = (bf16[1600,128]{1,0:T(8,128)(2,1)}, f32[1600,128]{1,0:T(8,128)}, f32[100,2400]{1,0:T(8,128)}, f32[100,800]{1,0:T(8,128)}, f32[100,3200]{1,0:T(8,12...) custom-call(bf16[2,4,100,768]{3,2,1,0:T(8,128)(2,1)} %get-tuple-element.65.refs_0_, ...), custom_call_target="tpu_custom_call" | custom-call | tf_op jit(solution)/shard_map/assemble/pallas_call | solution.py:1433
  384.1 1.3 reshape.41

commit v6 on v5

--- a/solution.py
+++ b/solution.py
@@ -286,6 +286,33 @@
     yield
 
 
+def gather_small(env, src, buf, sems):
+    lay = env.lay
+    links = Links(sems, env)
+    mine = buf.at[env.s]
+    own = mine.at[env.d]
+    local = links.local(src, own.at[env.t])
+    copies = []
+    for m in lay.tp_masks[1:]:
+        copies.append(links.send(src, own.at[env.t], (flips(env.c, m, env.s), env.s)))
+    yield
+    links.settle()
+    for copy in copies:
+        copy.wait_recv()
+    copies = []
+    for i in range(1, lay.n_dp):
+        there = lay.compose(env.t, (env.d + i) % lay.n_dp)
+        copies.append(links.send(own, own, (there, env.s)))
+    yield
+    for copy in copies:
+        copy.wait_recv()
+    copy = links.send(mine, mine, env.other())
+    yield
+    copy.wait_recv()
+    links.settle()
+    yield
+
+
 def reduce_sends(bits, core):
     return (1 << bits) - 1 + (1 << bits if core else 0)
 
@@ -696,14 +723,16 @@
         pack[...] = jnp.zeros_like(pack)
         pack[0:1, :R] = gains_r[...].astype(F32)
         pack[1:4, :R] = biases_r[...].astype(F32)
-        pack[4:6, : FH // 2] = fcb_r[...].astype(F32)
+        row = fcb_r[...].astype(F32).reshape(1, FH)
+        pack[4:5, : FH // 2] = row[:, : FH // 2]
+        pack[5:6, : FH // 2] = row[:, FH // 2 :]
         for h in range(2):
             out_s[h] = out_r[h * FH : (h + 1) * FH, :]
         par_w[...] = jnp.zeros_like(par_w)
         meet_all(env)
         links = Links(groups[0], env)
         crossing = [links.send(a, b, env.other()) for a, b in ((qkv_r, qkv_x), (fc_r, fc_x))]
-        params = gather_all(env, pack, small, groups[1])
+        params = gather_small(env, pack, small, groups[1])
         next(params)
 
         def fill_qkv(a, b, side):
@@ -728,9 +757,9 @@
 
         crossing[0].wait_recv()
         by_side(s, lambda side: fill_qkv(*((qkv_r, qkv_x) if side == 0 else (qkv_x, qkv_r)), side))
+        steps(params, 1)
         weights = gather_columns(env, qkv_s, wq_b, groups[2])
         next(weights)
-        steps(params, 4)
         rows_x = gather_blocks(env, x_s, x_v, groups[3], lay.tp_order, lay.tp_index, core=True)
         next(rows_x)
         proj = gather_all(env, proj_r, proj_b, groups[7])
@@ -741,7 +770,7 @@
         crossing[1].wait_recv()
         by_side(s, lambda side: fill_fc(*((fc_r, fc_x) if side == 0 else (fc_x, fc_r)), side))
         steps(weights, 1)
-        steps(params, 2)
+        steps(params, 1)
         steps(rows_x, 1)
         steps(proj, 1)
         steps(weights, 1)
@@ -896,7 +925,7 @@
     columns = sem_shapes(3 + gather_sends(k, False))
     blocks = sem_shapes(gather_sends(2, True))
     every = sem_shapes(gather_sends(2, False) + gather_sends(k, True))
-    scratch += sem_shapes(2) + every + columns + blocks * 2 + columns
+    scratch += sem_shapes(2) + sem_shapes(3 + n_dp) + columns + blocks * 2 + columns
     scratch += [DMA((2, HU)), DMA((2, n_dp)), DMA((2,))]
     scratch += every
     scratch += sem_shapes(gather_sends(k, True))
@@ -1204,6 +1233,7 @@
 
         for copy in loads(0):
             copy.start()
+        steps(proj, n_dp)
         for q in range(2):
             for copy in loads(q):
                 copy.wait()
@@ -1256,11 +1286,9 @@
                     carry = lax.fori_loop(j + 1, n_tiles, functools.partial(step, masked=False), carry)
                 put(1, j * tile, (carry[0] * SCALE).T.astype(BF))
                 put(2, j * tile, carry[1].T.astype(BF))
-                if q == 0 and j == 0:
-                    steps(proj, n_dp)
                 if q == 0 and j == 1:
                     steps(mixing, 4)
-                if q == 1 and j == 0:
+                if q == 0 and j == n_tiles - 1:
                     steps(proj, n_dp // 2)
                 if q == 1 and j >= n_tiles - 2:
                     steps(mixing, 1)
@@ -1447,7 +1475,7 @@
     x = jnp.transpose(tokens, (0, 2, 1)).reshape(D, T)
     dy = jnp.transpose(cotangent, (0, 2, 1)).reshape(D, T)
     (h1, wq, heads, o, pj, h2, fc, out, out_x, dy_all, lse, ob, x1, shift, par) = forward(
-        lay, x, gains, biases, fc_bias.reshape(2, FH // 2), qkv_weight, fc_weight, out_weight, proj_weight, dy
+        lay, x, gains, biases, fc_bias, qkv_weight, fc_weight, out_weight, proj_weight, dy
     )
     mix, dob, fc_sum, out_sum, dx1, vec, fcb = middle(
         lay, x, h2, dy_all, fc, out, out_x, shift, x1, dy, pj, par

time: 389 us -> 383 us (0.985)
  Pallas kernels: 382 us -> 377 us
    pallas_call x3, Pallas kernels: 376 us -> 371 us  [call(): pl.pallas_call(body, out_shape=outs, in_specs=in_specs, out_specs=out_spe...]
where the time goes in v6:
time: 383 us; the launch traced here: 379 us
  Pallas kernels  377 us (98%)
    pallas_call x3, Pallas kernels, call(): pl.pallas_call(body, out_shape=outs, in_specs=in_specs, out_specs=out_spe...  371 us

profile of v6, /device:TPU:0, one launch (start us, length us, event | category | flops | bytes accessed | tf_op | source)
XLA Modules:
  0.0 378.9 jit_solution(9508198572521326290)
XLA Ops:
  0.6 169.2 %forward.1 = (bf16[1600,1024]{1,0:T(8,128)(2,1)}, bf16[1600,768]{1,0:T(8,128)(2,1)}, bf16[3,2,64,2048]{3,2,1,0:T(8,128)(2,1)}, f32[2,64,2048]{2,1,0:T(8,128)}, b...) custom-call(bf16[1600,128]{1,0:T(8,128)(2,1)} %bitcast.14, ...), custom_call_target="tpu_custom_call" | custom-call | tf_op jit(solution)/shard_map/forward/pallas_call | solution.py:496
  169.8 83.9 %middle.1 = (bf16[2,4,128,1600]{3,2,1,0:T(8,128)(2,1)}, bf16[32,64,128]{2,1,0:T(8,128)(2,1)}, bf16[2,4,100,800]{3,2,1,0:T(8,128)(2,1)}, bf16[2,200,1600]{2,1,0:T...) custom-call(bf16[2,4,128,1600]{3,2,1,0:T(8,128)(2,1)} %get-tuple-element.48.refs_0_, ...), custom_call_target="tpu_custom_call" | custom-call | tf_op jit(solution)/shard_map/middle/pallas_call | solution.py:496
  253.7 117.5 %backward.1 = (f32[128,1600]{1,0:T(8,128)}, bf16[2,4,100,768]{3,2,1,0:T(8,128)(2,1)}, bf16[100,800]{1,0:T(8,128)(2,1)}, f32[8,128]{1,0:T(8,128)}, bf16[128,1600]{1,0:T(8,128)(2,1)}) custom-call(bf16[1600,128]{1,0:T(8,128)(2,1)} %bitcast.15, bf16[3,2,64,2048]{3,2,1,0:T(8,128)(2,1)} %get-tuple-element.45.refs_1_, f32[2,64,2048]{2,1,0:T(8,128)} %get-tuple-element.46.refs_2_, ...), custom_call_target="tpu_custom_call" | custom-call | tf_op jit(solution)/shard_map/backward/pallas_call | solution.py:496
  371.2 6.2 %assemble.1 = (bf16[1600,128]{1,0:T(8,128)(2,1)}, f32[1600,128]{1,0:T(8,128)}, f32[100,2400]{1,0:T(8,128)}, f32[100,800]{1,0:T(8,128)}, f32[100,3200]{1,0:T(8,12...) custom-call(bf16[2,4,100,768]{3,2,1,0:T(8,128)(2,1)} %get-tuple-element.65.refs_0_, ...), custom_call_target="tpu_custom_call" | custom-call | tf_op jit(solution)/shard_map/assemble/pallas_call | solution.py:1461
  377.4 1.3 reshape.37

commit v7 on v6

--- a/solution.py
+++ b/solution.py
@@ -994,7 +994,6 @@
         load_h2 = loads.local(h2_r, h2_v)
         load_out = [loads.local(out_r.at[:, s], out_b.at[0]), loads.local(outx_r, out_b.at[1])]
         load_dy = loads.local(dya_r, dy_v)
-        load_pj = loads.local(pj_r, pj_v)
         load_fc.wait()
         for c in range(n_ctx):
             fc_w[c * R : (c + 1) * R, :] = fc_b[lay.dp_index(c), lay.tp_index(c)]
@@ -1029,6 +1028,7 @@
                 du_v[q, at, :] = du
                 back_p[q, pl.ds(2 * i, 2)] = dot(du, fc_w[...], NT).astype(BF).reshape(2, T, D)
 
+        load_pj = loads.local(pj_r, pj_v)
         forth_and_back(1 - s)
         meet_all(env)
         rows = reduce_blocks(env, back_p, dh2_v, *spans[0])
@@ -1426,7 +1426,8 @@
         proj_o[...] = proj_r[...].astype(F32)
         gains_o[...] = small_r[0:1, :R]
         biases_o[...] = small_r[1:4, :R]
-        fcb_o[...] = small_r[4:6, : FH // 2]
+        row = jnp.concatenate([small_r[4:5, : FH // 2], small_r[5:6, : FH // 2]], axis=1)
+        fcb_o[...] = row.reshape(FH)
 
         def last(side):
             thirds = []
@@ -1456,7 +1457,7 @@
         struct(FB, half, dtype=F32),
         struct(1, R, dtype=F32),
         struct(3, R, dtype=F32),
-        struct(2, FH // 2, dtype=F32),
+        struct(FH, dtype=F32),
     ]
     return pl.pallas_call(
         body,
@@ -1495,7 +1496,7 @@
         out_grad,
         gains_grad,
         biases_grad,
-        fc_bias_grad.reshape(FH),
+        fc_bias_grad,
     )
 
 

time: 383 us -> 382 us (level)
  no operation moved by 1% of the time
where the time goes in v7:
time: 382 us; the launch traced here: 378 us
  Pallas kernels  377 us (99%)
    pallas_call x3, Pallas kernels, call(): pl.pallas_call(body, out_shape=outs, in_specs=in_specs, out_specs=out_spe...  371 us

profile of v7, /device:TPU:0, one launch (start us, length us, event | category | flops | bytes accessed | tf_op | source)
XLA Modules:
  0.0 377.6 jit_solution(3798890062706099558)
XLA Ops:
  0.6 169.2 %forward.1 = (bf16[1600,1024]{1,0:T(8,128)(2,1)}, bf16[1600,768]{1,0:T(8,128)(2,1)}, bf16[3,2,64,2048]{3,2,1,0:T(8,128)(2,1)}, f32[2,64,2048]{2,1,0:T(8,128)}, b...) custom-call(bf16[1600,128]{1,0:T(8,128)(2,1)} %bitcast.14, ...), custom_call_target="tpu_custom_call" | custom-call | tf_op jit(solution)/shard_map/forward/pallas_call | solution.py:496
  169.8 83.9 %middle.1 = (bf16[2,4,128,1600]{3,2,1,0:T(8,128)(2,1)}, bf16[32,64,128]{2,1,0:T(8,128)(2,1)}, bf16[2,4,100,800]{3,2,1,0:T(8,128)(2,1)}, bf16[2,200,1600]{2,1,0:T...) custom-call(bf16[2,4,128,1600]{3,2,1,0:T(8,128)(2,1)} %get-tuple-element.48.refs_0_, ...), custom_call_target="tpu_custom_call" | custom-call | tf_op jit(solution)/shard_map/middle/pallas_call | solution.py:496
  253.7 117.5 %backward.1 = (f32[128,1600]{1,0:T(8,128)}, bf16[2,4,100,768]{3,2,1,0:T(8,128)(2,1)}, bf16[100,800]{1,0:T(8,128)(2,1)}, f32[8,128]{1,0:T(8,128)}, bf16[128,1600]{1,0:T(8,128)(2,1)}) custom-call(bf16[1600,128]{1,0:T(8,128)(2,1)} %bitcast.15, bf16[3,2,64,2048]{3,2,1,0:T(8,128)(2,1)} %get-tuple-element.45.refs_1_, f32[2,64,2048]{2,1,0:T(8,128)} %get-tuple-element.46.refs_2_, ...), custom_call_target="tpu_custom_call" | custom-call | tf_op jit(solution)/shard_map/backward/pallas_call | solution.py:496
  371.2 6.2 %assemble.1 = (bf16[1600,128]{1,0:T(8,128)(2,1)}, f32[1600,128]{1,0:T(8,128)}, f32[100,2400]{1,0:T(8,128)}, f32[100,800]{1,0:T(8,128)}, f32[100,3200]{1,0:T(8,12...) custom-call(bf16[2,4,100,768]{3,2,1,0:T(8,128)(2,1)} %get-tuple-element.65.refs_0_, ...), custom_call_target="tpu_custom_call" | custom-call | tf_op jit(solution)/shard_map/assemble/pallas_call | solution.py:1462
